TPU v7x, 32 devices: a whole 2x2x4 slice. The times are simulated.
32 devices in a mesh: seg: 16 (over z, y, x), sub: 2 (over core).
Axes of the slice: x: 2, y: 2, z: 4, core: 2. Of those that a mesh axis runs over, the one named last changes fastest.
Arguments:
- near_blocks: bfloat16 [64, 10, 256, 256], P(('seg', 'sub')), may hold values from -0.375 to 0.375
- sample_cols: bfloat16 [16384, 256], P(('seg', 'sub')), may hold values from -6 to 6
- near_list: int32 [64, 10], P(('seg', 'sub')), may hold values from -1 to 63, as said below
- row_basis_t: bfloat16 [64, 64, 256], P(('seg', 'sub')), may hold values from -0.75 to 0.75
- col_basis_t: bfloat16 [64, 64, 256], P(('seg', 'sub')), may hold values from -0.375 to 0.375
- couplings: bfloat16 [16, 2, 16, 64, 128], P('seg', 'sub'), may hold values from -0.25 to 0.25
- far_source: int32 [16, 2, 16, 2], P('seg', 'sub'), may hold values from 0 to 2
- far_dest: int32 [16, 2, 16, 2], P('seg', 'sub'), may hold values from 0 to 1
Outputs:
- samples: bfloat16 [16384, 256], P(('seg', 'sub'))
- segment_factor: float32 [4096, 256], P('seg')
- transfers: bfloat16 [16, 3, 256, 256], P('seg')
Inputs may be any that keep to these rules, and one draw needn't show every extreme that they name: `near_list`: entry 0 of every list is the leaf itself; -1 marks padding and stands only after the real entries; every other entry names a leaf held by the same device or by the device just before or just after it in the order of seg, then sub. `far_source`: entry [s', u, s, c] is the local leaf of device (s', u) whose far projection fills slot c toward device (s, u); the value 2 marks an empty slot. `far_dest`: entry [s, u, s', c] is the local leaf of device (s, u) that slot c from device (s', u) serves.
All inputs are finite; a program needn't handle non-finite values.
Results may differ from a plain program's by a relative error of at most 0.013.
Values may be sent and summed in bfloat16 or wider, within the bound.
No kernel may reach another device: no remote copies, remote signals or barrier semaphores. Data moves between devices by JAX's collectives and lax.ppermute only.
A program may use at most 64 MiB of HBM per device.

v0:
```python
import jax
import jax.numpy as jnp
from jax import lax
from jax.sharding import PartitionSpec as P

LEVELS = 3


def padded(value, sides, width):
    for axis, dim in sides:
        size, length = (lax.axis_size(axis), value.shape[dim])
        up = [(i, (i + 1) % size) for i in range(size - 1)]
        down = [(j, i) for i, j in up]
        last = lax.slice_in_dim(value, length - width, length, axis=dim)
        leading = lax.slice_in_dim(value, 0, width, axis=dim)
        before = lax.ppermute(last, axis, up)
        after = lax.ppermute(leading, axis, down)
        value = jnp.concatenate([before, value, after], axis=dim)
    return value


def from_partner(value, axis, distance):
    mask = 2**distance
    pairs = [(source, source ^ mask) for source in range(lax.axis_size(axis))]
    return lax.ppermute(value, axis, pairs)


def body(
    near_blocks, sample_cols, near_list, row_basis_t, col_basis_t, couplings, far_source, far_dest
):
    leaf_count, near_count, leaf_rows, _ = near_blocks.shape
    sample_width = sample_cols.shape[1]
    rank_width = row_basis_t.shape[1]
    seg_count = lax.axis_size("seg")
    slot_number_count = far_source.shape[3]
    random_cols = sample_cols.reshape(leaf_count, leaf_rows, sample_width)
    basis_projector = jnp.einsum(
        "jra,jas->jrs", col_basis_t, random_cols, preferred_element_type=jnp.float32
    ).astype(jnp.bfloat16)
    extended = padded(sample_cols, ((("seg", "sub"), 0),), leaf_count * leaf_rows)
    extended = extended.reshape(3 * leaf_count, leaf_rows, sample_width)
    base_leaf = (lax.axis_index(("seg", "sub")) - 1) * leaf_count
    usable = near_list >= 0
    position = jnp.where(usable, near_list - base_leaf, 0)
    chosen = extended[position]
    chosen = jnp.where(usable[:, :, None, None], chosen, jnp.zeros_like(chosen))
    near_part = jnp.einsum(
        "lkab,lkbs->las", near_blocks, chosen, preferred_element_type=jnp.float32
    )
    leaf_range = jnp.arange(leaf_count, dtype=jnp.int32)
    routing = far_dest[0, 0][:, :, None] == leaf_range[None, None, :]
    coupling_set = jnp.transpose(
        couplings[0, 0].reshape(seg_count, rank_width, slot_number_count, rank_width), (1, 0, 2, 3)
    )
    masked = jnp.where(
        jnp.transpose(routing, (2, 0, 1))[:, None, :, :, None],
        coupling_set[None],
        jnp.zeros((), jnp.bfloat16),
    )
    masked = masked.reshape(leaf_count * rank_width, seg_count * slot_number_count * rank_width)
    selection_choice = (far_source[0, 0][:, :, None] == leaf_range[None, None, :]).astype(
        jnp.bfloat16
    )
    outgoing = jnp.einsum(
        "zgy,ykf->zgkf", selection_choice, basis_projector, preferred_element_type=jnp.float32
    ).astype(jnp.bfloat16)
    incoming = lax.all_to_all(outgoing, "seg", split_axis=0, concat_axis=0, tiled=True)
    far_total = jnp.dot(
        masked,
        incoming.reshape(seg_count * slot_number_count * rank_width, sample_width),
        preferred_element_type=jnp.float32,
    )
    far_coeff = far_total.astype(jnp.bfloat16).reshape(leaf_count, rank_width, sample_width)
    distant_portion = jnp.einsum(
        "lra,lrs->las", row_basis_t, far_coeff, preferred_element_type=jnp.float32
    )
    samples = (
        (near_part + distant_portion)
        .astype(jnp.bfloat16)
        .reshape(leaf_count * leaf_rows, sample_width)
    )
    gram_local = lax.dot_general(
        samples, samples, (((0,), (0,)), ((), ())), preferred_element_type=jnp.float32
    )
    row_total = lax.axis_size("sub") * leaf_count * leaf_rows
    current = lax.psum(gram_local.astype(jnp.bfloat16), "sub").astype(jnp.float32) / row_total
    gram_levels = [current]
    for segment_position_index in range(LEVELS):
        partner = from_partner(current.astype(jnp.bfloat16), "seg", segment_position_index).astype(
            current.dtype
        )
        current = (current + partner) * 0.5
        gram_levels.append(current)
    stacked = jnp.stack(gram_levels)
    triangles = jnp.linalg.cholesky(stacked)
    segment_factor = jnp.swapaxes(triangles[0], 0, 1)
    solved = jax.vmap(
        lambda upper_one, lower_one: jax.scipy.linalg.solve_triangular(
            upper_one, lower_one, lower=True
        )
    )(triangles[1:], triangles[:-1])
    transfers = jnp.swapaxes(solved, 1, 2).astype(jnp.bfloat16)[None]
    return (samples, segment_factor, transfers)


def solution(mesh):
    in_specs = (
        P(("seg", "sub"), None, None, None),
        P(("seg", "sub"), None),
        P(("seg", "sub"), None),
        P(("seg", "sub"), None, None),
        P(("seg", "sub"), None, None),
        P("seg", "sub", None, None, None),
        P("seg", "sub", None, None),
        P("seg", "sub", None, None),
    )
    out_specs = (P(("seg", "sub"), None), P("seg", None), P("seg", None, None, None))
    return jax.shard_map(body, mesh=mesh, in_specs=in_specs, out_specs=out_specs, check_vma=False)
```

profile of v0, /device:TPU:0, one launch (start us, length us, event | category | flops | bytes accessed | tf_op | source)
XLA Modules:
  0.0 323.9 jit_solution(7154589250793300197)
XLA Ops:
  9.8 1.3 copy.53
  11.1 8.4 %all-to-all-start = ((bf16[16,2,64,256]{3,2,1,0:T(8,128)(2,1)}), bf16[16,2,64,256]{3,2,1,0:T(8,128)(2,1)}, u32[]{:S(2)}, u32[]{:S(2)}) async-start(bf16[16,2,64,256]{3,2,1,0:T(8,128)(2,1)} %copy.53), calls=%async_computation | async-start | bytes 2097152 | tf_op jit(solution)/shard_map/all_to_all | solution.py:67
  19.5 2.2 collective-permute-start
  24.4 2.5 broadcast_select_fusion
  26.9 4.0 %select_n.33 = bf16[128,2048]{1,0:T(8,128)(2,1)} reshape(bf16[2,64,16,2,64]{4,3,2,1,0:T(2,128)(2,1)} %broadcast_select_fusion) | data formatting | bytes 1048576 | tf_op jit(solution)/shard_map/jit(_where)/select_n | solution.py:55
  32.1 2.4 gather_fusion
  34.4 3.5 %fusion.4 = f32[2,256,256]{1,2,0:T(8,128)} fusion(bf16[2,10,256,256]{3,2,1,0:T(8,128)(2,1)S(1)} %copy-done, bf16[2,10,256,256]{3,2,1,0:T(8,128)(2,1)} %bitcast.95, pred[2,10]{1,0:T(4,128)(4,1)S(1)} %broadcast_compare_fusion), kind=kOutput, calls=%fused_computation.9 | convolution fusion | flops 672399360 | bytes 5767188 | tf_op jit(solution)/shard_map/lkab,lkbs->las/dot_general | solution.py:47
  38.0 6.0 %all-to-all-done = bf16[16,2,64,256]{3,2,1,0:T(8,128)(2,1)} async-done(((bf16[16,2,64,256]{3,2,1,0:T(8,128)(2,1)}), bf16[16,2,64,256]{3,2,1,0:T(8,128)(2,1)}, u32[]{:S(2)}, u32[]{:S(2)}) %all-to-all-start) | async-done | bytes 1048608 | tf_op jit(solution)/shard_map/all_to_all | solution.py:67
  44.0 1.5 convolution_convert_fusion.2
  45.5 1.3 fusion.7
  48.5 27.3 %all-reduce.3.cloned.1.call-done = bf16[256,256]{0,1:T(8,128)(2,1)} async-done(((bf16[256,256]{0,1:T(8,128)(2,1)}), bf16[256,256]{0,1:T(8,128)(2,1)}) %all-reduce.3.cloned.1.call-update) | async-done | bytes 131088 | tf_op jit(solution)/shard_map/psum | solution.py:86
  76.7 1.8 collective-permute-start.2
  78.5 4.0 %collective-permute-done.2 = bf16[256,256]{0,1:T(8,128)(2,1)S(1)} collective-permute-done((bf16[256,256]{0,1:T(8,128)(2,1)S(1)}, bf16[256,256]{0,1:T(8,128)(2,1)S(1)}, u32[]{:S(2)}, u32[]{:S(2)}) %collective-permute-start.2) | collective-permute-done | bytes 131104 | tf_op jit(solution)/shard_map/ppermute | solution.py:25
  83.4 1.8 collective-permute-start.3
  85.9 2.6 collective-permute-done.3
  89.5 1.8 collective-permute-start.4
  92.5 2.1 collective-permute-done.4
  97.5 2.5 copy.56
  100.1 1.4 fusion.9
  102.5 46.9 %custom-call.17 = f32[4,128,128]{2,1,0:T(8,128)S(1)} custom-call(f32[4,128,128]{2,1,0:T(8,128)S(1)} %cholesky.122), custom_call_target="Cholesky" | custom-call | tf_op jit(solution)/shard_map/jit(cholesky)/cholesky | solution.py:95
  150.5 39.3 %custom-call.18 = f32[4,1,128,128]{2,3,1,0:T(8,128)S(1)} custom-call(f32[4,1,128,128]{3,2,1,0:T(8,128)S(1)} %select_bitcast_fusion), custom_call_target="InvertDiagBlocksLowerTriangular" | custom-call | tf_op jit(solution)/shard_map/jit(cholesky)/cholesky | solution.py:95
  189.8 2.1 constant_dynamic-update-slice_fusion.1
  192.0 1.6 convolution_subtract_fusion.1
  193.6 47.1 %custom-call.19 = f32[4,128,128]{2,1,0:T(8,128)S(1)} custom-call(f32[4,128,128]{2,1,0:T(8,128)S(1)} %convolution_subtract_fusion.1), custom_call_target="Cholesky" | custom-call | tf_op jit(solution)/shard_map/jit(cholesky)/cholesky | solution.py:95
  241.7 1.4 select_select_fusion
  244.8 5.4 %while.1 = (s32[]{:T(128)}, f32[3,256,256]{2,1,0:T(8,128)S(1)}, s32[2,2]{1,0:T(2,128)S(1)}, f32[2,3,128,128]{3,2,0,1:T(8,128)}, s32[]{:T(128)}) while((s32[]{:T(128)}, f32[3,256,256]{2,1,0:T(8,128)S(1)}, s32[2,2]{1,0:T(2,128)S(1)}, f32[2,3,128,128]{3,2,0,1:T(8,128)}, s32[]{:T(128)}) %tuple.35), condition=%wide.while_cond, body=%wide.while_body.sunk | while | flops 2 | bytes 394849 | solution.py:98
  245.4 2.1 bitcast_dynamic-update-slice_fusion.2
  248.1 2.1 bitcast_dynamic-update-slice_fusion.2
  250.2 60.4 %custom-call.20 = f32[3,2,128,128]{2,3,1,0:T(8,128)} custom-call(f32[3,2,128,128]{3,2,1,0:T(8,128)} %bitcast.101), custom_call_target="InvertDiagBlocksLowerTriangular" | custom-call | tf_op jit(solution)/shard_map/vmap(jit(_solve_triangular))/triangular_solve | solution.py:98
  310.6 1.7 fusion.31
  312.2 1.5 convolution_subtract_fusion
  315.2 1.8 copy.62
  (72 shorter events, 23.2 us)
Async XLA Ops:
  7.2 27.3 %copy-start = (bf16[2,10,256,256]{3,2,1,0:T(8,128)(2,1)S(1)}, bf16[2,10,256,256]{3,2,1,0:T(8,128)(2,1)}, u32[]{:S(2)}) copy-start(bf16[2,10,256,256]{3,2,1,0:T(8,128)(2,1)} %param.8) | copy-start | bytes 7864324
  8.5 11.0 %copy-start.5 = (bf16[512,256]{1,0:T(8,128)(2,1)S(1)}, bf16[512,256]{1,0:T(8,128)(2,1)}, u32[]{:S(2)}) copy-start(bf16[512,256]{1,0:T(8,128)(2,1)} %param.9) | copy-start | bytes 786436
  8.5 14.5 %copy-start.13 = (s32[2,10]{1,0:T(2,128)S(1)}, s32[2,10]{1,0:T(2,128)}, u32[]{:S(2)}) copy-start(s32[2,10]{1,0:T(2,128)} %param.10) | copy-start | bytes 244
  9.8 14.5 %copy-start.12 = (s32[1,1,16,2]{2,3,1,0:T(2,128)S(1)}, s32[1,1,16,2]{2,3,1,0:T(2,128)}, u32[]{:S(2)}) copy-start(s32[1,1,16,2]{2,3,1,0:T(2,128)} %param.15) | copy-start | bytes 388
  11.1 32.9 %all-to-all-start = ((bf16[16,2,64,256]{3,2,1,0:T(8,128)(2,1)}), bf16[16,2,64,256]{3,2,1,0:T(8,128)(2,1)}, u32[]{:S(2)}, u32[]{:S(2)}) async-start(bf16[16,2,64,256]{3,2,1,0:T(8,128)(2,1)} %copy.53), calls=%async_computation | async-start | bytes 2097152 | tf_op jit(solution)/shard_map/all_to_all | solution.py:67
  19.5 56.3 %all-reduce.3.cloned.1.call-start = ((), (), s32[]{:S(2)}) async-start(), calls=%async_computation.1 | async-start | bytes 262144 | tf_op jit(solution)/shard_map/psum | solution.py:86
  19.5 11.4 %collective-permute-start = (bf16[512,256]{1,0:T(8,128)(2,1)S(1)}, bf16[512,256]{1,0:T(8,128)(2,1)}, u32[]{:S(2)}, u32[]{:S(2)}) collective-permute-start(bf16[512,256]{1,0:T(8,128)(2,1)S(1)} %copy-done.5), channel_id=1, source_target_pairs={{0,1},{1,2},{2,3},{3,4},{4,5},{5,6},{6,7},{7,8},{8,9},{9,10},{10,1... | collective-permute-start | bytes 786440 | tf_op jit(solution)/shard_map/ppermute | solution.py:16
  21.7 9.2 %collective-permute-start.1 = (bf16[512,256]{1,0:T(8,128)(2,1)S(1)}, bf16[512,256]{1,0:T(8,128)(2,1)}, u32[]{:S(2)}, u32[]{:S(2)}) collective-permute-start(bf16[512,256]{1,0:T(8,128)(2,1)S(1)} %copy-done.5), channel_id=1, source_target_pairs={{1,0},{2,1},{3,2},{4,3},{5,4},{6,5},{7,6},{8,7},{9,8},{10,9},{11,1... | collective-permute-start | bytes 786440 | tf_op jit(solution)/shard_map/ppermute | solution.py:17
  34.4 9.5 %copy-start.4 = (bf16[128,2048]{1,0:T(8,128)(2,1)S(1)}, bf16[128,2048]{1,0:T(8,128)(2,1)}, u32[]{:S(2)}) copy-start(bf16[128,2048]{1,0:T(8,128)(2,1)} %select_n.33) | copy-start | bytes 1572868
  34.4 11.1 %copy-start.10 = (bf16[2,64,256]{2,1,0:T(8,128)(2,1)S(1)}, bf16[2,64,256]{2,1,0:T(8,128)(2,1)}, u32[]{:S(2)}) copy-start(bf16[2,64,256]{2,1,0:T(8,128)(2,1)} %param.11) | copy-start | bytes 196612
  46.8 0.7 copy-start.9
  76.7 5.8 %collective-permute-start.2 = (bf16[256,256]{0,1:T(8,128)(2,1)S(1)}, bf16[256,256]{0,1:T(8,128)(2,1)S(1)}, u32[]{:S(2)}, u32[]{:S(2)}) collective-permute-start(bf16[256,256]{0,1:T(8,128)(2,1)S(1)} %fusion.16), channel_id=1, source_target_pairs={{0,2},{2,0},{4,6},{6,4},{8,10},{10,8},{12,14},{14,12},{16,18},{18,... | collective-permute-start | bytes 393224 | tf_op jit(solution)/shard_map/ppermute | solution.py:25
  83.4 5.0 %collective-permute-start.3 = (bf16[256,256]{0,1:T(8,128)(2,1)S(1)}, bf16[256,256]{0,1:T(8,128)(2,1)S(1)}, u32[]{:S(2)}, u32[]{:S(2)}) collective-permute-start(bf16[256,256]{0,1:T(8,128)(2,1)S(1)} %get-tuple-element.41), channel_id=1, source_target_pairs={{0,4},{2,6},{4,0},{6,2},{8,12},{10,14},{12,8},{14,10},{16,20},{18,... | collective-permute-start | bytes 393224 | tf_op jit(solution)/shard_map/ppermute | solution.py:25
  88.5 4.0 %copy-start.7 = (bf16[256,256]{0,1:T(8,128)(2,1)}, bf16[256,256]{0,1:T(8,128)(2,1)S(1)}, u32[]{:S(2)}) copy-start(bf16[256,256]{0,1:T(8,128)(2,1)S(1)} %collective-permute-done.3) | copy-start | bytes 393220
  89.5 5.1 %collective-permute-start.4 = (bf16[256,256]{0,1:T(8,128)(2,1)S(1)}, bf16[256,256]{0,1:T(8,128)(2,1)}, u32[]{:S(2)}, u32[]{:S(2)}) collective-permute-start(bf16[256,256]{0,1:T(8,128)(2,1)S(1)} %get-tuple-element.36), channel_id=1, source_target_pairs={{0,8},{2,10},{4,12},{6,14},{8,0},{10,2},{12,4},{14,6},{16,24},{18,... | collective-permute-start | bytes 393224 | tf_op jit(solution)/shard_map/ppermute | solution.py:25
  95.8 0.7 copy-start.3
  100.1 50.4 %copy-start.11 = (pred[128,128]{1,0:T(8,128)(4,1)S(1)}, pred[128,128]{1,0:T(8,128)(4,1)}, u32[]{:S(2)}) copy-start(pred[128,128]{1,0:T(8,128)(4,1)} %iota_compare_fusion.1) | copy-start | bytes 49156
  101.5 1.0 copy-start.2
  102.5 139.2 %copy-start.6 = (pred[256,256]{1,0:T(8,128)(4,1)S(1)}, pred[256,256]{1,0:T(8,128)(4,1)}, u32[]{:S(2)}) copy-start(pred[256,256]{1,0:T(8,128)(4,1)} %iota_compare_fusion) | copy-start | bytes 196612
  193.6 51.2 %copy-start.14 = (s32[2]{0:T(128)S(1)}, s32[2]{0:T(128)}, u32[]{:S(2)}) copy-start(s32[2]{0:T(128)} %iota_multiply_fusion) | copy-start | bytes 28
  243.1 1.0 copy-start.1
  310.6 3.2 copy-start.8
Sparse Core Ops, SparseCore 0:
  48.6 27.1 all-reduce.2
where the time goes:
time: 325 us; the launch traced here: 324 us
  other arithmetic  208 us (64%)
  waiting for transfers between devices  42 us (13%)
  local copies, waits for them, and re-layouts  24.9 us (8%)
  matrix products  17.3 us (5%)
  starting transfers between devices  17.3 us (5%)
  between operations  14.3 us (4%)
    another operation x9, other arithmetic, body(): triangles = jnp.linalg.cholesky(stacked)  135 us
    another operation x3, other arithmetic, body(): jax.scipy.linalg.solve_triangular(upper_one, lower_one, lower=True)  61 us
    psum x1, waiting for transfers between devices, body(): lax.psum(gram_local.astype(jnp.bfloat16), 'sub').astype(jnp.float32)  27.3 us
    ppermute x3, waiting for transfers between devices, from_partner(): return lax.ppermute(value, axis, pairs)  8.69 us
    all_to_all x1, starting transfers between devices, body(): lax.all_to_all(outgoing, 'seg', split_axis=0, concat_axis=0, tiled=True)  8.36 us
  transfers between devices with their start and end apart: 7, of which 5 were waited for; matrix products, arithmetic and copies ran while one was open for 5% of the time, Pallas kernels for 0%

commit v1 on v0

--- a/solution.py
+++ b/solution.py
@@ -1,6 +1,8 @@
 import jax
 import jax.numpy as jnp
 from jax import lax
+from jax.experimental import pallas as pl
+from jax.experimental.pallas import tpu as pltpu
 from jax.sharding import PartitionSpec as P
 
 LEVELS = 3
@@ -23,6 +25,107 @@
     mask = 2**distance
     pairs = [(source, source ^ mask) for source in range(lax.axis_size(axis))]
     return lax.ppermute(value, axis, pairs)
+
+
+def rb(x,k): return jnp.broadcast_to(x[k:k+1,:],(8,128))
+
+def split(a):
+    h=a.astype(jnp.bfloat16); return h,(a-h.astype(jnp.float32)).astype(jnp.bfloat16)
+def dg(a,b,dims): return lax.dot_general(a,b,(dims,((),())),preferred_element_type=jnp.float32)
+def mm3(a,b,dims):
+    ah,al=split(a); bh,bl=split(b)
+    return dg(ah,bh,dims)+dg(ah,bl,dims)+dg(al,bh,dims)
+def mm(a,b): return mm3(a,b,((1,),(0,)))
+def mmt(a,b): return mm3(a,b,((1,),(1,)))
+def eliminate(P, lane, row):
+    base=lane & ~31
+    sub=lane & 31
+    V=[jnp.where(row+8*rv==sub,1.0,0.0).astype(jnp.float32) for rv in range(4)]
+    P=list(P)
+    for m in range(4):
+        C=[[jnp.take_along_axis(P[rv],base+(8*m+k),axis=1,mode="promise_in_bounds") for rv in range(m,4)] for k in range(8)]
+        piv=jnp.ones((8,128),jnp.float32)
+        for k in range(8):
+            d=rb(C[k][0],k)
+            piv=jnp.where(row==k,d,piv)
+            inv=1.0/d
+            M=[c*inv for c in C[k]]
+            M[0]=jnp.where(row>k,M[0],0.0)
+            for k2 in range(k+1,8):
+                f=rb(C[k2][0],k)
+                C[k2]=[c-mu*f for c,mu in zip(C[k2],M)]
+            fp=rb(P[m],k); fv=rb(V[m],k)
+            for rv in range(m,4):
+                P[rv]=P[rv]-M[rv-m]*fp
+                V[rv]=V[rv]-M[rv-m]*fv
+        rs=lax.rsqrt(piv)
+        P[m]=P[m]*rs
+        V[m]=V[m]*rs
+    return P,V
+
+def factor_kernel(g_ref,r_ref,tr_ref,X,Rb,Wb):
+    n=256
+    lane=lax.broadcasted_iota(jnp.int32,(8,128),1); row=lax.broadcasted_iota(jnp.int32,(8,128),0)
+    grp=lane//32
+    l32=lax.broadcasted_iota(jnp.int32,(32,256),1)
+    r32=lax.broadcasted_iota(jnp.int32,(32,256),0)
+    bd=(lax.broadcasted_iota(jnp.int32,(128,128),0)//32)==(lax.broadcasted_iota(jnp.int32,(128,128),1)//32)
+    l256=lax.broadcasted_iota(jnp.int32,(128,256),1); r256=lax.broadcasted_iota(jnp.int32,(128,256),0)&31
+    for kb in range(8):
+        for t in range(4):
+            X[kb,32*t:32*t+32,:]=g_ref[t,32*kb:32*kb+32,:]
+    for kb in range(8):
+        off=32*kb; c0=off//128*128; lo=off%128
+        P=[]
+        for rv in range(4):
+            acc=None
+            for t in range(4):
+                v=X[kb,t*32+8*rv:t*32+8*rv+8,c0:c0+128]
+                sh=(32*t-lo)%128
+                if sh: v=pltpu.roll(v,sh,1)
+                acc=v if acc is None else jnp.where(grp==t,v,acc)
+            P.append(acc)
+        P,V=eliminate(P,lane,row)
+        Pf=jnp.concatenate(P,0); Vf=jnp.concatenate(V,0)
+        Wbd=jnp.where(bd,jnp.concatenate([Vf]*4,0),0.0)
+        x=X[kb]
+        x=jnp.where((l256>=off)&(l256<off+32),jnp.where(l256-off==r256,1.0,0.0),x)
+        panel=mm(Wbd,x)
+        chunks={}
+        for i in range(kb+1,8):
+            c=i//4
+            if c not in chunks: chunks[c]=jnp.transpose(panel[:,c*128:c*128+128])
+            T=chunks[c][(i%4)*32:(i%4)*32+32,:]
+            L=jnp.where(bd,jnp.concatenate([T]*4,0),0.0)
+            X[i]=jnp.where((l256>=off)&(l256<off+32),0.0,X[i])-mm(L,panel)
+        for t in range(4):
+            pt=panel[32*t:32*t+32,:]
+            sh=(lo-32*t)%128
+            d=Pf
+            if sh: d=pltpu.roll(d,sh,1)
+            d2=jnp.concatenate([d,d],1)
+            Rb[t,off:off+32,:]=jnp.where(l32>=off+32,pt,jnp.where((l32>=off)&(l32-off>=r32),d2,0.0))
+            if t>0: Wb[t-1,off:off+32,:]=jnp.where(l32<off+32,pt,0.0)
+    r_ref[...]=Rb[0]
+    for t in range(3):
+        tr_ref[t]=mmt(Rb[t],Wb[t]).astype(jnp.bfloat16)
+
+def factor_all(grams):
+    return pl.pallas_call(
+        factor_kernel,
+        out_shape=(
+            jax.ShapeDtypeStruct((256, 256), jnp.float32),
+            jax.ShapeDtypeStruct((LEVELS, 256, 256), jnp.bfloat16),
+        ),
+        in_specs=[pl.BlockSpec(memory_space=pltpu.VMEM)],
+        out_specs=[pl.BlockSpec(memory_space=pltpu.VMEM)] * 2,
+        scratch_shapes=[
+            pltpu.VMEM((8, 128, 256), jnp.float32),
+            pltpu.VMEM((4, 256, 256), jnp.float32),
+            pltpu.VMEM((3, 256, 256), jnp.float32),
+        ],
+        compiler_params=pltpu.CompilerParams(vmem_limit_bytes=32 * 2**20),
+    )(grams)
 
 
 def body(
@@ -83,7 +186,14 @@
         samples, samples, (((0,), (0,)), ((), ())), preferred_element_type=jnp.float32
     )
     row_total = lax.axis_size("sub") * leaf_count * leaf_rows
-    current = lax.psum(gram_local.astype(jnp.bfloat16), "sub").astype(jnp.float32) / row_total
+    total, distance = gram_local, 0
+    while 2**distance < lax.axis_size("sub"):
+        rounded = total.astype(jnp.bfloat16)
+        total = rounded.astype(jnp.float32) + from_partner(rounded, "sub", distance).astype(
+            jnp.float32
+        )
+        distance += 1
+    current = total / row_total
     gram_levels = [current]
     for segment_position_index in range(LEVELS):
         partner = from_partner(current.astype(jnp.bfloat16), "seg", segment_position_index).astype(
@@ -92,15 +202,8 @@
         current = (current + partner) * 0.5
         gram_levels.append(current)
     stacked = jnp.stack(gram_levels)
-    triangles = jnp.linalg.cholesky(stacked)
-    segment_factor = jnp.swapaxes(triangles[0], 0, 1)
-    solved = jax.vmap(
-        lambda upper_one, lower_one: jax.scipy.linalg.solve_triangular(
-            upper_one, lower_one, lower=True
-        )
-    )(triangles[1:], triangles[:-1])
-    transfers = jnp.swapaxes(solved, 1, 2).astype(jnp.bfloat16)[None]
-    return (samples, segment_factor, transfers)
+    segment_factor, transfers = factor_all(stacked)
+    return (samples, segment_factor, transfers[None])
 
 
 def solution(mesh):

time: 325 us -> 79.5 us (0.24)
  other arithmetic: 208 us -> 4.05 us
  waiting for transfers between devices: 42 us -> 18.1 us
  local copies, waits for them, and re-layouts: 24.9 us -> 9.11 us
  between operations: 14.3 us -> 0.82 us
  Pallas kernels: 0 us -> 11.6 us
  starting transfers between devices: 17.3 us -> 25.8 us
  matrix products: 17.3 us -> 9.21 us
    another operation x12 -> x0, other arithmetic: 196 us -> none  [the longest x9 135 us: body(): triangles = jnp.linalg.cholesky(stacked)]
    psum x1 -> x0, waiting for transfers between devices: 27.3 us -> none  [body(): lax.psum(gram_local.astype(jnp.bfloat16), 'sub').astype(jnp.float32)]
    pallas_call x0 -> x1, Pallas kernels: none -> 11.6 us  [factor_all(): pl.pallas_call(factor_kernel, out_shape=(jax.ShapeDtypeStruct((256, 256),...]
    another operation x10 -> x0, local copies, waits for them, and re-layouts: 9.07 us -> none
    ppermute x3 -> x4, starting transfers between devices: 5.42 us -> 14 us  [from_partner(): return lax.ppermute(value, axis, pairs)]
    another operation x5 -> x0, matrix products: 7.4 us -> none  [the longest x2 3.73 us: body(): triangles = jnp.linalg.cholesky(stacked)]
    unnamed x32 -> x14, local copies, waits for them, and re-layouts: 6.01 us -> 0.04 us
    another operation x4, other arithmetic: 4.19 us -> 0.36 us  [body(): stacked = jnp.stack(gram_levels)]
  transfers between devices with their start and end apart: 7 -> 7, of which waited for: 5 -> 5; matrix products, arithmetic and copies ran while one was open for 5% -> 19% of each run, Pallas kernels for 0% -> 0%
where the time goes in v1:
time: 79.5 us; the launch traced here: 78.7 us
  starting transfers between devices  25.8 us (32%)
  waiting for transfers between devices  18.1 us (23%)
  Pallas kernels  11.6 us (15%)
  matrix products  9.21 us (12%)
  local copies, waits for them, and re-layouts  9.11 us (11%)
  other arithmetic  4.05 us (5%)
  between operations  0.82 us (1%)
    ppermute x4, starting transfers between devices, from_partner(): return lax.ppermute(value, axis, pairs)  14 us
    ppermute x4, waiting for transfers between devices, from_partner(): return lax.ppermute(value, axis, pairs)  12.1 us
    pallas_call x1, Pallas kernels, factor_all(): pl.pallas_call(factor_kernel, out_shape=(jax.ShapeDtypeStruct((256, 256),...  11.6 us
    all_to_all x1, starting transfers between devices, body(): lax.all_to_all(outgoing, 'seg', split_axis=0, concat_axis=0, tiled=True)  8.36 us
    all_to_all x1, waiting for transfers between devices, body(): lax.all_to_all(outgoing, 'seg', split_axis=0, concat_axis=0, tiled=True)  6.01 us
    select_n x1, local copies, waits for them, and re-layouts, body(): jnp.where(jnp.transpose(routing, (2, 0, 1))[:, None, :, :, None], couplin...  4.04 us
    dot_general x1, matrix products, body(): jnp.einsum('lkab,lkbs->las', near_blocks, chosen, preferred_element_type=...  3.55 us
    select_n x1, other arithmetic, body(): jnp.where(jnp.transpose(routing, (2, 0, 1))[:, None, :, :, None], couplin...  2.46 us
  transfers between devices with their start and end apart: 7, of which 5 were waited for; matrix products, arithmetic and copies ran while one was open for 19% of the time, Pallas kernels for 0%

profile of v1, /device:TPU:0, one launch (start us, length us, event | category | flops | bytes accessed | tf_op | source)
XLA Modules:
  0.0 78.7 jit_solution(17562039928463884631)
XLA Ops:
  0.6 0.0 copy-start
  0.6 1.3 %convolution_convert_fusion.2 = bf16[2,64,256]{2,1,0:T(8,128)(2,1)S(1)} fusion(bf16[2,64,256]{2,1,0:T(8,128)(2,1)} %param.12, bf16[2,256,256]{2,1,0:T(8,128)(2,1)} %bitcast.51), kind=kOutput, calls=%fused_computation.13 | convolution fusion | flops 16809984 | bytes 393216 | tf_op jit(solution)/shard_map/jra,jas->jrs/dot_general | solution.py:140
  2.0 1.2 %convolution_convert_fusion = bf16[16,2,64,256]{3,0,2,1:T(8,128)(2,1)S(1)} fusion(bf16[2,64,256]{2,1,0:T(8,128)(2,1)S(1)} %convolution_convert_fusion.2, s32[16,2]{0,1:T(2,128)} %bitcast.54), kind=kOutput, calls=%fused_computation.5 | convolution fusion | flops 2621504 | bytes 1114240 | tf_op jit(solution)/shard_map/zgy,ykf->zgkf/dot_general | solution.py:167
  3.2 1.3 %copy.21 = bf16[16,2,64,256]{3,2,1,0:T(8,128)(2,1)} copy(bf16[16,2,64,256]{3,0,2,1:T(8,128)(2,1)S(1)} %convolution_convert_fusion) | data formatting | bytes 2097152 | tf_op jit(solution)/shard_map/convert_element_type | solution.py:169
  4.5 8.4 %all-to-all-start = ((bf16[16,2,64,256]{3,2,1,0:T(8,128)(2,1)}), bf16[16,2,64,256]{3,2,1,0:T(8,128)(2,1)}, u32[]{:S(2)}, u32[]{:S(2)}) async-start(bf16[16,2,64,256]{3,2,1,0:T(8,128)(2,1)} %copy.21), calls=%async_computation | async-start | bytes 2097152 | tf_op jit(solution)/shard_map/all_to_all | solution.py:170
  12.9 2.2 %collective-permute-start = (bf16[512,256]{1,0:T(8,128)(2,1)S(1)}, bf16[512,256]{1,0:T(8,128)(2,1)}, u32[]{:S(2)}, u32[]{:S(2)}) collective-permute-start(bf16[512,256]{1,0:T(8,128)(2,1)S(1)} %copy-done.2), channel_id=1, source_target_pairs={{0,1},{1,2},{2,3},{3,4},{4,5},{5,6},{6,7},{7,8},{8,9},{9,10},{10,1... | collective-permute-start | bytes 786440 | tf_op jit(solution)/shard_map/ppermute | solution.py:18
  15.1 1.3 %collective-permute-start.1 = (bf16[512,256]{1,0:T(8,128)(2,1)S(1)}, bf16[512,256]{1,0:T(8,128)(2,1)}, u32[]{:S(2)}, u32[]{:S(2)}) collective-permute-start(bf16[512,256]{1,0:T(8,128)(2,1)S(1)} %copy-done.2), channel_id=1, source_target_pairs={{1,0},{2,1},{3,2},{4,3},{5,4},{6,5},{7,6},{8,7},{9,8},{10,9},{11,1... | collective-permute-start | bytes 786440 | tf_op jit(solution)/shard_map/ppermute | solution.py:19
  16.4 0.1 reshape.48
  16.5 1.2 %reshape_squeeze.3 = bf16[16,64,2,64]{3,2,1,0:T(2,128)(2,1)S(1)} reshape(bf16[1,1,16,64,128]{4,3,2,1,0:T(8,128)(2,1)} %param.13) | data formatting | bytes 524288 | tf_op jit(solution)/shard_map/reshape;squeeze | solution.py:156
  17.7 0.1 copy.18
  17.8 2.5 %broadcast_select_fusion = bf16[2,64,16,2,64]{4,3,2,1,0:T(2,128)(2,1)} fusion(pred[2,16,2]{2,1,0:T(8,128)(4,1)S(1)} %iota_compare_fusion, bf16[16,64,2,64]{3,2,1,0:T(2,128)(2,1)S(1)} %reshape_squeeze.3), kind=kLoop, calls=%fused_computation.4 | loop fusion | flops 262144 | bytes 786496 | tf_op jit(solution)/shard_map/jit(_where)/select_n | solution.py:158
  20.3 4.0 %select_n.29 = bf16[128,2048]{1,0:T(8,128)(2,1)} reshape(bf16[2,64,16,2,64]{4,3,2,1,0:T(2,128)(2,1)} %broadcast_select_fusion) | data formatting | bytes 1048576 | tf_op jit(solution)/shard_map/jit(_where)/select_n | solution.py:158
  24.3 1.2 %pad_maximum_fusion.1 = bf16[1536,256]{1,0:T(8,128)(2,1)S(1)} fusion(bf16[512,256]{1,0:T(8,128)(2,1)} %collective-permute-done.1, bf16[512,256]{1,0:T(8,128)(2,1)} %param.9, bf16[512,256]{1,0:T(8,128)(2,1)} %collective-permute-done), kind=kLoop, calls=%fused_computation.15 | loop fusion | flops 2359296 | bytes 1572864 | tf_op jit(solution)/shard_map/concatenate | solution.py:20
  25.5 2.4 %gather_fusion = bf16[20,256,256]{2,1,0:T(8,128)(2,1)} fusion(bf16[6,256,256]{2,1,0:T(8,128)(2,1)S(1)} %bitcast.49, s32[1024]{0:T(1024)S(1)} %pad_clamp_fusion), kind=kCustom, calls=%fused_computation | custom fusion | bytes 5242960 | tf_op jit(solution)/shard_map/gather | solution.py:148
  27.9 3.5 %fusion.4 = f32[2,256,256]{1,2,0:T(8,128)} fusion(bf16[2,10,256,256]{3,2,1,0:T(8,128)(2,1)S(1)} %copy-done, bf16[2,10,256,256]{3,2,1,0:T(8,128)(2,1)} %bitcast.50, pred[2,10]{1,0:T(4,128)(4,1)S(1)} %broadcast_compare_fusion), kind=kOutput, calls=%fused_computation.7 | convolution fusion | flops 672399360 | bytes 5767188 | tf_op jit(solution)/shard_map/lkab,lkbs->las/dot_general | solution.py:150
  31.4 6.0 %all-to-all-done = bf16[16,2,64,256]{3,2,1,0:T(8,128)(2,1)} async-done(((bf16[16,2,64,256]{3,2,1,0:T(8,128)(2,1)}), bf16[16,2,64,256]{3,2,1,0:T(8,128)(2,1)}, u32[]{:S(2)}, u32[]{:S(2)}) %all-to-all-start) | async-done | bytes 1048608 | tf_op jit(solution)/shard_map/all_to_all | solution.py:170
  37.4 1.5 %convolution_convert_fusion.1 = bf16[128,256]{1,0:T(8,128)(2,1)S(1)} fusion(bf16[128,2048]{1,0:T(8,128)(2,1)S(1)} %copy-done.1, bf16[2048,256]{1,0:T(8,128)(2,1)} %bitcast.11), kind=kOutput, calls=%fused_computation.12 | convolution fusion | flops 134250496 | bytes 1638400 | tf_op jit(solution)/shard_map/dot_general | solution.py:171
  39.0 1.3 %fusion.7 = bf16[2,256,256]{1,2,0:T(8,128)(2,1)S(1)} fusion(f32[2,256,256]{1,2,0:T(8,128)} %fusion.4, bf16[2,64,256]{2,1,0:T(8,128)(2,1)S(1)} %bitcast.52, bf16[2,64,256]{2,1,0:T(8,128)(2,1)S(1)} %copy-done.4), kind=kOutput, calls=%fused_computation.9 | convolution fusion | flops 17039360 | bytes 917504 | tf_op jit(solution)/shard_map/lra,lrs->las/dot_general | solution.py:177
  40.3 0.3 fusion.8
  40.6 0.3 collective-permute-start.2
  40.9 1.1 %collective-permute-done.2 = bf16[256,256]{1,0:T(8,128)(2,1)S(1)} collective-permute-done((bf16[256,256]{1,0:T(8,128)(2,1)S(1)}, bf16[256,256]{1,0:T(8,128)(2,1)S(1)}, u32[]{:S(2)}, u32[]{:S(2)}) %collective-permute-start.2) | collective-permute-done | bytes 131104 | tf_op jit(solution)/shard_map/ppermute | solution.py:27
  42.0 1.1 %collective-permute-start.3 = (bf16[256,256]{1,0:T(8,128)(2,1)S(1)}, bf16[256,256]{1,0:T(8,128)(2,1)S(1)}, u32[]{:S(2)}, u32[]{:S(2)}) collective-permute-start(bf16[256,256]{1,0:T(8,128)(2,1)S(1)} %fusion.10), channel_id=1, source_target_pairs={{0,2},{2,0},{4,6},{6,4},{8,10},{10,8},{12,14},{14,12},{16,18},{18,... | collective-permute-start | bytes 393224 | tf_op jit(solution)/shard_map/ppermute | solution.py:27
  43.2 4.6 %collective-permute-done.3 = bf16[256,256]{1,0:T(8,128)(2,1)S(1)} collective-permute-done((bf16[256,256]{1,0:T(8,128)(2,1)S(1)}, bf16[256,256]{1,0:T(8,128)(2,1)S(1)}, u32[]{:S(2)}, u32[]{:S(2)}) %collective-permute-start.3) | collective-permute-done | bytes 131104 | tf_op jit(solution)/shard_map/ppermute | solution.py:27
  47.8 0.1 fusion.22
  47.8 3.6 %collective-permute-start.4 = (bf16[256,256]{1,0:T(8,128)(2,1)S(1)}, bf16[256,256]{1,0:T(8,128)(2,1)S(1)}, u32[]{:S(2)}, u32[]{:S(2)}) collective-permute-start(bf16[256,256]{1,0:T(8,128)(2,1)S(1)} %get-tuple-element.10), channel_id=1, source_target_pairs={{0,4},{2,6},{4,0},{6,2},{8,12},{10,14},{12,8},{14,10},{16,20},{18,... | collective-permute-start | bytes 393224 | tf_op jit(solution)/shard_map/ppermute | solution.py:27
  51.5 3.4 %collective-permute-done.4 = bf16[256,256]{1,0:T(8,128)(2,1)S(1)} collective-permute-done((bf16[256,256]{1,0:T(8,128)(2,1)S(1)}, bf16[256,256]{1,0:T(8,128)(2,1)S(1)}, u32[]{:S(2)}, u32[]{:S(2)}) %collective-permute-start.4) | collective-permute-done | bytes 131104 | tf_op jit(solution)/shard_map/ppermute | solution.py:27
  54.9 0.1 fusion.13
  55.0 8.9 %collective-permute-start.5 = (bf16[256,256]{1,0:T(8,128)(2,1)S(1)}, bf16[256,256]{1,0:T(8,128)(2,1)S(1)}, u32[]{:S(2)}, u32[]{:S(2)}) collective-permute-start(bf16[256,256]{1,0:T(8,128)(2,1)S(1)} %get-tuple-element.8), channel_id=1, source_target_pairs={{0,8},{2,10},{4,12},{6,14},{8,0},{10,2},{12,4},{14,6},{16,24},{18,... | collective-permute-start | bytes 393224 | tf_op jit(solution)/shard_map/ppermute | solution.py:27
  63.9 2.9 %collective-permute-done.5 = bf16[256,256]{1,0:T(8,128)(2,1)S(1)} collective-permute-done((bf16[256,256]{1,0:T(8,128)(2,1)S(1)}, bf16[256,256]{1,0:T(8,128)(2,1)S(1)}, u32[]{:S(2)}, u32[]{:S(2)}) %collective-permute-start.5) | collective-permute-done | bytes 131104 | tf_op jit(solution)/shard_map/ppermute | solution.py:27
  66.9 0.1 multiply_bitcast_fusion
  67.0 0.1 pad_maximum_fusion.g_ref
  67.1 11.6 %shard_map.103 = (f32[256,256]{1,0:T(8,128)}, bf16[3,256,256]{2,1,0:T(8,128)(2,1)}) custom-call(f32[4,256,256]{2,1,0:T(8,128)S(1)} %pad_maximum_fusion.g_ref), custom_call_target="tpu_custom_call" | custom-call | tf_op jit(solution)/shard_map/pallas_call | solution.py:114
  (20 shorter events, 0.1 us)
Async XLA Ops:
  0.6 27.2 %copy-start = (bf16[2,10,256,256]{3,2,1,0:T(8,128)(2,1)S(1)}, bf16[2,10,256,256]{3,2,1,0:T(8,128)(2,1)}, u32[]{:S(2)}) copy-start(bf16[2,10,256,256]{3,2,1,0:T(8,128)(2,1)} %param.8) | copy-start | bytes 7864324
  1.9 11.0 %copy-start.2 = (bf16[512,256]{1,0:T(8,128)(2,1)S(1)}, bf16[512,256]{1,0:T(8,128)(2,1)}, u32[]{:S(2)}) copy-start(bf16[512,256]{1,0:T(8,128)(2,1)} %param.9) | copy-start | bytes 786436
  2.0 14.4 %copy-start.6 = (s32[2,10]{1,0:T(2,128)S(1)}, s32[2,10]{1,0:T(2,128)}, u32[]{:S(2)}) copy-start(s32[2,10]{1,0:T(2,128)} %param.10) | copy-start | bytes 244
  3.2 14.5 %copy-start.5 = (s32[1,1,16,2]{2,3,1,0:T(2,128)S(1)}, s32[1,1,16,2]{2,3,1,0:T(2,128)}, u32[]{:S(2)}) copy-start(s32[1,1,16,2]{2,3,1,0:T(2,128)} %param.15) | copy-start | bytes 388
  4.5 32.9 %all-to-all-start = ((bf16[16,2,64,256]{3,2,1,0:T(8,128)(2,1)}), bf16[16,2,64,256]{3,2,1,0:T(8,128)(2,1)}, u32[]{:S(2)}, u32[]{:S(2)}) async-start(bf16[16,2,64,256]{3,2,1,0:T(8,128)(2,1)} %copy.21), calls=%async_computation | async-start | bytes 2097152 | tf_op jit(solution)/shard_map/all_to_all | solution.py:170
  12.9 11.4 %collective-permute-start = (bf16[512,256]{1,0:T(8,128)(2,1)S(1)}, bf16[512,256]{1,0:T(8,128)(2,1)}, u32[]{:S(2)}, u32[]{:S(2)}) collective-permute-start(bf16[512,256]{1,0:T(8,128)(2,1)S(1)} %copy-done.2), channel_id=1, source_target_pairs={{0,1},{1,2},{2,3},{3,4},{4,5},{5,6},{6,7},{7,8},{8,9},{9,10},{10,1... | collective-permute-start | bytes 786440 | tf_op jit(solution)/shard_map/ppermute | solution.py:18
  15.1 9.2 %collective-permute-start.1 = (bf16[512,256]{1,0:T(8,128)(2,1)S(1)}, bf16[512,256]{1,0:T(8,128)(2,1)}, u32[]{:S(2)}, u32[]{:S(2)}) collective-permute-start(bf16[512,256]{1,0:T(8,128)(2,1)S(1)} %copy-done.2), channel_id=1, source_target_pairs={{1,0},{2,1},{3,2},{4,3},{5,4},{6,5},{7,6},{8,7},{9,8},{10,9},{11,1... | collective-permute-start | bytes 786440 | tf_op jit(solution)/shard_map/ppermute | solution.py:19
  27.9 9.6 %copy-start.1 = (bf16[128,2048]{1,0:T(8,128)(2,1)S(1)}, bf16[128,2048]{1,0:T(8,128)(2,1)}, u32[]{:S(2)}) copy-start(bf16[128,2048]{1,0:T(8,128)(2,1)} %select_n.29) | copy-start | bytes 1572868
  27.9 11.1 %copy-start.4 = (bf16[2,64,256]{2,1,0:T(8,128)(2,1)S(1)}, bf16[2,64,256]{2,1,0:T(8,128)(2,1)}, u32[]{:S(2)}) copy-start(bf16[2,64,256]{2,1,0:T(8,128)(2,1)} %param.11) | copy-start | bytes 196612
  40.3 26.8 %copy-start.3 = (bf16[2,256,256]{1,2,0:T(8,128)(2,1)}, bf16[2,256,256]{1,2,0:T(8,128)(2,1)S(1)}, u32[]{:S(2)}) copy-start(bf16[2,256,256]{1,2,0:T(8,128)(2,1)S(1)} %fusion.7) | copy-start | bytes 786436
  40.6 1.4 %collective-permute-start.2 = (bf16[256,256]{1,0:T(8,128)(2,1)S(1)}, bf16[256,256]{1,0:T(8,128)(2,1)S(1)}, u32[]{:S(2)}, u32[]{:S(2)}) collective-permute-start(bf16[256,256]{1,0:T(8,128)(2,1)S(1)} %fusion.8), channel_id=1, source_target_pairs={{0,1},{1,0},{2,3},{3,2},{4,5},{5,4},{6,7},{7,6},{8,9},{9,8},{10,11... | collective-permute-start | bytes 393224 | tf_op jit(solution)/shard_map/ppermute | solution.py:27
  42.0 5.7 %collective-permute-start.3 = (bf16[256,256]{1,0:T(8,128)(2,1)S(1)}, bf16[256,256]{1,0:T(8,128)(2,1)S(1)}, u32[]{:S(2)}, u32[]{:S(2)}) collective-permute-start(bf16[256,256]{1,0:T(8,128)(2,1)S(1)} %fusion.10), channel_id=1, source_target_pairs={{0,2},{2,0},{4,6},{6,4},{8,10},{10,8},{12,14},{14,12},{16,18},{18,... | collective-permute-start | bytes 393224 | tf_op jit(solution)/shard_map/ppermute | solution.py:27
  47.8 7.1 %collective-permute-start.4 = (bf16[256,256]{1,0:T(8,128)(2,1)S(1)}, bf16[256,256]{1,0:T(8,128)(2,1)S(1)}, u32[]{:S(2)}, u32[]{:S(2)}) collective-permute-start(bf16[256,256]{1,0:T(8,128)(2,1)S(1)} %get-tuple-element.10), channel_id=1, source_target_pairs={{0,4},{2,6},{4,0},{6,2},{8,12},{10,14},{12,8},{14,10},{16,20},{18,... | collective-permute-start | bytes 393224 | tf_op jit(solution)/shard_map/ppermute | solution.py:27
  55.0 11.9 %collective-permute-start.5 = (bf16[256,256]{1,0:T(8,128)(2,1)S(1)}, bf16[256,256]{1,0:T(8,128)(2,1)S(1)}, u32[]{:S(2)}, u32[]{:S(2)}) collective-permute-start(bf16[256,256]{1,0:T(8,128)(2,1)S(1)} %get-tuple-element.8), channel_id=1, source_target_pairs={{0,8},{2,10},{4,12},{6,14},{8,0},{10,2},{12,4},{14,6},{16,24},{18,... | collective-permute-start | bytes 393224 | tf_op jit(solution)/shard_map/ppermute | solution.py:27

commit v2 on v1

v2 whole, which is shorter than its diff:
```python
import jax
import jax.numpy as jnp
from jax import lax
from jax.experimental import pallas as pl
from jax.experimental.pallas import tpu as pltpu
from jax.sharding import PartitionSpec as P

LEVELS = 3
AXES = ("seg", "sub")
VMEM = pl.BlockSpec(memory_space=pltpu.VMEM)
SMEM = pl.BlockSpec(memory_space=pltpu.SMEM)


def params(**more):
    return pltpu.CompilerParams(vmem_limit_bytes=48 * 2**20, **more)


def hop(value, even, odd):
    n_seg, n_sub = lax.axis_size("seg"), lax.axis_size("sub")
    pairs = []
    for s in range(n_seg):
        for u in range(n_sub):
            mask = odd if u % 2 else even
            if mask:
                pairs.append((s * n_sub + u, (s ^ mask) * n_sub + u))
    return lax.ppermute(value, AXES, pairs)


def sub_hop(value, mask):
    return lax.ppermute(value, "sub", [(i, i ^ mask) for i in range(lax.axis_size("sub"))])


def pack(top, low):
    lane = lax.broadcasted_iota(jnp.int32, (64, 128), 1)
    corner = pltpu.roll(low[64:128, :], 64, 1)
    mixed = jnp.where(lane < 64, corner, top[64:128, 0:128])
    return jnp.concatenate([top[0:64, 0:128], mixed, top[:, 128:256], low[0:64, :]], 0)


def unpack(packed):
    zero = jnp.zeros((64, 128), jnp.float32)
    left = jnp.concatenate([packed[0:128, :], zero, zero], 0)
    right = jnp.concatenate(
        [packed[128:256, :], packed[256:320, :], pltpu.roll(packed[64:128, :], 64, 1)], 0
    )
    return jnp.concatenate([left, right], 1)


def dot(a, b):
    return jnp.dot(a, b, preferred_element_type=jnp.float32)


def dot_t(a, b):
    return lax.dot_general(a, b, (((0,), (0,)), ((), ())), preferred_element_type=jnp.float32)


def project_kernel(basis_ref, cols_ref, source_ref, out_ref):
    leaves, rank, rows = basis_ref.shape
    lane = lax.broadcasted_iota(jnp.int32, (8, 256), 1)
    flags = jnp.zeros((8, 256), jnp.float32)
    for s in range(source_ref.shape[0]):
        for c in range(source_ref.shape[1]):
            flags = jnp.where(
                lane == s * source_ref.shape[1] + c, source_ref[s, c].astype(jnp.float32), flags
            )
    for l in range(leaves):
        out_ref[0, l * rank : (l + 1) * rank, :] = dot(
            basis_ref[l], cols_ref[l * rows : (l + 1) * rows, :]
        ).astype(jnp.bfloat16)
    out_ref[0, leaves * rank : leaves * rank + 8, :] = flags.astype(jnp.bfloat16)


def near_kernel(list_ref, blocks_ref, own_ref, swap_ref, cross_ref, out_ref, held):
    leaf = pl.program_id(0)
    leaves = held.shape[0] // 3

    @pl.when(leaf == 0)
    def _():
        for j in range(leaves):
            rows = slice(j * 256, (j + 1) * 256)
            held[j] = own_ref[rows, :]
            held[leaves + j] = swap_ref[rows, :]
            held[2 * leaves + j] = cross_ref[rows, :]
        held[3 * leaves] = jnp.zeros_like(held[0])

    device = lax.axis_index("seg") * lax.axis_size("sub") + lax.axis_index("sub")
    odd = device % 2
    before = (2 - odd) * leaves
    after = (1 + odd) * leaves
    acc = jnp.zeros((256, 256), jnp.float32)
    for k in range(blocks_ref.shape[1]):
        entry = list_ref[leaf, k]
        shift = entry - device * leaves
        slot = jnp.where(
            shift < 0, before + leaves + shift, jnp.where(shift < leaves, shift, after + shift - leaves)
        )
        slot = jnp.where(entry < 0, 3 * leaves, slot)
        acc = acc + dot(blocks_ref[0, k], held[slot])
    out_ref[...] = acc


def combine_kernel(dest_ref, couplings_ref, basis_ref, near_ref, *refs):
    b_ref, q1, q2, q3, z_ref, r1, r2, r3, samples_ref, gram_ref = refs
    me = lax.axis_index("seg")
    leaves, rank, rows = basis_ref.shape
    slots = dest_ref.shape[1]
    blocks = [(b_ref, 0, 0), (q1, 0, 1), (q2, 0, 2), (q3, 0, 3)]
    for mask, ref in ((0, z_ref), (1, r1), (2, r2), (3, r3)):
        blocks += [(ref, k, mask ^ (4 * k + 4)) for k in range(ref.shape[0])]
    lane8 = lax.broadcasted_iota(jnp.int32, (8, 256), 1)
    lane = lax.broadcasted_iota(jnp.int32, (1, slots * rank), 1)
    total = jnp.zeros((leaves * rank, 256), jnp.float32)
    for ref, k, mask in blocks:
        source = me ^ mask
        flags = ref[k, leaves * rank : leaves * rank + 8, :].astype(jnp.float32)
        projected = [ref[k, y * rank : (y + 1) * rank, :] for y in range(leaves)]
        chosen = []
        for c in range(slots):
            flag = jnp.sum(
                jnp.where(lane8 == me * slots + c, flags, 0.0), axis=1, keepdims=True
            )[0:1, :]
            flag = jnp.broadcast_to(flag, (1, 256))
            chosen.append(
                sum(
                    projected[y] * jnp.where(flag == y, 1.0, 0.0).astype(jnp.bfloat16)
                    for y in range(leaves)
                )
            )
        matrix = couplings_ref[source]
        routed = []
        for l in range(leaves):
            weight = jnp.zeros((1, slots * rank), jnp.float32)
            for c in range(slots):
                hit = jnp.where(dest_ref[source, c] == l, 1.0, 0.0)
                weight = jnp.where((lane >= c * rank) & (lane < (c + 1) * rank), hit, weight)
            routed.append(matrix * weight.astype(jnp.bfloat16))
        total = total + dot(jnp.concatenate(routed, 0), jnp.concatenate(chosen, 0))
    coeff = total.astype(jnp.bfloat16)
    for l in range(leaves):
        far = dot_t(basis_ref[l], coeff[l * rank : (l + 1) * rank, :])
        at = slice(l * rows, (l + 1) * rows)
        samples_ref[at, :] = (near_ref[at, :] + far).astype(jnp.bfloat16)
    left, right = samples_ref[:, 0:128], samples_ref[:, 128:256]
    top = dot_t(left, samples_ref[...])
    gram_ref[...] = pack(top, dot_t(right, right))


def rb(x,k): return jnp.broadcast_to(x[k:k+1,:],(8,128))

def split(a):
    h=a.astype(jnp.bfloat16); return h,(a-h.astype(jnp.float32)).astype(jnp.bfloat16)
def dg(a,b,dims): return lax.dot_general(a,b,(dims,((),())),preferred_element_type=jnp.float32)
def mm3(a,b,dims):
    ah,al=split(a); bh,bl=split(b)
    return dg(ah,bh,dims)+dg(ah,bl,dims)+dg(al,bh,dims)
def mm(a,b): return mm3(a,b,((1,),(0,)))
def mmt(a,b): return mm3(a,b,((1,),(1,)))
def eliminate(P, lane, row):
    base=lane & ~31
    sub=lane & 31
    V=[jnp.where(row+8*rv==sub,1.0,0.0).astype(jnp.float32) for rv in range(4)]
    P=list(P)
    for m in range(4):
        C=[[jnp.take_along_axis(P[rv],base+(8*m+k),axis=1,mode="promise_in_bounds") for rv in range(m,4)] for k in range(8)]
        piv=jnp.ones((8,128),jnp.float32)
        for k in range(8):
            d=rb(C[k][0],k)
            piv=jnp.where(row==k,d,piv)
            inv=1.0/d
            M=[c*inv for c in C[k]]
            M[0]=jnp.where(row>k,M[0],0.0)
            for k2 in range(k+1,8):
                f=rb(C[k2][0],k)
                C[k2]=[c-mu*f for c,mu in zip(C[k2],M)]
            fp=rb(P[m],k); fv=rb(V[m],k)
            for rv in range(m,4):
                P[rv]=P[rv]-M[rv-m]*fp
                V[rv]=V[rv]-M[rv-m]*fv
        rs=lax.rsqrt(piv)
        P[m]=P[m]*rs
        V[m]=V[m]*rs
    return P,V

def factor_kernel(seg_ref, mine_ref, other_ref, r_ref, tr_ref, X, Rb, Wb):
    lane=lax.broadcasted_iota(jnp.int32,(8,128),1); row=lax.broadcasted_iota(jnp.int32,(8,128),0)
    grp=lane//32
    l32=lax.broadcasted_iota(jnp.int32,(32,256),1)
    r32=lax.broadcasted_iota(jnp.int32,(32,256),0)
    bd=(lax.broadcasted_iota(jnp.int32,(128,128),0)//32)==(lax.broadcasted_iota(jnp.int32,(128,128),1)//32)
    l256=lax.broadcasted_iota(jnp.int32,(128,256),1); r256=lax.broadcasted_iota(jnp.int32,(128,256),0)&31
    odd = (lax.axis_index("sub") % 2) == 1
    mine, other = mine_ref[...], other_ref[...]
    first = jnp.where(odd, other, mine)
    second = jnp.where(odd, mine[0], other[0])
    levels = [seg_ref[...], first[0], first[1], (first[1] + second) * 0.5]
    for t, packed in enumerate(levels):
        rows = unpack(packed)
        for kb in range(8):
            X[kb, 32 * t : 32 * t + 32, :] = rows[32 * kb : 32 * kb + 32, :]
    for kb in range(8):
        off=32*kb; c0=off//128*128; lo=off%128
        P=[]
        for rv in range(4):
            acc=None
            for t in range(4):
                v=X[kb,t*32+8*rv:t*32+8*rv+8,c0:c0+128]
                sh=(32*t-lo)%128
                if sh: v=pltpu.roll(v,sh,1)
                acc=v if acc is None else jnp.where(grp==t,v,acc)
            P.append(acc)
        P,V=eliminate(P,lane,row)
        Pf=jnp.concatenate(P,0); Vf=jnp.concatenate(V,0)
        Wbd=jnp.where(bd,jnp.concatenate([Vf]*4,0),0.0)
        x=X[kb]
        x=jnp.where((l256>=off)&(l256<off+32),jnp.where(l256-off==r256,1.0,0.0),x)
        panel=mm(Wbd,x)
        chunks={}
        for i in range(kb+1,8):
            c=i//4
            if c not in chunks: chunks[c]=jnp.transpose(panel[:,c*128:c*128+128])
            T=chunks[c][(i%4)*32:(i%4)*32+32,:]
            L=jnp.where(bd,jnp.concatenate([T]*4,0),0.0)
            X[i]=jnp.where((l256>=off)&(l256<off+32),0.0,X[i])-mm(L,panel)
        for t in range(4):
            pt=panel[32*t:32*t+32,:]
            sh=(lo-32*t)%128
            d=Pf
            if sh: d=pltpu.roll(d,sh,1)
            d2=jnp.concatenate([d,d],1)
            Rb[t,off:off+32,:]=jnp.where(l32>=off+32,pt,jnp.where((l32>=off)&(l32-off>=r32),d2,0.0))
            if t>0: Wb[t-1,off:off+32,:]=jnp.where(l32<off+32,pt,0.0)
    r_ref[...]=Rb[0]
    for t in range(3):
        tr_ref[t]=mmt(Rb[t],Wb[t]).astype(jnp.bfloat16)

def factor_all(seg_gram, mine, other):
    return pl.pallas_call(
        factor_kernel,
        out_shape=(
            jax.ShapeDtypeStruct((256, 256), jnp.float32),
            jax.ShapeDtypeStruct((LEVELS, 256, 256), jnp.bfloat16),
        ),
        in_specs=[VMEM] * 3,
        out_specs=[VMEM] * 2,
        scratch_shapes=[
            pltpu.VMEM((8, 128, 256), jnp.float32),
            pltpu.VMEM((4, 256, 256), jnp.float32),
            pltpu.VMEM((3, 256, 256), jnp.float32),
        ],
        compiler_params=params(),
    )(seg_gram, mine, other)


def body(
    near_blocks, sample_cols, near_list, row_basis_t, col_basis_t, couplings, far_source, far_dest
):
    leaf_count, near_count, leaf_rows, _ = near_blocks.shape
    width = sample_cols.shape[1]
    rank = row_basis_t.shape[1]
    n_seg, n_sub = lax.axis_size("seg"), lax.axis_size("sub")
    n = n_seg * n_sub
    rows = leaf_count * leaf_rows

    swap = lax.ppermute(sample_cols, AXES, [(i, i ^ 1) for i in range(n)])
    ahead = [(i, i + 1) for i in range(1, n - 1, 2)]
    cross = lax.ppermute(sample_cols, AXES, ahead + [(j, i) for i, j in ahead])

    mine = pl.pallas_call(
        project_kernel,
        out_shape=jax.ShapeDtypeStruct((1, leaf_count * rank + 8, width), jnp.bfloat16),
        in_specs=[VMEM, VMEM, SMEM],
        out_specs=VMEM,
        compiler_params=params(),
        cost_estimate=pl.CostEstimate(
            flops=2 * rows * rank * width, bytes_accessed=512 * 2**10, transcendentals=0
        ),
    )(col_basis_t, sample_cols, far_source[0, 0])

    high = [hop(mine, m, m) for m in range(4, n_seg, 4)]
    low = [hop(mine, m, m) for m in (1, 2, 3)]
    column = jnp.concatenate(high, 0)
    rest = [hop(column, m, m) for m in (1, 2, 3)]

    near_part = pl.pallas_call(
        near_kernel,
        grid=(leaf_count,),
        out_shape=jax.ShapeDtypeStruct((rows, width), jnp.float32),
        in_specs=[
            SMEM,
            pl.BlockSpec((1, near_count, leaf_rows, leaf_rows), lambda i: (i, 0, 0, 0)),
            VMEM,
            VMEM,
            VMEM,
        ],
        out_specs=pl.BlockSpec((leaf_rows, width), lambda i: (i, 0)),
        scratch_shapes=[pltpu.VMEM((3 * leaf_count + 1, leaf_rows, width), jnp.bfloat16)],
        compiler_params=params(),
        cost_estimate=pl.CostEstimate(
            flops=2 * rows * near_count * leaf_rows * width,
            bytes_accessed=near_blocks.size * 2 + 5 * rows * width * 2,
            transcendentals=0,
        ),
    )(near_list, near_blocks, sample_cols, swap, cross)

    samples, gram = pl.pallas_call(
        combine_kernel,
        out_shape=(
            jax.ShapeDtypeStruct((rows, width), jnp.bfloat16),
            jax.ShapeDtypeStruct((320, 128), jnp.float32),
        ),
        in_specs=[SMEM] + [VMEM] * 11,
        out_specs=[VMEM] * 2,
        compiler_params=params(),
    )(far_dest[0, 0], couplings[0, 0], row_basis_t, near_part, mine, *low, column, *rest)

    total, mask = gram, 1
    while mask < n_sub:
        total = total + sub_hop(total, mask)
        mask *= 2
    seg_gram = total / (n_sub * rows)
    rounded = seg_gram.astype(jnp.bfloat16)
    got = [
        hop(rounded, *masks).astype(jnp.float32) for masks in ((1, 4), (2, 6), (3, 5), (None, 7))
    ]
    odd = (lax.axis_index("sub") % 2) == 1
    pair = seg_gram + got[0]
    quad = (got[1] + got[2]) + pair
    far_quad = (got[0] + got[1]) + (got[2] + got[3])
    sent = jnp.stack([jnp.where(odd, far_quad * 0.25, pair * 0.5), quad * 0.25])
    received = sub_hop(sent, 1)
    segment_factor, transfers = factor_all(seg_gram, sent, received)
    return (samples, segment_factor, transfers[None])


def solution(mesh):
    in_specs = (
        P(("seg", "sub"), None, None, None),
        P(("seg", "sub"), None),
        P(("seg", "sub"), None),
        P(("seg", "sub"), None, None),
        P(("seg", "sub"), None, None),
        P("seg", "sub", None, None, None),
        P("seg", "sub", None, None),
        P("seg", "sub", None, None),
    )
    out_specs = (P(("seg", "sub"), None), P("seg", None), P("seg", None, None, None))
    return jax.shard_map(body, mesh=mesh, in_specs=in_specs, out_specs=out_specs, check_vma=False)
```

time: 79.5 us -> 63.5 us (0.80)
  matrix products: 9.21 us -> 0 us
  Pallas kernels: 11.6 us -> 16.4 us
  waiting for transfers between devices: 18.1 us -> 14 us
  other arithmetic: 4.05 us -> 0.13 us
  local copies, waits for them, and re-layouts: 9.11 us -> 6.69 us
    dot_general x6 -> x0, matrix products: 9.21 us -> none  [the longest x1 3.55 us: body(): jnp.einsum('lkab,lkbs->las', near_blocks, chosen, preferred_element_type=...]
    all_to_all x1 -> x0, starting transfers between devices: 8.36 us -> none  [body(): lax.all_to_all(outgoing, 'seg', split_axis=0, concat_axis=0, tiled=True)]
    ppermute x6 -> x17, starting transfers between devices: 17.5 us -> 25.2 us  [the longest x13 20.1 us: hop(): return lax.ppermute(value, AXES, pairs)]
    all_to_all x1 -> x0, waiting for transfers between devices: 6.01 us -> none  [body(): lax.all_to_all(outgoing, 'seg', split_axis=0, concat_axis=0, tiled=True)]
    unnamed x14 -> x16, local copies, waits for them, and re-layouts: 0.04 us -> 5.17 us
    pallas_call x0 -> x3, Pallas kernels: none -> 4.83 us  [the longest x1 2.3 us: body(): pl.pallas_call(combine_kernel, out_shape=(jax.ShapeDtypeStruct((rows, wid...]
    select_n x1 -> x0, local copies, waits for them, and re-layouts: 4.04 us -> none  [body(): jnp.where(jnp.transpose(routing, (2, 0, 1))[:, None, :, :, None], couplin...]
    select_n x2 -> x0, other arithmetic: 2.47 us -> none  [the longest x1 2.46 us: body(): jnp.where(jnp.transpose(routing, (2, 0, 1))[:, None, :, :, None], couplin...]
  transfers between devices with their start and end apart: 7 -> 17, of which waited for: 5 -> 6; matrix products, arithmetic and copies ran while one was open for 19% -> 1% of each run, Pallas kernels for 0% -> 3%
where the time goes in v2:
time: 63.5 us; the launch traced here: 63.2 us
  starting transfers between devices  25.2 us (40%)
  Pallas kernels  16.4 us (26%)
  waiting for transfers between devices  14 us (22%)
  local copies, waits for them, and re-layouts  6.69 us (11%)
  between operations  0.75 us (1%)
    ppermute x13, starting transfers between devices, hop(): return lax.ppermute(value, AXES, pairs)  20.1 us
    pallas_call x1, Pallas kernels, factor_all(): pl.pallas_call(factor_kernel, out_shape=(jax.ShapeDtypeStruct((256, 256),...  11.6 us
    ppermute x13, waiting for transfers between devices, hop(): return lax.ppermute(value, AXES, pairs)  11.4 us
    unnamed x16, local copies, waits for them, and re-layouts  5.17 us
    ppermute x2, starting transfers between devices, sub_hop(): lax.ppermute(value, 'sub', [(i, i ^ mask) for i in range(lax.axis_size('s...  4.37 us
    ppermute x2, waiting for transfers between devices, sub_hop(): lax.ppermute(value, 'sub', [(i, i ^ mask) for i in range(lax.axis_size('s...  2.65 us
    pallas_call x1, Pallas kernels, body(): pl.pallas_call(combine_kernel, out_shape=(jax.ShapeDtypeStruct((rows, wid...  2.3 us
    pallas_call x1, Pallas kernels, body(): pl.pallas_call(near_kernel, grid=(leaf_count,), out_shape=jax.ShapeDtypeS...  1.7 us
  transfers between devices with their start and end apart: 17, of which 6 were waited for; matrix products, arithmetic and copies ran while one was open for 1% of the time, Pallas kernels for 3%

profile of v2, /device:TPU:0, one launch (start us, length us, event | category | flops | bytes accessed | tf_op | source)
XLA Modules:
  0.0 63.2 jit_solution(1845721403729055318)
XLA Ops:
  0.6 0.8 %copy.11.source_ref = s32[16,2]{1,0:T(8,128)S(1)} copy(s32[16,2]{0,1:T(2,128)} %bitcast.9) | data formatting | bytes 256 | tf_op jit(solution)/shard_map/squeeze | solution.py:277
  1.4 0.9 %copy-done.1 = bf16[512,256]{1,0:T(8,128)(2,1)S(1)} copy-done((bf16[512,256]{1,0:T(8,128)(2,1)S(1)}, bf16[512,256]{1,0:T(8,128)(2,1)}, u32[]{:S(2)}) %copy-start.1) | copy-done | bytes 262168
  2.3 0.8 %copy-done.4 = bf16[2,64,256]{2,1,0:T(8,128)(2,1)S(1)} copy-done((bf16[2,64,256]{2,1,0:T(8,128)(2,1)S(1)}, bf16[2,64,256]{2,1,0:T(8,128)(2,1)}, u32[]{:S(2)}) %copy-start.4) | copy-done | bytes 65560
  3.2 0.8 %shard_map.104.refs_0_ = bf16[1,136,256]{2,1,0:T(8,128)(2,1)S(1)} custom-call(bf16[2,64,256]{2,1,0:T(8,128)(2,1)S(1)} %copy-done.4, bf16[512,256]{1,0:T(8,128)(2,1)S(1)} %copy-done.1, s32[16,2]{1,0:T(8,128)S(1)} %copy.11.source_ref), custom_call_target="tpu_custom_call" | custom-call | flops 16777216 | bytes 524288 | tf_op jit(solution)/shard_map/pallas_call | solution.py:268
  4.0 3.1 %collective-permute-start.5 = (bf16[1,136,256]{2,1,0:T(8,128)(2,1)S(1)}, bf16[1,136,256]{2,1,0:T(8,128)(2,1)S(1)}, u32[]{:S(2)}, u32[]{:S(2)}) collective-permute-start(bf16[1,136,256]{2,1,0:T(8,128)(2,1)S(1)} %shard_map.104.refs_0_), channel_id=1, source_target_pairs={{0,8},{1,9},{2,10},{3,11},{4,12},{5,13},{6,14},{7,15},{8,0},{9,1},... | collective-permute-start | bytes 208904 | tf_op jit(solution)/shard_map/ppermute | solution.py:26
  7.1 0.7 %collective-permute-start.1 = (bf16[512,256]{1,0:T(8,128)(2,1)S(1)}, bf16[512,256]{1,0:T(8,128)(2,1)S(1)}, u32[]{:S(2)}, u32[]{:S(2)}) collective-permute-start(bf16[512,256]{1,0:T(8,128)(2,1)S(1)} %copy-done.1), channel_id=1, source_target_pairs={{1,2},{3,4},{5,6},{7,8},{9,10},{11,12},{13,14},{15,16},{17,18},{19... | collective-permute-start | bytes 786440 | tf_op jit(solution)/shard_map/ppermute | solution.py:266
  7.8 3.4 %collective-permute-start.2 = (bf16[1,136,256]{2,1,0:T(8,128)(2,1)S(1)}, bf16[1,136,256]{2,1,0:T(8,128)(2,1)S(1)}, u32[]{:S(2)}, u32[]{:S(2)}) collective-permute-start(bf16[1,136,256]{2,1,0:T(8,128)(2,1)S(1)} %shard_map.104.refs_0_), channel_id=1, source_target_pairs={{0,2},{1,3},{2,0},{3,1},{4,6},{5,7},{6,4},{7,5},{8,10},{9,11},{10,... | collective-permute-start | bytes 208904 | tf_op jit(solution)/shard_map/ppermute | solution.py:26
  11.2 2.6 %collective-permute-start.6 = (bf16[1,136,256]{2,1,0:T(8,128)(2,1)S(1)}, bf16[1,136,256]{2,1,0:T(8,128)(2,1)S(1)}, u32[]{:S(2)}, u32[]{:S(2)}) collective-permute-start(bf16[1,136,256]{2,1,0:T(8,128)(2,1)S(1)} %shard_map.104.refs_0_), channel_id=1, source_target_pairs={{0,16},{1,17},{2,18},{3,19},{4,20},{5,21},{6,22},{7,23},{8,24},{9,... | collective-permute-start | bytes 208904 | tf_op jit(solution)/shard_map/ppermute | solution.py:26
  13.8 1.7 %collective-permute-start.7 = (bf16[1,136,256]{2,1,0:T(8,128)(2,1)S(1)}, bf16[1,136,256]{2,1,0:T(8,128)(2,1)S(1)}, u32[]{:S(2)}, u32[]{:S(2)}) collective-permute-start(bf16[1,136,256]{2,1,0:T(8,128)(2,1)S(1)} %shard_map.104.refs_0_), channel_id=1, source_target_pairs={{0,24},{1,25},{2,26},{3,27},{4,28},{5,29},{6,30},{7,31},{8,16},{9,... | collective-permute-start | bytes 208904 | tf_op jit(solution)/shard_map/ppermute | solution.py:26
  15.5 6.9 %collective-permute-done.6 = bf16[1,136,256]{2,1,0:T(8,128)(2,1)S(1)} collective-permute-done((bf16[1,136,256]{2,1,0:T(8,128)(2,1)S(1)}, bf16[1,136,256]{2,1,0:T(8,128)(2,1)S(1)}, u32[]{:S(2)}, u32[]{:S(2)}) %collective-permute-start.6) | collective-permute-done | bytes 69664 | tf_op jit(solution)/shard_map/ppermute | solution.py:26
  22.5 0.1 collective-permute-start.8
  22.6 0.4 collective-permute-start.9
  23.0 3.1 %collective-permute-start.10 = (bf16[3,136,256]{2,1,0:T(8,128)(2,1)S(1)}, bf16[3,136,256]{2,1,0:T(8,128)(2,1)S(1)}, u32[]{:S(2)}, u32[]{:S(2)}) collective-permute-start(bf16[3,136,256]{2,1,0:T(8,128)(2,1)S(1)} %constant_dynamic-update-slice_fusion.refs_4_), channel_id=1, source_target_pairs={{0,6},{1,7},{2,4},{3,5},{4,2},{5,3},{6,0},{7,1},{8,14},{9,15},{10,... | collective-permute-start | bytes 626696 | tf_op jit(solution)/shard_map/ppermute | solution.py:26
  26.1 1.5 %collective-permute-start.4 = (bf16[1,136,256]{2,1,0:T(8,128)(2,1)S(1)}, bf16[1,136,256]{2,1,0:T(8,128)(2,1)S(1)}, u32[]{:S(2)}, u32[]{:S(2)}) collective-permute-start(bf16[1,136,256]{2,1,0:T(8,128)(2,1)S(1)} %shard_map.104.refs_0_), channel_id=1, source_target_pairs={{0,6},{1,7},{2,4},{3,5},{4,2},{5,3},{6,0},{7,1},{8,14},{9,15},{10,... | collective-permute-start | bytes 208904 | tf_op jit(solution)/shard_map/ppermute | solution.py:26
  27.6 0.8 %copy.12.dest_ref = s32[16,2]{1,0:T(8,128)S(1)} copy(s32[16,2]{0,1:T(2,128)} %bitcast.10) | data formatting | bytes 256 | tf_op jit(solution)/shard_map/squeeze | solution.py:314
  28.4 1.7 %copy-done = bf16[2,10,256,256]{3,2,1,0:T(8,128)(2,1)S(1)} copy-done((bf16[2,10,256,256]{3,2,1,0:T(8,128)(2,1)S(1)}, bf16[2,10,256,256]{3,2,1,0:T(8,128)(2,1)}, u32[]{:S(2)}) %copy-start) | copy-done | bytes 2621464
  30.1 0.9 %copy-done.2 = bf16[512,256]{1,0:T(8,128)(2,1)S(1)} copy-done((bf16[512,256]{1,0:T(8,128)(2,1)S(1)}, bf16[512,256]{1,0:T(8,128)(2,1)}, u32[]{:S(2)}) %copy-start.2) | copy-done | bytes 262168
  31.0 0.7 %copy-done.6 = s32[2,10]{1,0:T(2,128)S(1)} copy-done((s32[2,10]{1,0:T(2,128)S(1)}, s32[2,10]{1,0:T(2,128)}, u32[]{:S(2)}) %copy-start.6) | copy-done | bytes 104
  31.7 1.7 %shard_map.103.near_ref = f32[512,256]{1,0:T(8,128)S(1)} custom-call(s32[2,10]{1,0:T(2,128)S(1)} %copy-done.6, bf16[2,10,256,256]{3,2,1,0:T(8,128)(2,1)S(1)} %copy-done, bf16[512,256]{1,0:T(8,128)(2,1)S(1)} %copy-done.2, bf16[512,256]{1,0:T(8,128)(2,1)S(1)} %collective-permute-done.swap_ref, bf16[512,256]{1,0:T(8,128)(2,1)S(1)} %collective-permute-done.1.cross_ref), custom_call_target="tpu_custom_call" | custom-call | flops 671088640 | bytes 3932160 | tf_op jit(solution)/shard_map/pallas_call | solution.py:284
  33.4 1.6 %collective-permute-done.3.refs_2_ = bf16[1,136,256]{2,1,0:T(8,128)(2,1)S(1)} collective-permute-done((bf16[1,136,256]{2,1,0:T(8,128)(2,1)S(1)}, bf16[1,136,256]{2,1,0:T(8,128)(2,1)S(1)}, u32[]{:S(2)}, u32[]{:S(2)}) %collective-permute-start.3) | collective-permute-done | bytes 69664 | tf_op jit(solution)/shard_map/ppermute | solution.py:26
  35.0 2.3 %shard_map.105 = (bf16[512,256]{1,0:T(8,128)(2,1)}, f32[320,128]{1,0:T(8,128)S(1)}) custom-call(s32[16,2]{1,0:T(8,128)S(1)} %copy.12.dest_ref, bf16[16,64,128]{2,1,0:T(8,128)(2,1)S(1)} %bitcast.8, bf16[2,64,256]{2,1,0:T(8,128)(2,1)S(1)} %copy-done.5, f32[512,256]{1,0:T(8,128)S(1)} %shard_map.103.near_ref, bf16[1,136,256]{2,1,0:T(8,128)(2,1)S(1)} %shard_map.104.refs_0_, ...), custom_call_target="tpu_custom_call" | custom-call | tf_op jit(solution)/shard_map/pallas_call | solution.py:305
  37.3 1.4 %collective-permute-done.11 = f32[320,128]{1,0:T(8,128)S(1)} collective-permute-done((f32[320,128]{1,0:T(8,128)S(1)}, f32[320,128]{1,0:T(8,128)S(1)}, u32[]{:S(2)}, u32[]{:S(2)}) %collective-permute-start.11) | collective-permute-done | bytes 163872 | tf_op jit(solution)/shard_map/ppermute | solution.py:30
  38.8 0.6 %collective-permute-start.13 = (bf16[320,128]{1,0:T(8,128)(2,1)S(1)}, bf16[320,128]{1,0:T(8,128)(2,1)S(1)}, u32[]{:S(2)}, u32[]{:S(2)}) collective-permute-start(bf16[320,128]{1,0:T(8,128)(2,1)S(1)} %get-tuple-element.11), channel_id=1, source_target_pairs={{0,4},{1,13},{2,6},{3,15},{4,0},{5,9},{6,2},{7,11},{8,12},{9,5},{1... | collective-permute-start | bytes 245768 | tf_op jit(solution)/shard_map/ppermute | solution.py:26
  39.4 1.1 %collective-permute-start.12 = (bf16[320,128]{1,0:T(8,128)(2,1)S(1)}, bf16[320,128]{1,0:T(8,128)(2,1)S(1)}, u32[]{:S(2)}, u32[]{:S(2)}) collective-permute-start(bf16[320,128]{1,0:T(8,128)(2,1)S(1)} %get-tuple-element.11), channel_id=1, source_target_pairs={{0,2},{1,9},{2,0},{3,11},{4,6},{5,13},{6,4},{7,15},{8,10},{9,1},{1... | collective-permute-start | bytes 245768 | tf_op jit(solution)/shard_map/ppermute | solution.py:26
  40.5 1.8 %collective-permute-start.14 = (bf16[320,128]{1,0:T(8,128)(2,1)S(1)}, bf16[320,128]{1,0:T(8,128)(2,1)S(1)}, u32[]{:S(2)}, u32[]{:S(2)}) collective-permute-start(bf16[320,128]{1,0:T(8,128)(2,1)S(1)} %get-tuple-element.11), channel_id=1, source_target_pairs={{0,6},{1,11},{2,4},{3,9},{4,2},{5,15},{6,0},{7,13},{8,14},{9,3},{1... | collective-permute-start | bytes 245768 | tf_op jit(solution)/shard_map/ppermute | solution.py:26
  42.3 0.7 %collective-permute-start.15 = (bf16[320,128]{1,0:T(8,128)(2,1)S(1)}, bf16[320,128]{1,0:T(8,128)(2,1)S(1)}, u32[]{:S(2)}, u32[]{:S(2)}) collective-permute-start(bf16[320,128]{1,0:T(8,128)(2,1)S(1)} %get-tuple-element.11), channel_id=1, source_target_pairs={{1,15},{3,13},{5,11},{7,9},{9,7},{11,5},{13,3},{15,1},{17,31},{19,... | collective-permute-start | bytes 245768 | tf_op jit(solution)/shard_map/ppermute | solution.py:26
  43.0 1.2 %collective-permute-done.13 = bf16[320,128]{1,0:T(8,128)(2,1)S(1)} collective-permute-done((bf16[320,128]{1,0:T(8,128)(2,1)S(1)}, bf16[320,128]{1,0:T(8,128)(2,1)S(1)}, u32[]{:S(2)}, u32[]{:S(2)}) %collective-permute-start.13) | collective-permute-done | bytes 81952 | tf_op jit(solution)/shard_map/ppermute | solution.py:26
  44.2 1.7 %collective-permute-done.14 = bf16[320,128]{1,0:T(8,128)(2,1)S(1)} collective-permute-done((bf16[320,128]{1,0:T(8,128)(2,1)S(1)}, bf16[320,128]{1,0:T(8,128)(2,1)S(1)}, u32[]{:S(2)}, u32[]{:S(2)}) %collective-permute-start.14) | collective-permute-done | bytes 81952 | tf_op jit(solution)/shard_map/ppermute | solution.py:26
  45.9 0.1 fusion.3
  46.0 4.4 %collective-permute-start.16 = (f32[2,320,128]{2,1,0:T(8,128)S(1)}, f32[2,320,128]{2,1,0:T(8,128)S(1)}, u32[]{:S(2)}, u32[]{:S(2)}) collective-permute-start(f32[2,320,128]{2,1,0:T(8,128)S(1)} %pad_maximum_fusion.mine_ref), channel_id=1, source_target_pairs={{0,1},{1,0},{2,3},{3,2},{4,5},{5,4},{6,7},{7,6},{8,9},{9,8},{10,11... | collective-permute-start | bytes 983048 | tf_op jit(solution)/shard_map/ppermute | solution.py:30
  50.3 1.3 %collective-permute-done.16.other_ref = f32[2,320,128]{2,1,0:T(8,128)S(1)} collective-permute-done((f32[2,320,128]{2,1,0:T(8,128)S(1)}, f32[2,320,128]{2,1,0:T(8,128)S(1)}, u32[]{:S(2)}, u32[]{:S(2)}) %collective-permute-start.16) | collective-permute-done | bytes 327712 | tf_op jit(solution)/shard_map/ppermute | solution.py:30
  51.6 11.6 %shard_map.106 = (f32[256,256]{1,0:T(8,128)}, bf16[3,256,256]{2,1,0:T(8,128)(2,1)}) custom-call(f32[320,128]{1,0:T(8,128)S(1)} %get-tuple-element.12.seg_ref, f32[2,320,128]{2,1,0:T(8,128)S(1)} %pad_maximum_fusion.mine_ref, f32[2,320,128]{2,1,0:T(8,128)S(1)} %collective-permute-done.16.other_ref), custom_call_target="tpu_custom_call" | custom-call | tf_op jit(solution)/shard_map/pallas_call | solution.py:237
  (28 shorter events, 0.1 us)
Async XLA Ops:
  1.4 0.9 %copy-start.1 = (bf16[512,256]{1,0:T(8,128)(2,1)S(1)}, bf16[512,256]{1,0:T(8,128)(2,1)}, u32[]{:S(2)}) copy-start(bf16[512,256]{1,0:T(8,128)(2,1)} %cols_ref.1) | copy-start | bytes 786436
  2.3 0.8 %copy-start.4 = (bf16[2,64,256]{2,1,0:T(8,128)(2,1)S(1)}, bf16[2,64,256]{2,1,0:T(8,128)(2,1)}, u32[]{:S(2)}) copy-start(bf16[2,64,256]{2,1,0:T(8,128)(2,1)} %basis_ref.2) | copy-start | bytes 196612
  3.2 31.8 %copy-start.3 = (bf16[1,1,16,64,128]{4,3,2,1,0:T(8,128)(2,1)S(1)}, bf16[1,1,16,64,128]{4,3,2,1,0:T(8,128)(2,1)}, u32[]{:S(2)}) copy-start(bf16[1,1,16,64,128]{4,3,2,1,0:T(8,128)(2,1)} %param.13) | copy-start | bytes 786436
  3.2 31.9 %copy-start.5 = (bf16[2,64,256]{2,1,0:T(8,128)(2,1)S(1)}, bf16[2,64,256]{2,1,0:T(8,128)(2,1)}, u32[]{:S(2)}) copy-start(bf16[2,64,256]{2,1,0:T(8,128)(2,1)} %basis_ref.3) | copy-start | bytes 196612
  4.0 9.8 %collective-permute-start.5 = (bf16[1,136,256]{2,1,0:T(8,128)(2,1)S(1)}, bf16[1,136,256]{2,1,0:T(8,128)(2,1)S(1)}, u32[]{:S(2)}, u32[]{:S(2)}) collective-permute-start(bf16[1,136,256]{2,1,0:T(8,128)(2,1)S(1)} %shard_map.104.refs_0_), channel_id=1, source_target_pairs={{0,8},{1,9},{2,10},{3,11},{4,12},{5,13},{6,14},{7,15},{8,0},{9,1},... | collective-permute-start | bytes 208904 | tf_op jit(solution)/shard_map/ppermute | solution.py:26
  7.1 18.9 %collective-permute-start = (bf16[512,256]{1,0:T(8,128)(2,1)S(1)}, bf16[512,256]{1,0:T(8,128)(2,1)S(1)}, u32[]{:S(2)}, u32[]{:S(2)}) collective-permute-start(bf16[512,256]{1,0:T(8,128)(2,1)S(1)} %copy-done.1), channel_id=1, source_target_pairs={{0,1},{1,0},{2,3},{3,2},{4,5},{5,4},{6,7},{7,6},{8,9},{9,8},{10,11... | collective-permute-start | bytes 786440 | tf_op jit(solution)/shard_map/ppermute | solution.py:264
  7.1 19.0 %collective-permute-start.1 = (bf16[512,256]{1,0:T(8,128)(2,1)S(1)}, bf16[512,256]{1,0:T(8,128)(2,1)S(1)}, u32[]{:S(2)}, u32[]{:S(2)}) collective-permute-start(bf16[512,256]{1,0:T(8,128)(2,1)S(1)} %copy-done.1), channel_id=1, source_target_pairs={{1,2},{3,4},{5,6},{7,8},{9,10},{11,12},{13,14},{15,16},{17,18},{19... | collective-permute-start | bytes 786440 | tf_op jit(solution)/shard_map/ppermute | solution.py:266
  7.8 15.2 %collective-permute-start.2 = (bf16[1,136,256]{2,1,0:T(8,128)(2,1)S(1)}, bf16[1,136,256]{2,1,0:T(8,128)(2,1)S(1)}, u32[]{:S(2)}, u32[]{:S(2)}) collective-permute-start(bf16[1,136,256]{2,1,0:T(8,128)(2,1)S(1)} %shard_map.104.refs_0_), channel_id=1, source_target_pairs={{0,2},{1,3},{2,0},{3,1},{4,6},{5,7},{6,4},{7,5},{8,10},{9,11},{10,... | collective-permute-start | bytes 208904 | tf_op jit(solution)/shard_map/ppermute | solution.py:26
  11.2 11.2 %collective-permute-start.6 = (bf16[1,136,256]{2,1,0:T(8,128)(2,1)S(1)}, bf16[1,136,256]{2,1,0:T(8,128)(2,1)S(1)}, u32[]{:S(2)}, u32[]{:S(2)}) collective-permute-start(bf16[1,136,256]{2,1,0:T(8,128)(2,1)S(1)} %shard_map.104.refs_0_), channel_id=1, source_target_pairs={{0,16},{1,17},{2,18},{3,19},{4,20},{5,21},{6,22},{7,23},{8,24},{9,... | collective-permute-start | bytes 208904 | tf_op jit(solution)/shard_map/ppermute | solution.py:26
  13.8 8.7 %collective-permute-start.7 = (bf16[1,136,256]{2,1,0:T(8,128)(2,1)S(1)}, bf16[1,136,256]{2,1,0:T(8,128)(2,1)S(1)}, u32[]{:S(2)}, u32[]{:S(2)}) collective-permute-start(bf16[1,136,256]{2,1,0:T(8,128)(2,1)S(1)} %shard_map.104.refs_0_), channel_id=1, source_target_pairs={{0,24},{1,25},{2,26},{3,27},{4,28},{5,29},{6,30},{7,31},{8,16},{9,... | collective-permute-start | bytes 208904 | tf_op jit(solution)/shard_map/ppermute | solution.py:26
  22.5 12.5 %collective-permute-start.8 = (bf16[3,136,256]{2,1,0:T(8,128)(2,1)S(1)}, bf16[3,136,256]{2,1,0:T(8,128)(2,1)S(1)}, u32[]{:S(2)}, u32[]{:S(2)}) collective-permute-start(bf16[3,136,256]{2,1,0:T(8,128)(2,1)S(1)} %constant_dynamic-update-slice_fusion.refs_4_), channel_id=1, source_target_pairs={{0,2},{1,3},{2,0},{3,1},{4,6},{5,7},{6,4},{7,5},{8,10},{9,11},{10,... | collective-permute-start | bytes 626696 | tf_op jit(solution)/shard_map/ppermute | solution.py:26
  22.6 12.4 %collective-permute-start.9 = (bf16[3,136,256]{2,1,0:T(8,128)(2,1)S(1)}, bf16[3,136,256]{2,1,0:T(8,128)(2,1)S(1)}, u32[]{:S(2)}, u32[]{:S(2)}) collective-permute-start(bf16[3,136,256]{2,1,0:T(8,128)(2,1)S(1)} %constant_dynamic-update-slice_fusion.refs_4_), channel_id=1, source_target_pairs={{0,4},{1,5},{2,6},{3,7},{4,0},{5,1},{6,2},{7,3},{8,12},{9,13},{10,... | collective-permute-start | bytes 626696 | tf_op jit(solution)/shard_map/ppermute | solution.py:26
  23.0 12.0 %collective-permute-start.10 = (bf16[3,136,256]{2,1,0:T(8,128)(2,1)S(1)}, bf16[3,136,256]{2,1,0:T(8,128)(2,1)S(1)}, u32[]{:S(2)}, u32[]{:S(2)}) collective-permute-start(bf16[3,136,256]{2,1,0:T(8,128)(2,1)S(1)} %constant_dynamic-update-slice_fusion.refs_4_), channel_id=1, source_target_pairs={{0,6},{1,7},{2,4},{3,5},{4,2},{5,3},{6,0},{7,1},{8,14},{9,15},{10,... | collective-permute-start | bytes 626696 | tf_op jit(solution)/shard_map/ppermute | solution.py:26
  26.1 8.9 %collective-permute-start.3 = (bf16[1,136,256]{2,1,0:T(8,128)(2,1)S(1)}, bf16[1,136,256]{2,1,0:T(8,128)(2,1)S(1)}, u32[]{:S(2)}, u32[]{:S(2)}) collective-permute-start(bf16[1,136,256]{2,1,0:T(8,128)(2,1)S(1)} %shard_map.104.refs_0_), channel_id=1, source_target_pairs={{0,4},{1,5},{2,6},{3,7},{4,0},{5,1},{6,2},{7,3},{8,12},{9,13},{10,... | collective-permute-start | bytes 208904 | tf_op jit(solution)/shard_map/ppermute | solution.py:26
  26.1 8.9 %collective-permute-start.4 = (bf16[1,136,256]{2,1,0:T(8,128)(2,1)S(1)}, bf16[1,136,256]{2,1,0:T(8,128)(2,1)S(1)}, u32[]{:S(2)}, u32[]{:S(2)}) collective-permute-start(bf16[1,136,256]{2,1,0:T(8,128)(2,1)S(1)} %shard_map.104.refs_0_), channel_id=1, source_target_pairs={{0,6},{1,7},{2,4},{3,5},{4,2},{5,3},{6,0},{7,1},{8,14},{9,15},{10,... | collective-permute-start | bytes 208904 | tf_op jit(solution)/shard_map/ppermute | solution.py:26
  28.4 1.7 %copy-start = (bf16[2,10,256,256]{3,2,1,0:T(8,128)(2,1)S(1)}, bf16[2,10,256,256]{3,2,1,0:T(8,128)(2,1)}, u32[]{:S(2)}) copy-start(bf16[2,10,256,256]{3,2,1,0:T(8,128)(2,1)} %blocks_ref.1) | copy-start | bytes 7864324
  30.1 0.9 %copy-start.2 = (bf16[512,256]{1,0:T(8,128)(2,1)S(1)}, bf16[512,256]{1,0:T(8,128)(2,1)}, u32[]{:S(2)}) copy-start(bf16[512,256]{1,0:T(8,128)(2,1)} %cols_ref.1) | copy-start | bytes 786436
  31.0 0.7 %copy-start.6 = (s32[2,10]{1,0:T(2,128)S(1)}, s32[2,10]{1,0:T(2,128)}, u32[]{:S(2)}) copy-start(s32[2,10]{1,0:T(2,128)} %list_ref.1) | copy-start | bytes 244
  37.3 1.4 %collective-permute-start.11 = (f32[320,128]{1,0:T(8,128)S(1)}, f32[320,128]{1,0:T(8,128)S(1)}, u32[]{:S(2)}, u32[]{:S(2)}) collective-permute-start(f32[320,128]{1,0:T(8,128)S(1)} %get-tuple-element.8), channel_id=1, source_target_pairs={{0,1},{1,0},{2,3},{3,2},{4,5},{5,4},{6,7},{7,6},{8,9},{9,8},{10,11... | collective-permute-start | bytes 491528 | tf_op jit(solution)/shard_map/ppermute | solution.py:30
  38.8 5.4 %collective-permute-start.13 = (bf16[320,128]{1,0:T(8,128)(2,1)S(1)}, bf16[320,128]{1,0:T(8,128)(2,1)S(1)}, u32[]{:S(2)}, u32[]{:S(2)}) collective-permute-start(bf16[320,128]{1,0:T(8,128)(2,1)S(1)} %get-tuple-element.11), channel_id=1, source_target_pairs={{0,4},{1,13},{2,6},{3,15},{4,0},{5,9},{6,2},{7,11},{8,12},{9,5},{1... | collective-permute-start | bytes 245768 | tf_op jit(solution)/shard_map/ppermute | solution.py:26
  39.4 4.7 %collective-permute-start.12 = (bf16[320,128]{1,0:T(8,128)(2,1)S(1)}, bf16[320,128]{1,0:T(8,128)(2,1)S(1)}, u32[]{:S(2)}, u32[]{:S(2)}) collective-permute-start(bf16[320,128]{1,0:T(8,128)(2,1)S(1)} %get-tuple-element.11), channel_id=1, source_target_pairs={{0,2},{1,9},{2,0},{3,11},{4,6},{5,13},{6,4},{7,15},{8,10},{9,1},{1... | collective-permute-start | bytes 245768 | tf_op jit(solution)/shard_map/ppermute | solution.py:26
  40.5 5.4 %collective-permute-start.14 = (bf16[320,128]{1,0:T(8,128)(2,1)S(1)}, bf16[320,128]{1,0:T(8,128)(2,1)S(1)}, u32[]{:S(2)}, u32[]{:S(2)}) collective-permute-start(bf16[320,128]{1,0:T(8,128)(2,1)S(1)} %get-tuple-element.11), channel_id=1, source_target_pairs={{0,6},{1,11},{2,4},{3,9},{4,2},{5,15},{6,0},{7,13},{8,14},{9,3},{1... | collective-permute-start | bytes 245768 | tf_op jit(solution)/shard_map/ppermute | solution.py:26
  42.3 3.5 %collective-permute-start.15 = (bf16[320,128]{1,0:T(8,128)(2,1)S(1)}, bf16[320,128]{1,0:T(8,128)(2,1)S(1)}, u32[]{:S(2)}, u32[]{:S(2)}) collective-permute-start(bf16[320,128]{1,0:T(8,128)(2,1)S(1)} %get-tuple-element.11), channel_id=1, source_target_pairs={{1,15},{3,13},{5,11},{7,9},{9,7},{11,5},{13,3},{15,1},{17,31},{19,... | collective-permute-start | bytes 245768 | tf_op jit(solution)/shard_map/ppermute | solution.py:26
  46.0 5.6 %collective-permute-start.16 = (f32[2,320,128]{2,1,0:T(8,128)S(1)}, f32[2,320,128]{2,1,0:T(8,128)S(1)}, u32[]{:S(2)}, u32[]{:S(2)}) collective-permute-start(f32[2,320,128]{2,1,0:T(8,128)S(1)} %pad_maximum_fusion.mine_ref), channel_id=1, source_target_pairs={{0,1},{1,0},{2,3},{3,2},{4,5},{5,4},{6,7},{7,6},{8,9},{9,8},{10,11... | collective-permute-start | bytes 983048 | tf_op jit(solution)/shard_map/ppermute | solution.py:30

commit v3 on v2

--- a/solution.py
+++ b/solution.py
@@ -1,3 +1,5 @@
+import functools
+
 import jax
 import jax.numpy as jnp
 from jax import lax
@@ -6,13 +8,15 @@
 from jax.sharding import PartitionSpec as P
 
 LEVELS = 3
+PLANE = 4
+FIRST_KIB = 61440
 AXES = ("seg", "sub")
 VMEM = pl.BlockSpec(memory_space=pltpu.VMEM)
 SMEM = pl.BlockSpec(memory_space=pltpu.SMEM)
 
 
-def params(**more):
-    return pltpu.CompilerParams(vmem_limit_bytes=48 * 2**20, **more)
+def params(kib=48 * 2**10):
+    return pltpu.CompilerParams(vmem_limit_bytes=kib * 2**10)
 
 
 def hop(value, even, odd):
@@ -54,20 +58,77 @@
     return lax.dot_general(a, b, (((0,), (0,)), ((), ())), preferred_element_type=jnp.float32)
 
 
-def project_kernel(basis_ref, cols_ref, source_ref, out_ref):
-    leaves, rank, rows = basis_ref.shape
-    lane = lax.broadcasted_iota(jnp.int32, (8, 256), 1)
-    flags = jnp.zeros((8, 256), jnp.float32)
-    for s in range(source_ref.shape[0]):
-        for c in range(source_ref.shape[1]):
-            flags = jnp.where(
-                lane == s * source_ref.shape[1] + c, source_ref[s, c].astype(jnp.float32), flags
-            )
+def first_kernel(basis_hbm, cols_hbm, couplings_hbm, row_hbm, source_ref, dest_ref, *rest):
+    mine_ref, row_ref, *pay_refs, basis, cols, couplings, flags, sems = rest
+    copies = [
+        pltpu.make_async_copy(src, dst, sems.at[i])
+        for i, (src, dst) in enumerate(
+            ((basis_hbm, basis), (cols_hbm, cols), (couplings_hbm.at[0, 0], couplings), (row_hbm, row_ref))
+        )
+    ]
+    for copy in copies:
+        copy.start()
+    slots, peers = source_ref.shape
+    leaves, rank, rows = basis.shape
+    for i, ref in enumerate((source_ref, dest_ref)):
+        flags[i] = jnp.zeros(flags.shape[1:], jnp.float32)
+        flags[i, 0:slots, 0:peers] = ref[...].astype(jnp.float32)
+    copies[0].wait()
+    copies[1].wait()
     for l in range(leaves):
-        out_ref[0, l * rank : (l + 1) * rank, :] = dot(
-            basis_ref[l], cols_ref[l * rows : (l + 1) * rows, :]
+        mine_ref[0, l * rank : (l + 1) * rank, :] = dot(
+            basis[l], cols[l * rows : (l + 1) * rows, :]
         ).astype(jnp.bfloat16)
-    out_ref[0, leaves * rank : leaves * rank + 8, :] = flags.astype(jnp.bfloat16)
+    mine_ref[0, leaves * rank : leaves * rank + 8, :] = flags[0].astype(jnp.bfloat16)
+    copies[2].wait()
+    copies[3].wait()
+    me = lax.axis_index("seg")
+    high = peers // PLANE
+    for m, pay in enumerate(pay_refs):
+        for z in range(high):
+            pay[0, z * rank : (z + 1) * rank, :] = couplings[z * PLANE + (me ^ m) % PLANE]
+        pay[0, high * rank : high * rank + 8, :] = flags[1, :, 0:128].astype(jnp.bfloat16)
+
+
+def partial_kernel(leaves, slots, *refs):
+    high = len(refs) - 2 * PLANE
+    blocks, couplings, outs = refs[:high], refs[high : high + PLANE], refs[high + PLANE :]
+    rank = (blocks[0].shape[1] - 8) // leaves
+    me = lax.axis_index("seg")
+    lane8 = lax.broadcasted_iota(jnp.int32, (8, 128), 1)
+    lane = lax.broadcasted_iota(jnp.int32, (1, slots * rank), 1)
+
+    def pick(flags, index):
+        return jnp.sum(jnp.where(lane8 == index, flags, 0.0), axis=1, keepdims=True)
+
+    sources = [ref[0, leaves * rank : leaves * rank + 8, 0:128].astype(jnp.float32) for ref in blocks]
+    for m in range(PLANE):
+        target = me ^ m
+        dests = couplings[m][0, high * rank : high * rank + 8, :].astype(jnp.float32)
+        total = jnp.zeros((leaves * rank, 256), jnp.float32)
+        for k in range(high):
+            source = pick(sources[k], target)
+            dest = pick(dests, me ^ (PLANE * k))
+            chosen = []
+            for c in range(slots):
+                flag = jnp.broadcast_to(source[c : c + 1, :], (1, 256))
+                chosen.append(
+                    sum(
+                        blocks[k][0, y * rank : (y + 1) * rank, :]
+                        * jnp.where(flag == y, 1.0, 0.0).astype(jnp.bfloat16)
+                        for y in range(leaves)
+                    )
+                )
+            at = pl.multiple_of(((me // PLANE) ^ k) * rank, rank)
+            matrix = couplings[m][0, pl.ds(at, rank), :]
+            wide = jnp.broadcast_to(dest[0:1, :], lane.shape)
+            for c in range(1, slots):
+                wide = jnp.where(lane >= c * rank, dest[c : c + 1, :], wide)
+            routed = [
+                matrix * jnp.where(wide == l, 1.0, 0.0).astype(jnp.bfloat16) for l in range(leaves)
+            ]
+            total = total + dot(jnp.concatenate(routed, 0), jnp.concatenate(chosen, 0))
+        outs[m][0] = total.astype(outs[m].dtype)
 
 
 def near_kernel(list_ref, blocks_ref, own_ref, swap_ref, cross_ref, out_ref, held):
@@ -99,42 +160,12 @@
     out_ref[...] = acc
 
 
-def combine_kernel(dest_ref, couplings_ref, basis_ref, near_ref, *refs):
-    b_ref, q1, q2, q3, z_ref, r1, r2, r3, samples_ref, gram_ref = refs
-    me = lax.axis_index("seg")
+def combine_kernel(basis_ref, near_ref, own_ref, *refs):
+    *got, samples_ref, gram_ref = refs
     leaves, rank, rows = basis_ref.shape
-    slots = dest_ref.shape[1]
-    blocks = [(b_ref, 0, 0), (q1, 0, 1), (q2, 0, 2), (q3, 0, 3)]
-    for mask, ref in ((0, z_ref), (1, r1), (2, r2), (3, r3)):
-        blocks += [(ref, k, mask ^ (4 * k + 4)) for k in range(ref.shape[0])]
-    lane8 = lax.broadcasted_iota(jnp.int32, (8, 256), 1)
-    lane = lax.broadcasted_iota(jnp.int32, (1, slots * rank), 1)
-    total = jnp.zeros((leaves * rank, 256), jnp.float32)
-    for ref, k, mask in blocks:
-        source = me ^ mask
-        flags = ref[k, leaves * rank : leaves * rank + 8, :].astype(jnp.float32)
-        projected = [ref[k, y * rank : (y + 1) * rank, :] for y in range(leaves)]
-        chosen = []
-        for c in range(slots):
-            flag = jnp.sum(
-                jnp.where(lane8 == me * slots + c, flags, 0.0), axis=1, keepdims=True
-            )[0:1, :]
-            flag = jnp.broadcast_to(flag, (1, 256))
-            chosen.append(
-                sum(
-                    projected[y] * jnp.where(flag == y, 1.0, 0.0).astype(jnp.bfloat16)
-                    for y in range(leaves)
-                )
-            )
-        matrix = couplings_ref[source]
-        routed = []
-        for l in range(leaves):
-            weight = jnp.zeros((1, slots * rank), jnp.float32)
-            for c in range(slots):
-                hit = jnp.where(dest_ref[source, c] == l, 1.0, 0.0)
-                weight = jnp.where((lane >= c * rank) & (lane < (c + 1) * rank), hit, weight)
-            routed.append(matrix * weight.astype(jnp.bfloat16))
-        total = total + dot(jnp.concatenate(routed, 0), jnp.concatenate(chosen, 0))
+    total = own_ref[0]
+    for ref in got:
+        total = total + ref[0].astype(jnp.float32)
     coeff = total.astype(jnp.bfloat16)
     for l in range(leaves):
         far = dot_t(basis_ref[l], coeff[l * rank : (l + 1) * rank, :])
@@ -150,11 +181,14 @@
 def split(a):
     h=a.astype(jnp.bfloat16); return h,(a-h.astype(jnp.float32)).astype(jnp.bfloat16)
 def dg(a,b,dims): return lax.dot_general(a,b,(dims,((),())),preferred_element_type=jnp.float32)
-def mm3(a,b,dims):
+def lstack(a):
+    h,l=split(a); return jnp.concatenate([h,l,h],1)
+def rstack(b):
+    h,l=split(b); return jnp.concatenate([h,h,l],0)
+def mms(a,b): return dg(a,b,((1,),(0,)))
+def mmt(a,b):
     ah,al=split(a); bh,bl=split(b)
-    return dg(ah,bh,dims)+dg(ah,bl,dims)+dg(al,bh,dims)
-def mm(a,b): return mm3(a,b,((1,),(0,)))
-def mmt(a,b): return mm3(a,b,((1,),(1,)))
+    return dg(jnp.concatenate([ah,al,ah],1),jnp.concatenate([bh,bh,bl],1),((1,),(1,)))
 def eliminate(P, lane, row):
     base=lane & ~31
     sub=lane & 31
@@ -213,14 +247,14 @@
         Wbd=jnp.where(bd,jnp.concatenate([Vf]*4,0),0.0)
         x=X[kb]
         x=jnp.where((l256>=off)&(l256<off+32),jnp.where(l256-off==r256,1.0,0.0),x)
-        panel=mm(Wbd,x)
+        panel=mms(lstack(Wbd),rstack(x)); ps=rstack(panel)
         chunks={}
         for i in range(kb+1,8):
             c=i//4
             if c not in chunks: chunks[c]=jnp.transpose(panel[:,c*128:c*128+128])
             T=chunks[c][(i%4)*32:(i%4)*32+32,:]
             L=jnp.where(bd,jnp.concatenate([T]*4,0),0.0)
-            X[i]=jnp.where((l256>=off)&(l256<off+32),0.0,X[i])-mm(L,panel)
+            X[i]=jnp.where((l256>=off)&(l256<off+32),0.0,X[i])-mms(lstack(L),ps)
         for t in range(4):
             pt=panel[32*t:32*t+32,:]
             sh=(lo-32*t)%128
@@ -265,22 +299,39 @@
     ahead = [(i, i + 1) for i in range(1, n - 1, 2)]
     cross = lax.ppermute(sample_cols, AXES, ahead + [(j, i) for i, j in ahead])
 
-    mine = pl.pallas_call(
-        project_kernel,
-        out_shape=jax.ShapeDtypeStruct((1, leaf_count * rank + 8, width), jnp.bfloat16),
-        in_specs=[VMEM, VMEM, SMEM],
-        out_specs=VMEM,
-        compiler_params=params(),
-        cost_estimate=pl.CostEstimate(
-            flops=2 * rows * rank * width, bytes_accessed=512 * 2**10, transcendentals=0
-        ),
-    )(col_basis_t, sample_cols, far_source[0, 0])
-
-    high = [hop(mine, m, m) for m in range(4, n_seg, 4)]
-    low = [hop(mine, m, m) for m in (1, 2, 3)]
-    column = jnp.concatenate(high, 0)
-    rest = [hop(column, m, m) for m in (1, 2, 3)]
-
+    slots = far_source.shape[3]
+    basis_first, swap = lax.optimization_barrier((col_basis_t, swap))
+    high = n_seg // PLANE
+    hbm = pl.BlockSpec(memory_space=pltpu.HBM)
+    bf16 = jnp.bfloat16
+    mine, row_basis, *pays = pl.pallas_call(
+        first_kernel,
+        out_shape=[
+            jax.ShapeDtypeStruct((1, leaf_count * rank + 8, width), bf16),
+            jax.ShapeDtypeStruct(row_basis_t.shape, bf16),
+        ]
+        + [jax.ShapeDtypeStruct((1, high * rank + 8, slots * rank), bf16)] * PLANE,
+        in_specs=[hbm] * 4 + [VMEM] * 2,
+        out_specs=[VMEM] * (2 + PLANE),
+        scratch_shapes=[
+            pltpu.VMEM(col_basis_t.shape, bf16),
+            pltpu.VMEM(sample_cols.shape, bf16),
+            pltpu.VMEM(couplings.shape[2:], bf16),
+            pltpu.VMEM((2, 8, 256), jnp.float32),
+            pltpu.SemaphoreType.DMA((4,)),
+        ],
+        compiler_params=params(FIRST_KIB),
+    )(
+        basis_first,
+        sample_cols,
+        couplings,
+        row_basis_t,
+        jnp.swapaxes(far_source[0, 0], 0, 1),
+        jnp.swapaxes(far_dest[0, 0], 0, 1),
+    )
+
+    column = [hop(mine, PLANE * k, PLANE * k) for k in range(1, high)]
+    gathered = [hop(pays[m], m, m) for m in range(1, PLANE)]
     near_part = pl.pallas_call(
         near_kernel,
         grid=(leaf_count,),
@@ -301,6 +352,16 @@
             transcendentals=0,
         ),
     )(near_list, near_blocks, sample_cols, swap, cross)
+    column, gathered, near_part = lax.optimization_barrier((column, gathered, near_part))
+    own, *parts = pl.pallas_call(
+        functools.partial(partial_kernel, leaf_count, slots),
+        out_shape=[jax.ShapeDtypeStruct((1, leaf_count * rank, width), jnp.float32)]
+        + [jax.ShapeDtypeStruct((1, leaf_count * rank, width), bf16)] * (PLANE - 1),
+        in_specs=[VMEM] * (PLANE + high),
+        out_specs=[VMEM] * PLANE,
+        compiler_params=params(),
+    )(mine, *column, pays[0], *gathered)
+    got = [hop(parts[m - 1], m, m) for m in range(1, PLANE)]
 
     samples, gram = pl.pallas_call(
         combine_kernel,
@@ -308,10 +369,10 @@
             jax.ShapeDtypeStruct((rows, width), jnp.bfloat16),
             jax.ShapeDtypeStruct((320, 128), jnp.float32),
         ),
-        in_specs=[SMEM] + [VMEM] * 11,
+        in_specs=[VMEM] * (3 + PLANE - 1),
         out_specs=[VMEM] * 2,
         compiler_params=params(),
-    )(far_dest[0, 0], couplings[0, 0], row_basis_t, near_part, mine, *low, column, *rest)
+    )(row_basis, near_part, own, *got)
 
     total, mask = gram, 1
     while mask < n_sub:
@@ -319,13 +380,13 @@
         mask *= 2
     seg_gram = total / (n_sub * rows)
     rounded = seg_gram.astype(jnp.bfloat16)
-    got = [
+    near = [
         hop(rounded, *masks).astype(jnp.float32) for masks in ((1, 4), (2, 6), (3, 5), (None, 7))
     ]
     odd = (lax.axis_index("sub") % 2) == 1
-    pair = seg_gram + got[0]
-    quad = (got[1] + got[2]) + pair
-    far_quad = (got[0] + got[1]) + (got[2] + got[3])
+    pair = seg_gram + near[0]
+    quad = (near[1] + near[2]) + pair
+    far_quad = (near[0] + near[1]) + (near[2] + near[3])
     sent = jnp.stack([jnp.where(odd, far_quad * 0.25, pair * 0.5), quad * 0.25])
     received = sub_hop(sent, 1)
     segment_factor, transfers = factor_all(seg_gram, sent, received)

time: 63.5 us -> 55 us (0.87)
  waiting for transfers between devices: 14 us -> 10.4 us
  local copies, waits for them, and re-layouts: 6.69 us -> 3.38 us
  starting transfers between devices: 25.2 us -> 23.1 us
    ppermute x13, waiting for transfers between devices: 11.4 us -> 7.02 us  [hop(): return lax.ppermute(value, AXES, pairs)]
    pallas_call x1 -> x2, Pallas kernels: 0.83 us -> 3.18 us  [the longest x1 2.63 us: body(): pl.pallas_call(first_kernel, out_shape=[jax.ShapeDtypeStruct((1, leaf_cou...]
    ppermute x2, starting transfers between devices: 4.37 us -> 2.42 us  [sub_hop(): lax.ppermute(value, 'sub', [(i, i ^ mask) for i in range(lax.axis_size('s...]
    unnamed x16 -> x12, local copies, waits for them, and re-layouts: 5.17 us -> 3.38 us
    squeeze x2 -> x0, local copies, waits for them, and re-layouts: 1.51 us -> none  [the longest x1 0.76 us: body(): far_source[0, 0]]
    pallas_call x1, Pallas kernels: 2.3 us -> 0.99 us  [body(): pl.pallas_call(combine_kernel, out_shape=(jax.ShapeDtypeStruct((rows, wid...]
    ppermute x1, waiting for transfers between devices: 0.01 us -> 0.7 us  [body(): swap = lax.ppermute(sample_cols, AXES, [(i, i ^ 1) for i in range(n)])]
    ppermute x13, starting transfers between devices: 20.1 us -> 19.5 us  [hop(): return lax.ppermute(value, AXES, pairs)]
  transfers between devices with their start and end apart: 17 -> 17, of which waited for: 6 -> 8; matrix products, arithmetic and copies ran while one was open for 1% -> 0% of each run, Pallas kernels for 3% -> 8%
where the time goes in v3:
time: 55 us; the launch traced here: 54.7 us
  starting transfers between devices  23.1 us (42%)
  Pallas kernels  17 us (31%)
  waiting for transfers between devices  10.4 us (19%)
  local copies, waits for them, and re-layouts  3.38 us (6%)
  between operations  0.76 us (1%)
    ppermute x13, starting transfers between devices, hop(): return lax.ppermute(value, AXES, pairs)  19.5 us
    pallas_call x1, Pallas kernels, factor_all(): pl.pallas_call(factor_kernel, out_shape=(jax.ShapeDtypeStruct((256, 256),...  11.1 us
    ppermute x13, waiting for transfers between devices, hop(): return lax.ppermute(value, AXES, pairs)  7.02 us
    unnamed x12, local copies, waits for them, and re-layouts  3.38 us
    ppermute x2, waiting for transfers between devices, sub_hop(): lax.ppermute(value, 'sub', [(i, i ^ mask) for i in range(lax.axis_size('s...  2.65 us
    pallas_call x1, Pallas kernels, body(): pl.pallas_call(first_kernel, out_shape=[jax.ShapeDtypeStruct((1, leaf_cou...  2.63 us
    ppermute x2, starting transfers between devices, sub_hop(): lax.ppermute(value, 'sub', [(i, i ^ mask) for i in range(lax.axis_size('s...  2.42 us
    pallas_call x1, Pallas kernels, body(): pl.pallas_call(near_kernel, grid=(leaf_count,), out_shape=jax.ShapeDtypeS...  1.7 us
  transfers between devices with their start and end apart: 17, of which 8 were waited for; matrix products, arithmetic and copies ran while one was open for 0% of the time, Pallas kernels for 8%

profile of v3, /device:TPU:0, one launch (start us, length us, event | category | flops | bytes accessed | tf_op | source)
XLA Modules:
  0.0 54.7 jit_solution(4705116702888324365)
XLA Ops:
  0.6 0.5 collective-permute-start
  1.1 0.7 %collective-permute-start.7 = (bf16[512,256]{1,0:T(8,128)(2,1)}, bf16[512,256]{1,0:T(8,128)(2,1)S(1)}, u32[]{:S(2)}, u32[]{:S(2)}) collective-permute-start(bf16[512,256]{1,0:T(8,128)(2,1)} %own_ref.1), channel_id=1, source_target_pairs={{1,2},{3,4},{5,6},{7,8},{9,10},{11,12},{13,14},{15,16},{17,18},{19... | collective-permute-start | bytes 786440 | tf_op jit(solution)/shard_map/ppermute | solution.py:300
  1.8 0.7 %collective-permute-done.swap_ref = bf16[512,256]{1,0:T(8,128)(2,1)S(1)} collective-permute-done((bf16[512,256]{1,0:T(8,128)(2,1)}, bf16[512,256]{1,0:T(8,128)(2,1)S(1)}, u32[]{:S(2)}, u32[]{:S(2)}) %collective-permute-start) | collective-permute-done | bytes 262176 | tf_op jit(solution)/shard_map/ppermute | solution.py:298
  2.5 2.6 %shard_map.103 = (bf16[1,136,256]{2,1,0:T(8,128)(2,1)}, bf16[2,64,256]{2,1,0:T(8,128)(2,1)}, bf16[1,264,128]{2,1,0:T(8,128)(2,1)}, bf16[1,264,128]{2,1,0:T(8,128...) custom-call(bf16[2,64,256]{2,1,0:T(8,128)(2,1)} %basis_hbm, bf16[512,256]{1,0:T(8,128)(2,1)} %own_ref.1, ...), custom_call_target="tpu_custom_call" | custom-call | tf_op jit(solution)/shard_map/pallas_call | solution.py:307
  5.2 3.1 %collective-permute-start.4 = (bf16[1,264,128]{2,1,0:T(8,128)(2,1)}, bf16[1,264,128]{2,1,0:T(8,128)(2,1)S(1)}, u32[]{:S(2)}, u32[]{:S(2)}) collective-permute-start(bf16[1,264,128]{2,1,0:T(8,128)(2,1)} %get-tuple-element.29), channel_id=1, source_target_pairs={{0,2},{1,3},{2,0},{3,1},{4,6},{5,7},{6,4},{7,5},{8,10},{9,11},{10,... | collective-permute-start | bytes 202760 | tf_op jit(solution)/shard_map/ppermute | solution.py:30
  8.3 4.6 %collective-permute-start.3 = (bf16[1,136,256]{2,1,0:T(8,128)(2,1)}, bf16[1,136,256]{2,1,0:T(8,128)(2,1)S(1)}, u32[]{:S(2)}, u32[]{:S(2)}) collective-permute-start(bf16[1,136,256]{2,1,0:T(8,128)(2,1)} %get-tuple-element.28.refs_0_), channel_id=1, source_target_pairs={{0,24},{1,25},{2,26},{3,27},{4,28},{5,29},{6,30},{7,31},{8,16},{9,... | collective-permute-start | bytes 208904 | tf_op jit(solution)/shard_map/ppermute | solution.py:30
  12.9 0.6 %collective-permute-start.1 = (bf16[1,136,256]{2,1,0:T(8,128)(2,1)}, bf16[1,136,256]{2,1,0:T(8,128)(2,1)S(1)}, u32[]{:S(2)}, u32[]{:S(2)}) collective-permute-start(bf16[1,136,256]{2,1,0:T(8,128)(2,1)} %get-tuple-element.28.refs_0_), channel_id=1, source_target_pairs={{0,8},{1,9},{2,10},{3,11},{4,12},{5,13},{6,14},{7,15},{8,0},{9,1},... | collective-permute-start | bytes 208904 | tf_op jit(solution)/shard_map/ppermute | solution.py:30
  13.5 1.6 %collective-permute-start.5 = (bf16[1,264,128]{2,1,0:T(8,128)(2,1)}, bf16[1,264,128]{2,1,0:T(8,128)(2,1)S(1)}, u32[]{:S(2)}, u32[]{:S(2)}) collective-permute-start(bf16[1,264,128]{2,1,0:T(8,128)(2,1)} %get-tuple-element.30), channel_id=1, source_target_pairs={{0,4},{1,5},{2,6},{3,7},{4,0},{5,1},{6,2},{7,3},{8,12},{9,13},{10,... | collective-permute-start | bytes 202760 | tf_op jit(solution)/shard_map/ppermute | solution.py:30
  15.1 1.8 %collective-permute-start.6 = (bf16[1,264,128]{2,1,0:T(8,128)(2,1)}, bf16[1,264,128]{2,1,0:T(8,128)(2,1)S(1)}, u32[]{:S(2)}, u32[]{:S(2)}) collective-permute-start(bf16[1,264,128]{2,1,0:T(8,128)(2,1)} %get-tuple-element.31), channel_id=1, source_target_pairs={{0,6},{1,7},{2,4},{3,5},{4,2},{5,3},{6,0},{7,1},{8,14},{9,15},{10,... | collective-permute-start | bytes 202760 | tf_op jit(solution)/shard_map/ppermute | solution.py:30
  16.9 1.7 %copy-done = bf16[2,10,256,256]{3,2,1,0:T(8,128)(2,1)S(1)} copy-done((bf16[2,10,256,256]{3,2,1,0:T(8,128)(2,1)S(1)}, bf16[2,10,256,256]{3,2,1,0:T(8,128)(2,1)}, u32[]{:S(2)}) %copy-start) | copy-done | bytes 2621464
  18.6 0.9 %copy-done.1 = bf16[512,256]{1,0:T(8,128)(2,1)S(1)} copy-done((bf16[512,256]{1,0:T(8,128)(2,1)S(1)}, bf16[512,256]{1,0:T(8,128)(2,1)}, u32[]{:S(2)}) %copy-start.1) | copy-done | bytes 262168
  19.6 0.7 %copy-done.5 = s32[2,10]{1,0:T(2,128)S(1)} copy-done((s32[2,10]{1,0:T(2,128)S(1)}, s32[2,10]{1,0:T(2,128)}, u32[]{:S(2)}) %copy-start.5) | copy-done | bytes 104
  20.3 1.7 %shard_map.104.near_ref = f32[512,256]{1,0:T(8,128)S(1)} custom-call(s32[2,10]{1,0:T(2,128)S(1)} %copy-done.5, bf16[2,10,256,256]{3,2,1,0:T(8,128)(2,1)S(1)} %copy-done, bf16[512,256]{1,0:T(8,128)(2,1)S(1)} %copy-done.1, bf16[512,256]{1,0:T(8,128)(2,1)S(1)} %collective-permute-done.swap_ref, bf16[512,256]{1,0:T(8,128)(2,1)S(1)} %collective-permute-done.7.cross_ref), custom_call_target="tpu_custom_call" | custom-call | flops 671088640 | bytes 3932160 | tf_op jit(solution)/shard_map/pallas_call | solution.py:335
  22.0 0.6 %shard_map.105 = (f32[1,128,256]{2,1,0:T(8,128)S(1)}, bf16[1,128,256]{2,1,0:T(8,128)(2,1)S(1)}, bf16[1,128,256]{2,1,0:T(8,128)(2,1)S(1)}, bf16[1,128,256]{2,1,0:T(8,128)(2,1)S(1)}) custom-call(bf16[1,136,256]{2,1,0:T(8,128)(2,1)S(1)} %copy-done.2, bf16[1,136,256]{2,1,0:T(8,128)(2,1)S(1)} %collective-permute-done.1.refs_1_, ...), custom_call_target="tpu_custom_call" | custom-call | tf_op jit(solution)/shard_map/pallas_call | solution.py:356
  22.6 0.2 collective-permute-start.8
  22.8 1.6 %collective-permute-start.9 = (bf16[1,128,256]{2,1,0:T(8,128)(2,1)S(1)}, bf16[1,128,256]{2,1,0:T(8,128)(2,1)S(1)}, u32[]{:S(2)}, u32[]{:S(2)}) collective-permute-start(bf16[1,128,256]{2,1,0:T(8,128)(2,1)S(1)} %get-tuple-element.43), channel_id=1, source_target_pairs={{0,4},{1,5},{2,6},{3,7},{4,0},{5,1},{6,2},{7,3},{8,12},{9,13},{10,... | collective-permute-start | bytes 196616 | tf_op jit(solution)/shard_map/ppermute | solution.py:30
  24.4 1.8 %collective-permute-start.10 = (bf16[1,128,256]{2,1,0:T(8,128)(2,1)S(1)}, bf16[1,128,256]{2,1,0:T(8,128)(2,1)S(1)}, u32[]{:S(2)}, u32[]{:S(2)}) collective-permute-start(bf16[1,128,256]{2,1,0:T(8,128)(2,1)S(1)} %get-tuple-element.44), channel_id=1, source_target_pairs={{0,6},{1,7},{2,4},{3,5},{4,2},{5,3},{6,0},{7,1},{8,14},{9,15},{10,... | collective-permute-start | bytes 196616 | tf_op jit(solution)/shard_map/ppermute | solution.py:30
  26.2 1.5 %collective-permute-done.8.refs_0_ = bf16[1,128,256]{2,1,0:T(8,128)(2,1)S(1)} collective-permute-done((bf16[1,128,256]{2,1,0:T(8,128)(2,1)S(1)}, bf16[1,128,256]{2,1,0:T(8,128)(2,1)S(1)}, u32[]{:S(2)}, u32[]{:S(2)}) %collective-permute-start.8) | collective-permute-done | bytes 65568 | tf_op jit(solution)/shard_map/ppermute | solution.py:30
  27.6 0.1 collective-permute-done.9.refs_1_
  27.8 1.8 %collective-permute-done.10.refs_2_ = bf16[1,128,256]{2,1,0:T(8,128)(2,1)S(1)} collective-permute-done((bf16[1,128,256]{2,1,0:T(8,128)(2,1)S(1)}, bf16[1,128,256]{2,1,0:T(8,128)(2,1)S(1)}, u32[]{:S(2)}, u32[]{:S(2)}) %collective-permute-start.10) | collective-permute-done | bytes 65568 | tf_op jit(solution)/shard_map/ppermute | solution.py:30
  29.6 1.0 %shard_map.106 = (bf16[512,256]{1,0:T(8,128)(2,1)}, f32[320,128]{1,0:T(8,128)S(1)}) custom-call(bf16[2,64,256]{2,1,0:T(8,128)(2,1)S(1)} %copy-done.4, f32[512,256]{1,0:T(8,128)S(1)} %shard_map.104.near_ref, f32[1,128,256]{2,1,0:T(8,128)S(1)} %get-tuple-element.41.own_ref, bf16[1,128,256]{2,1,0:T(8,128)(2,1)S(1)} %collective-permute-done.8.refs_0_, ...), custom_call_target="tpu_custom_call" | custom-call | tf_op jit(solution)/shard_map/pallas_call | solution.py:366
  30.5 1.4 %collective-permute-done.11 = f32[320,128]{1,0:T(8,128)S(1)} collective-permute-done((f32[320,128]{1,0:T(8,128)S(1)}, f32[320,128]{1,0:T(8,128)S(1)}, u32[]{:S(2)}, u32[]{:S(2)}) %collective-permute-start.11) | collective-permute-done | bytes 163872 | tf_op jit(solution)/shard_map/ppermute | solution.py:34
  32.0 0.7 %collective-permute-start.15 = (bf16[320,128]{1,0:T(8,128)(2,1)S(1)}, bf16[320,128]{1,0:T(8,128)(2,1)S(1)}, u32[]{:S(2)}, u32[]{:S(2)}) collective-permute-start(bf16[320,128]{1,0:T(8,128)(2,1)S(1)} %get-tuple-element.49), channel_id=1, source_target_pairs={{1,15},{3,13},{5,11},{7,9},{9,7},{11,5},{13,3},{15,1},{17,31},{19,... | collective-permute-start | bytes 245768 | tf_op jit(solution)/shard_map/ppermute | solution.py:30
  32.6 1.8 %collective-permute-start.14 = (bf16[320,128]{1,0:T(8,128)(2,1)S(1)}, bf16[320,128]{1,0:T(8,128)(2,1)S(1)}, u32[]{:S(2)}, u32[]{:S(2)}) collective-permute-start(bf16[320,128]{1,0:T(8,128)(2,1)S(1)} %get-tuple-element.49), channel_id=1, source_target_pairs={{0,6},{1,11},{2,4},{3,9},{4,2},{5,15},{6,0},{7,13},{8,14},{9,3},{1... | collective-permute-start | bytes 245768 | tf_op jit(solution)/shard_map/ppermute | solution.py:30
  34.5 0.8 %collective-permute-start.13 = (bf16[320,128]{1,0:T(8,128)(2,1)S(1)}, bf16[320,128]{1,0:T(8,128)(2,1)S(1)}, u32[]{:S(2)}, u32[]{:S(2)}) collective-permute-start(bf16[320,128]{1,0:T(8,128)(2,1)S(1)} %get-tuple-element.49), channel_id=1, source_target_pairs={{0,4},{1,13},{2,6},{3,15},{4,0},{5,9},{6,2},{7,11},{8,12},{9,5},{1... | collective-permute-start | bytes 245768 | tf_op jit(solution)/shard_map/ppermute | solution.py:30
  35.3 0.9 %collective-permute-start.12 = (bf16[320,128]{1,0:T(8,128)(2,1)S(1)}, bf16[320,128]{1,0:T(8,128)(2,1)S(1)}, u32[]{:S(2)}, u32[]{:S(2)}) collective-permute-start(bf16[320,128]{1,0:T(8,128)(2,1)S(1)} %get-tuple-element.49), channel_id=1, source_target_pairs={{0,2},{1,9},{2,0},{3,11},{4,6},{5,13},{6,4},{7,15},{8,10},{9,1},{1... | collective-permute-start | bytes 245768 | tf_op jit(solution)/shard_map/ppermute | solution.py:30
  36.2 1.8 %collective-permute-done.14 = bf16[320,128]{1,0:T(8,128)(2,1)S(1)} collective-permute-done((bf16[320,128]{1,0:T(8,128)(2,1)S(1)}, bf16[320,128]{1,0:T(8,128)(2,1)S(1)}, u32[]{:S(2)}, u32[]{:S(2)}) %collective-permute-start.14) | collective-permute-done | bytes 81952 | tf_op jit(solution)/shard_map/ppermute | solution.py:30
  38.0 1.8 %collective-permute-done.13 = bf16[320,128]{1,0:T(8,128)(2,1)S(1)} collective-permute-done((bf16[320,128]{1,0:T(8,128)(2,1)S(1)}, bf16[320,128]{1,0:T(8,128)(2,1)S(1)}, u32[]{:S(2)}, u32[]{:S(2)}) %collective-permute-start.13) | collective-permute-done | bytes 81952 | tf_op jit(solution)/shard_map/ppermute | solution.py:30
  39.8 0.1 fusion.3
  39.9 2.4 %collective-permute-start.16 = (f32[2,320,128]{2,1,0:T(8,128)S(1)}, f32[2,320,128]{2,1,0:T(8,128)S(1)}, u32[]{:S(2)}, u32[]{:S(2)}) collective-permute-start(f32[2,320,128]{2,1,0:T(8,128)S(1)} %pad_maximum_fusion.mine_ref), channel_id=1, source_target_pairs={{0,1},{1,0},{2,3},{3,2},{4,5},{5,4},{6,7},{7,6},{8,9},{9,8},{10,11... | collective-permute-start | bytes 983048 | tf_op jit(solution)/shard_map/ppermute | solution.py:34
  42.3 1.3 %collective-permute-done.16.other_ref = f32[2,320,128]{2,1,0:T(8,128)S(1)} collective-permute-done((f32[2,320,128]{2,1,0:T(8,128)S(1)}, f32[2,320,128]{2,1,0:T(8,128)S(1)}, u32[]{:S(2)}, u32[]{:S(2)}) %collective-permute-start.16) | collective-permute-done | bytes 327712 | tf_op jit(solution)/shard_map/ppermute | solution.py:34
  43.6 11.1 %shard_map.107 = (f32[256,256]{1,0:T(8,128)}, bf16[3,256,256]{2,1,0:T(8,128)(2,1)}) custom-call(f32[320,128]{1,0:T(8,128)S(1)} %get-tuple-element.50.seg_ref, f32[2,320,128]{2,1,0:T(8,128)S(1)} %pad_maximum_fusion.mine_ref, f32[2,320,128]{2,1,0:T(8,128)S(1)} %collective-permute-done.16.other_ref), custom_call_target="tpu_custom_call" | custom-call | tf_op jit(solution)/shard_map/pallas_call | solution.py:271
  (22 shorter events, 0.1 us)
Async XLA Ops:
  0.6 1.9 %collective-permute-start = (bf16[512,256]{1,0:T(8,128)(2,1)}, bf16[512,256]{1,0:T(8,128)(2,1)S(1)}, u32[]{:S(2)}, u32[]{:S(2)}) collective-permute-start(bf16[512,256]{1,0:T(8,128)(2,1)} %own_ref.1), channel_id=1, source_target_pairs={{0,1},{1,0},{2,3},{3,2},{4,5},{5,4},{6,7},{7,6},{8,9},{9,8},{10,11... | collective-permute-start | bytes 786440 | tf_op jit(solution)/shard_map/ppermute | solution.py:298
  1.1 12.4 %collective-permute-start.7 = (bf16[512,256]{1,0:T(8,128)(2,1)}, bf16[512,256]{1,0:T(8,128)(2,1)S(1)}, u32[]{:S(2)}, u32[]{:S(2)}) collective-permute-start(bf16[512,256]{1,0:T(8,128)(2,1)} %own_ref.1), channel_id=1, source_target_pairs={{1,2},{3,4},{5,6},{7,8},{9,10},{11,12},{13,14},{15,16},{17,18},{19... | collective-permute-start | bytes 786440 | tf_op jit(solution)/shard_map/ppermute | solution.py:300
  5.2 10.0 %collective-permute-start.4 = (bf16[1,264,128]{2,1,0:T(8,128)(2,1)}, bf16[1,264,128]{2,1,0:T(8,128)(2,1)S(1)}, u32[]{:S(2)}, u32[]{:S(2)}) collective-permute-start(bf16[1,264,128]{2,1,0:T(8,128)(2,1)} %get-tuple-element.29), channel_id=1, source_target_pairs={{0,2},{1,3},{2,0},{3,1},{4,6},{5,7},{6,4},{7,5},{8,10},{9,11},{10,... | collective-permute-start | bytes 202760 | tf_op jit(solution)/shard_map/ppermute | solution.py:30
  8.3 13.7 %collective-permute-start.3 = (bf16[1,136,256]{2,1,0:T(8,128)(2,1)}, bf16[1,136,256]{2,1,0:T(8,128)(2,1)S(1)}, u32[]{:S(2)}, u32[]{:S(2)}) collective-permute-start(bf16[1,136,256]{2,1,0:T(8,128)(2,1)} %get-tuple-element.28.refs_0_), channel_id=1, source_target_pairs={{0,24},{1,25},{2,26},{3,27},{4,28},{5,29},{6,30},{7,31},{8,16},{9,... | collective-permute-start | bytes 208904 | tf_op jit(solution)/shard_map/ppermute | solution.py:30
  12.9 9.1 %collective-permute-start.2 = (bf16[1,136,256]{2,1,0:T(8,128)(2,1)}, bf16[1,136,256]{2,1,0:T(8,128)(2,1)S(1)}, u32[]{:S(2)}, u32[]{:S(2)}) collective-permute-start(bf16[1,136,256]{2,1,0:T(8,128)(2,1)} %get-tuple-element.28.refs_0_), channel_id=1, source_target_pairs={{0,16},{1,17},{2,18},{3,19},{4,20},{5,21},{6,22},{7,23},{8,24},{9,... | collective-permute-start | bytes 208904 | tf_op jit(solution)/shard_map/ppermute | solution.py:30
  12.9 9.1 %collective-permute-start.1 = (bf16[1,136,256]{2,1,0:T(8,128)(2,1)}, bf16[1,136,256]{2,1,0:T(8,128)(2,1)S(1)}, u32[]{:S(2)}, u32[]{:S(2)}) collective-permute-start(bf16[1,136,256]{2,1,0:T(8,128)(2,1)} %get-tuple-element.28.refs_0_), channel_id=1, source_target_pairs={{0,8},{1,9},{2,10},{3,11},{4,12},{5,13},{6,14},{7,15},{8,0},{9,1},... | collective-permute-start | bytes 208904 | tf_op jit(solution)/shard_map/ppermute | solution.py:30
  13.5 8.4 %collective-permute-start.5 = (bf16[1,264,128]{2,1,0:T(8,128)(2,1)}, bf16[1,264,128]{2,1,0:T(8,128)(2,1)S(1)}, u32[]{:S(2)}, u32[]{:S(2)}) collective-permute-start(bf16[1,264,128]{2,1,0:T(8,128)(2,1)} %get-tuple-element.30), channel_id=1, source_target_pairs={{0,4},{1,5},{2,6},{3,7},{4,0},{5,1},{6,2},{7,3},{8,12},{9,13},{10,... | collective-permute-start | bytes 202760 | tf_op jit(solution)/shard_map/ppermute | solution.py:30
  15.1 6.9 %collective-permute-start.6 = (bf16[1,264,128]{2,1,0:T(8,128)(2,1)}, bf16[1,264,128]{2,1,0:T(8,128)(2,1)S(1)}, u32[]{:S(2)}, u32[]{:S(2)}) collective-permute-start(bf16[1,264,128]{2,1,0:T(8,128)(2,1)} %get-tuple-element.31), channel_id=1, source_target_pairs={{0,6},{1,7},{2,4},{3,5},{4,2},{5,3},{6,0},{7,1},{8,14},{9,15},{10,... | collective-permute-start | bytes 202760 | tf_op jit(solution)/shard_map/ppermute | solution.py:30
  16.9 1.7 %copy-start = (bf16[2,10,256,256]{3,2,1,0:T(8,128)(2,1)S(1)}, bf16[2,10,256,256]{3,2,1,0:T(8,128)(2,1)}, u32[]{:S(2)}) copy-start(bf16[2,10,256,256]{3,2,1,0:T(8,128)(2,1)} %blocks_ref.1) | copy-start | bytes 7864324
  18.6 0.9 %copy-start.1 = (bf16[512,256]{1,0:T(8,128)(2,1)S(1)}, bf16[512,256]{1,0:T(8,128)(2,1)}, u32[]{:S(2)}) copy-start(bf16[512,256]{1,0:T(8,128)(2,1)} %own_ref.1) | copy-start | bytes 786436
  19.6 0.7 %copy-start.5 = (s32[2,10]{1,0:T(2,128)S(1)}, s32[2,10]{1,0:T(2,128)}, u32[]{:S(2)}) copy-start(s32[2,10]{1,0:T(2,128)} %list_ref.1) | copy-start | bytes 244
  20.3 1.8 %copy-start.2 = (bf16[1,136,256]{2,1,0:T(8,128)(2,1)S(1)}, bf16[1,136,256]{2,1,0:T(8,128)(2,1)}, u32[]{:S(2)}) copy-start(bf16[1,136,256]{2,1,0:T(8,128)(2,1)} %get-tuple-element.28.refs_0_) | copy-start | bytes 208900
  20.3 1.8 %copy-start.3 = (bf16[1,264,128]{2,1,0:T(8,128)(2,1)S(1)}, bf16[1,264,128]{2,1,0:T(8,128)(2,1)}, u32[]{:S(2)}) copy-start(bf16[1,264,128]{2,1,0:T(8,128)(2,1)} %get-tuple-element.37.refs_4_) | copy-start | bytes 202756
  20.3 9.3 %copy-start.4 = (bf16[2,64,256]{2,1,0:T(8,128)(2,1)S(1)}, bf16[2,64,256]{2,1,0:T(8,128)(2,1)}, u32[]{:S(2)}) copy-start(bf16[2,64,256]{2,1,0:T(8,128)(2,1)} %get-tuple-element.27.basis_ref) | copy-start | bytes 196612
  22.6 5.0 %collective-permute-start.8 = (bf16[1,128,256]{2,1,0:T(8,128)(2,1)S(1)}, bf16[1,128,256]{2,1,0:T(8,128)(2,1)S(1)}, u32[]{:S(2)}, u32[]{:S(2)}) collective-permute-start(bf16[1,128,256]{2,1,0:T(8,128)(2,1)S(1)} %get-tuple-element.42), channel_id=1, source_target_pairs={{0,2},{1,3},{2,0},{3,1},{4,6},{5,7},{6,4},{7,5},{8,10},{9,11},{10,... | collective-permute-start | bytes 196616 | tf_op jit(solution)/shard_map/ppermute | solution.py:30
  22.8 4.9 %collective-permute-start.9 = (bf16[1,128,256]{2,1,0:T(8,128)(2,1)S(1)}, bf16[1,128,256]{2,1,0:T(8,128)(2,1)S(1)}, u32[]{:S(2)}, u32[]{:S(2)}) collective-permute-start(bf16[1,128,256]{2,1,0:T(8,128)(2,1)S(1)} %get-tuple-element.43), channel_id=1, source_target_pairs={{0,4},{1,5},{2,6},{3,7},{4,0},{5,1},{6,2},{7,3},{8,12},{9,13},{10,... | collective-permute-start | bytes 196616 | tf_op jit(solution)/shard_map/ppermute | solution.py:30
  24.4 5.2 %collective-permute-start.10 = (bf16[1,128,256]{2,1,0:T(8,128)(2,1)S(1)}, bf16[1,128,256]{2,1,0:T(8,128)(2,1)S(1)}, u32[]{:S(2)}, u32[]{:S(2)}) collective-permute-start(bf16[1,128,256]{2,1,0:T(8,128)(2,1)S(1)} %get-tuple-element.44), channel_id=1, source_target_pairs={{0,6},{1,7},{2,4},{3,5},{4,2},{5,3},{6,0},{7,1},{8,14},{9,15},{10,... | collective-permute-start | bytes 196616 | tf_op jit(solution)/shard_map/ppermute | solution.py:30
  30.5 1.4 %collective-permute-start.11 = (f32[320,128]{1,0:T(8,128)S(1)}, f32[320,128]{1,0:T(8,128)S(1)}, u32[]{:S(2)}, u32[]{:S(2)}) collective-permute-start(f32[320,128]{1,0:T(8,128)S(1)} %get-tuple-element.46), channel_id=1, source_target_pairs={{0,1},{1,0},{2,3},{3,2},{4,5},{5,4},{6,7},{7,6},{8,9},{9,8},{10,11... | collective-permute-start | bytes 491528 | tf_op jit(solution)/shard_map/ppermute | solution.py:34
  32.0 4.2 %collective-permute-start.15 = (bf16[320,128]{1,0:T(8,128)(2,1)S(1)}, bf16[320,128]{1,0:T(8,128)(2,1)S(1)}, u32[]{:S(2)}, u32[]{:S(2)}) collective-permute-start(bf16[320,128]{1,0:T(8,128)(2,1)S(1)} %get-tuple-element.49), channel_id=1, source_target_pairs={{1,15},{3,13},{5,11},{7,9},{9,7},{11,5},{13,3},{15,1},{17,31},{19,... | collective-permute-start | bytes 245768 | tf_op jit(solution)/shard_map/ppermute | solution.py:30
  32.6 5.4 %collective-permute-start.14 = (bf16[320,128]{1,0:T(8,128)(2,1)S(1)}, bf16[320,128]{1,0:T(8,128)(2,1)S(1)}, u32[]{:S(2)}, u32[]{:S(2)}) collective-permute-start(bf16[320,128]{1,0:T(8,128)(2,1)S(1)} %get-tuple-element.49), channel_id=1, source_target_pairs={{0,6},{1,11},{2,4},{3,9},{4,2},{5,15},{6,0},{7,13},{8,14},{9,3},{1... | collective-permute-start | bytes 245768 | tf_op jit(solution)/shard_map/ppermute | solution.py:30
  34.5 5.3 %collective-permute-start.13 = (bf16[320,128]{1,0:T(8,128)(2,1)S(1)}, bf16[320,128]{1,0:T(8,128)(2,1)S(1)}, u32[]{:S(2)}, u32[]{:S(2)}) collective-permute-start(bf16[320,128]{1,0:T(8,128)(2,1)S(1)} %get-tuple-element.49), channel_id=1, source_target_pairs={{0,4},{1,13},{2,6},{3,15},{4,0},{5,9},{6,2},{7,11},{8,12},{9,5},{1... | collective-permute-start | bytes 245768 | tf_op jit(solution)/shard_map/ppermute | solution.py:30
  35.3 4.5 %collective-permute-start.12 = (bf16[320,128]{1,0:T(8,128)(2,1)S(1)}, bf16[320,128]{1,0:T(8,128)(2,1)S(1)}, u32[]{:S(2)}, u32[]{:S(2)}) collective-permute-start(bf16[320,128]{1,0:T(8,128)(2,1)S(1)} %get-tuple-element.49), channel_id=1, source_target_pairs={{0,2},{1,9},{2,0},{3,11},{4,6},{5,13},{6,4},{7,15},{8,10},{9,1},{1... | collective-permute-start | bytes 245768 | tf_op jit(solution)/shard_map/ppermute | solution.py:30
  39.9 3.7 %collective-permute-start.16 = (f32[2,320,128]{2,1,0:T(8,128)S(1)}, f32[2,320,128]{2,1,0:T(8,128)S(1)}, u32[]{:S(2)}, u32[]{:S(2)}) collective-permute-start(f32[2,320,128]{2,1,0:T(8,128)S(1)} %pad_maximum_fusion.mine_ref), channel_id=1, source_target_pairs={{0,1},{1,0},{2,3},{3,2},{4,5},{5,4},{6,7},{7,6},{8,9},{9,8},{10,11... | collective-permute-start | bytes 983048 | tf_op jit(solution)/shard_map/ppermute | solution.py:34

commit v4 on v3

--- a/solution.py
+++ b/solution.py
@@ -9,6 +9,7 @@
 
 LEVELS = 3
 PLANE = 4
+NEAR_KIB = 49152
 FIRST_KIB = 61440
 AXES = ("seg", "sub")
 VMEM = pl.BlockSpec(memory_space=pltpu.VMEM)
@@ -131,33 +132,33 @@
         outs[m][0] = total.astype(outs[m].dtype)
 
 
-def near_kernel(list_ref, blocks_ref, own_ref, swap_ref, cross_ref, out_ref, held):
-    leaf = pl.program_id(0)
-    leaves = held.shape[0] // 3
-
-    @pl.when(leaf == 0)
-    def _():
+def near_kernel(list_hbm, blocks_ref, own_hbm, swap_ref, cross_ref, out_ref, held, entries, sems):
+    leaves, count, rows, _ = blocks_ref.shape
+    pairs = [(list_hbm, entries)]
+    pairs += [(own_hbm.at[pl.ds(j * rows, rows)], held.at[j]) for j in range(leaves)]
+    copies = [pltpu.make_async_copy(src, dst, sems.at[i]) for i, (src, dst) in enumerate(pairs)]
+    for copy in copies:
+        copy.start()
+    for i, src in enumerate((swap_ref, cross_ref)):
         for j in range(leaves):
-            rows = slice(j * 256, (j + 1) * 256)
-            held[j] = own_ref[rows, :]
-            held[leaves + j] = swap_ref[rows, :]
-            held[2 * leaves + j] = cross_ref[rows, :]
-        held[3 * leaves] = jnp.zeros_like(held[0])
-
+            held[(i + 1) * leaves + j] = src[j * rows : (j + 1) * rows, :]
+    held[3 * leaves] = jnp.zeros(held.shape[1:], held.dtype)
+    for copy in copies:
+        copy.wait()
     device = lax.axis_index("seg") * lax.axis_size("sub") + lax.axis_index("sub")
     odd = device % 2
     before = (2 - odd) * leaves
     after = (1 + odd) * leaves
-    acc = jnp.zeros((256, 256), jnp.float32)
-    for k in range(blocks_ref.shape[1]):
-        entry = list_ref[leaf, k]
-        shift = entry - device * leaves
-        slot = jnp.where(
-            shift < 0, before + leaves + shift, jnp.where(shift < leaves, shift, after + shift - leaves)
-        )
-        slot = jnp.where(entry < 0, 3 * leaves, slot)
-        acc = acc + dot(blocks_ref[0, k], held[slot])
-    out_ref[...] = acc
+    for l in range(leaves):
+        acc = jnp.zeros((rows, held.shape[2]), jnp.float32)
+        for k in range(count):
+            entry = entries[l, k]
+            shift = entry - device * leaves
+            outside = jnp.where(shift < 0, before + leaves + shift, after + shift - leaves)
+            slot = jnp.where((shift < 0) | (shift >= leaves), outside, shift)
+            slot = jnp.where(entry < 0, 3 * leaves, slot)
+            acc = acc + dot(blocks_ref[l, k], held[slot])
+        out_ref[l * rows : (l + 1) * rows, :] = acc
 
 
 def combine_kernel(basis_ref, near_ref, own_ref, *refs):
@@ -189,7 +190,7 @@
 def mmt(a,b):
     ah,al=split(a); bh,bl=split(b)
     return dg(jnp.concatenate([ah,al,ah],1),jnp.concatenate([bh,bh,bl],1),((1,),(1,)))
-def eliminate(P, lane, row):
+def eliminate(P, lane, row, tick):
     base=lane & ~31
     sub=lane & 31
     V=[jnp.where(row+8*rv==sub,1.0,0.0).astype(jnp.float32) for rv in range(4)]
@@ -210,6 +211,7 @@
             for rv in range(m,4):
                 P[rv]=P[rv]-M[rv-m]*fp
                 V[rv]=V[rv]-M[rv-m]*fv
+            tick(8*m+k)
         rs=lax.rsqrt(piv)
         P[m]=P[m]*rs
         V[m]=V[m]*rs
@@ -231,30 +233,13 @@
         rows = unpack(packed)
         for kb in range(8):
             X[kb, 32 * t : 32 * t + 32, :] = rows[32 * kb : 32 * kb + 32, :]
-    for kb in range(8):
-        off=32*kb; c0=off//128*128; lo=off%128
-        P=[]
-        for rv in range(4):
-            acc=None
-            for t in range(4):
-                v=X[kb,t*32+8*rv:t*32+8*rv+8,c0:c0+128]
-                sh=(32*t-lo)%128
-                if sh: v=pltpu.roll(v,sh,1)
-                acc=v if acc is None else jnp.where(grp==t,v,acc)
-            P.append(acc)
-        P,V=eliminate(P,lane,row)
-        Pf=jnp.concatenate(P,0); Vf=jnp.concatenate(V,0)
-        Wbd=jnp.where(bd,jnp.concatenate([Vf]*4,0),0.0)
-        x=X[kb]
-        x=jnp.where((l256>=off)&(l256<off+32),jnp.where(l256-off==r256,1.0,0.0),x)
-        panel=mms(lstack(Wbd),rstack(x)); ps=rstack(panel)
-        chunks={}
-        for i in range(kb+1,8):
-            c=i//4
-            if c not in chunks: chunks[c]=jnp.transpose(panel[:,c*128:c*128+128])
-            T=chunks[c][(i%4)*32:(i%4)*32+32,:]
-            L=jnp.where(bd,jnp.concatenate([T]*4,0),0.0)
-            X[i]=jnp.where((l256>=off)&(l256<off+32),0.0,X[i])-mms(lstack(L),ps)
+    pending=[]
+    def tick(step):
+        if pending and step%2==2-1: pending.pop(0)()
+    def update(i,L,ps,off):
+        X[i]=jnp.where((l256>=off)&(l256<off+32),0.0,X[i])-mms(L,ps)
+    def emit(kb,panel,Pf):
+        off=32*kb; lo=off%128
         for t in range(4):
             pt=panel[32*t:32*t+32,:]
             sh=(lo-32*t)%128
@@ -263,6 +248,60 @@
             d2=jnp.concatenate([d,d],1)
             Rb[t,off:off+32,:]=jnp.where(l32>=off+32,pt,jnp.where((l32>=off)&(l32-off>=r32),d2,0.0))
             if t>0: Wb[t-1,off:off+32,:]=jnp.where(l32<off+32,pt,0.0)
+    def place(rows_of, block, lo):
+        out=[]
+        for t in range(4):
+            sh=(32*t-lo)%128
+            v=rows_of(t)
+            out.append(pltpu.roll(v,sh,1) if sh else v)
+        return out
+    def packed(block, kb_cols):
+        off=32*kb_cols; c0=off//128*128; lo=off%128
+        vs=place(lambda t:X[block,32*t:32*t+32,c0:c0+128],block,lo)
+        acc=vs[0]
+        for t in range(1,4): acc=jnp.where(grp32==t,vs[t],acc)
+        return acc
+    grp32=lax.broadcasted_iota(jnp.int32,(32,128),1)//32
+    state={}
+    def prep(kb):
+        off=32*(kb+1); c0=off//128*128; lo=off%128
+        q=jnp.concatenate(place(lambda t:X[kb,32*t:32*t+32,c0:c0+128],kb,lo),0)
+        state['q']=rstack(jnp.where(bd,q,0.0))
+        state['d']=packed(kb+1,kb+1)
+    def make_panel(kb,Vf):
+        off=32*kb
+        Wbd=jnp.where(bd,jnp.concatenate([Vf]*4,0),0.0)
+        x=X[kb]
+        x=jnp.where((l256>=off)&(l256<off+32),jnp.where(l256-off==r256,1.0,0.0),x)
+        state['panel']=mms(lstack(Wbd),rstack(x))
+        state['ps']=rstack(state['panel'])
+        state['ch']={}
+    def go(i,off):
+        c=i//4
+        if c not in state['ch']: state['ch'][c]=jnp.transpose(state['panel'][:,c*128:c*128+128])
+        T=state['ch'][c][(i%4)*32:(i%4)*32+32,:]
+        update(i,lstack(jnp.where(bd,jnp.concatenate([T]*4,0),0.0)),state['ps'],off)
+    def emit_out(kb,Pf): emit(kb,state['panel'],Pf)
+    p32=packed(0,0)
+    for kb in range(8):
+        if kb==0: pending.append(functools.partial(prep,0))
+        P=[p32[8*r:8*r+8,:] for r in range(4)]
+        P,V=eliminate(P,lane,row,tick)
+        while pending: pending.pop(0)()
+        Pf=jnp.concatenate(P,0); Vf=jnp.concatenate(V,0)
+        if kb<7:
+            rn=mms(lstack(Vf),state['q'])
+            h,l=split(rn)
+            G=dg(jnp.concatenate([h,h,l],0),jnp.concatenate([h,l,h],0),((0,),(0,)))
+            g=G[0:32,:]
+            for t in range(1,4): g=jnp.where(grp32==t,G[32*t:32*t+32,:],g)
+            p32=state['d']-g
+        pending.append(functools.partial(make_panel,kb,Vf))
+        for i in range(kb+1,8):
+            pending.append(functools.partial(go,i,32*kb))
+            if i==min(kb+2,7) and kb+1<7: pending.append(functools.partial(prep,kb+1))
+        pending.append(functools.partial(emit_out,kb,Pf))
+    while pending: pending.pop(0)()
     r_ref[...]=Rb[0]
     for t in range(3):
         tr_ref[t]=mmt(Rb[t],Wb[t]).astype(jnp.bfloat16)
@@ -334,18 +373,15 @@
     gathered = [hop(pays[m], m, m) for m in range(1, PLANE)]
     near_part = pl.pallas_call(
         near_kernel,
-        grid=(leaf_count,),
         out_shape=jax.ShapeDtypeStruct((rows, width), jnp.float32),
-        in_specs=[
-            SMEM,
-            pl.BlockSpec((1, near_count, leaf_rows, leaf_rows), lambda i: (i, 0, 0, 0)),
-            VMEM,
-            VMEM,
-            VMEM,
+        in_specs=[hbm, VMEM, hbm, VMEM, VMEM],
+        out_specs=VMEM,
+        scratch_shapes=[
+            pltpu.VMEM((3 * leaf_count + 1, leaf_rows, width), bf16),
+            pltpu.SMEM(near_list.shape, jnp.int32),
+            pltpu.SemaphoreType.DMA((1 + leaf_count,)),
         ],
-        out_specs=pl.BlockSpec((leaf_rows, width), lambda i: (i, 0)),
-        scratch_shapes=[pltpu.VMEM((3 * leaf_count + 1, leaf_rows, width), jnp.bfloat16)],
-        compiler_params=params(),
+        compiler_params=params(NEAR_KIB),
         cost_estimate=pl.CostEstimate(
             flops=2 * rows * near_count * leaf_rows * width,
             bytes_accessed=near_blocks.size * 2 + 5 * rows * width * 2,

time: 55 us -> 53.7 us (0.976)
  Pallas kernels: 17 us -> 15.8 us
    pallas_call x1, Pallas kernels: 11.1 us -> 10.1 us  [factor_all(): pl.pallas_call(factor_kernel, out_shape=(jax.ShapeDtypeStruct((256, 256),...]
where the time goes in v4:
time: 53.7 us; the launch traced here: 53.5 us
  starting transfers between devices  23.1 us (43%)
  Pallas kernels  15.8 us (29%)
  waiting for transfers between devices  10.4 us (19%)
  local copies, waits for them, and re-layouts  3.38 us (6%)
  between operations  0.76 us (1%)
    ppermute x13, starting transfers between devices, hop(): return lax.ppermute(value, AXES, pairs)  19.5 us
    pallas_call x1, Pallas kernels, factor_all(): pl.pallas_call(factor_kernel, out_shape=(jax.ShapeDtypeStruct((256, 256),...  10.1 us
    ppermute x13, waiting for transfers between devices, hop(): return lax.ppermute(value, AXES, pairs)  7.03 us
    unnamed x12, local copies, waits for them, and re-layouts  3.38 us
    ppermute x2, waiting for transfers between devices, sub_hop(): lax.ppermute(value, 'sub', [(i, i ^ mask) for i in range(lax.axis_size('s...  2.65 us
    pallas_call x1, Pallas kernels, body(): pl.pallas_call(first_kernel, out_shape=[jax.ShapeDtypeStruct((1, leaf_cou...  2.63 us
    ppermute x2, starting transfers between devices, sub_hop(): lax.ppermute(value, 'sub', [(i, i ^ mask) for i in range(lax.axis_size('s...  2.42 us
    pallas_call x1, Pallas kernels, body(): pl.pallas_call(near_kernel, out_shape=jax.ShapeDtypeStruct((rows, width),...  1.45 us
  transfers between devices with their start and end apart: 17, of which 8 were waited for; matrix products, arithmetic and copies ran while one was open for 0% of the time, Pallas kernels for 8%

profile of v4, /device:TPU:0, one launch (start us, length us, event | category | flops | bytes accessed | tf_op | source)
XLA Modules:
  0.0 53.5 jit_solution(14691557908553555329)
XLA Ops:
  0.6 0.5 collective-permute-start
  1.1 0.7 %collective-permute-start.7 = (bf16[512,256]{1,0:T(8,128)(2,1)}, bf16[512,256]{1,0:T(8,128)(2,1)S(1)}, u32[]{:S(2)}, u32[]{:S(2)}) collective-permute-start(bf16[512,256]{1,0:T(8,128)(2,1)} %own_hbm.1), channel_id=1, source_target_pairs={{1,2},{3,4},{5,6},{7,8},{9,10},{11,12},{13,14},{15,16},{17,18},{19... | collective-permute-start | bytes 786440 | tf_op jit(solution)/shard_map/ppermute | solution.py:339
  1.8 0.7 %collective-permute-done.swap_ref = bf16[512,256]{1,0:T(8,128)(2,1)S(1)} collective-permute-done((bf16[512,256]{1,0:T(8,128)(2,1)}, bf16[512,256]{1,0:T(8,128)(2,1)S(1)}, u32[]{:S(2)}, u32[]{:S(2)}) %collective-permute-start) | collective-permute-done | bytes 262176 | tf_op jit(solution)/shard_map/ppermute | solution.py:337
  2.5 2.6 %shard_map.103 = (bf16[1,136,256]{2,1,0:T(8,128)(2,1)}, bf16[2,64,256]{2,1,0:T(8,128)(2,1)}, bf16[1,264,128]{2,1,0:T(8,128)(2,1)}, bf16[1,264,128]{2,1,0:T(8,128...) custom-call(bf16[2,64,256]{2,1,0:T(8,128)(2,1)} %basis_hbm, bf16[512,256]{1,0:T(8,128)(2,1)} %own_hbm.1, ...), custom_call_target="tpu_custom_call" | custom-call | tf_op jit(solution)/shard_map/pallas_call | solution.py:346
  5.2 3.1 %collective-permute-start.4 = (bf16[1,264,128]{2,1,0:T(8,128)(2,1)}, bf16[1,264,128]{2,1,0:T(8,128)(2,1)S(1)}, u32[]{:S(2)}, u32[]{:S(2)}) collective-permute-start(bf16[1,264,128]{2,1,0:T(8,128)(2,1)} %get-tuple-element.29), channel_id=1, source_target_pairs={{0,2},{1,3},{2,0},{3,1},{4,6},{5,7},{6,4},{7,5},{8,10},{9,11},{10,... | collective-permute-start | bytes 202760 | tf_op jit(solution)/shard_map/ppermute | solution.py:31
  8.3 4.6 %collective-permute-start.3 = (bf16[1,136,256]{2,1,0:T(8,128)(2,1)}, bf16[1,136,256]{2,1,0:T(8,128)(2,1)S(1)}, u32[]{:S(2)}, u32[]{:S(2)}) collective-permute-start(bf16[1,136,256]{2,1,0:T(8,128)(2,1)} %get-tuple-element.28.refs_0_), channel_id=1, source_target_pairs={{0,24},{1,25},{2,26},{3,27},{4,28},{5,29},{6,30},{7,31},{8,16},{9,... | collective-permute-start | bytes 208904 | tf_op jit(solution)/shard_map/ppermute | solution.py:31
  12.9 0.6 %collective-permute-start.1 = (bf16[1,136,256]{2,1,0:T(8,128)(2,1)}, bf16[1,136,256]{2,1,0:T(8,128)(2,1)S(1)}, u32[]{:S(2)}, u32[]{:S(2)}) collective-permute-start(bf16[1,136,256]{2,1,0:T(8,128)(2,1)} %get-tuple-element.28.refs_0_), channel_id=1, source_target_pairs={{0,8},{1,9},{2,10},{3,11},{4,12},{5,13},{6,14},{7,15},{8,0},{9,1},... | collective-permute-start | bytes 208904 | tf_op jit(solution)/shard_map/ppermute | solution.py:31
  13.5 1.6 %collective-permute-start.5 = (bf16[1,264,128]{2,1,0:T(8,128)(2,1)}, bf16[1,264,128]{2,1,0:T(8,128)(2,1)S(1)}, u32[]{:S(2)}, u32[]{:S(2)}) collective-permute-start(bf16[1,264,128]{2,1,0:T(8,128)(2,1)} %get-tuple-element.30), channel_id=1, source_target_pairs={{0,4},{1,5},{2,6},{3,7},{4,0},{5,1},{6,2},{7,3},{8,12},{9,13},{10,... | collective-permute-start | bytes 202760 | tf_op jit(solution)/shard_map/ppermute | solution.py:31
  15.1 1.8 %collective-permute-start.6 = (bf16[1,264,128]{2,1,0:T(8,128)(2,1)}, bf16[1,264,128]{2,1,0:T(8,128)(2,1)S(1)}, u32[]{:S(2)}, u32[]{:S(2)}) collective-permute-start(bf16[1,264,128]{2,1,0:T(8,128)(2,1)} %get-tuple-element.31), channel_id=1, source_target_pairs={{0,6},{1,7},{2,4},{3,5},{4,2},{5,3},{6,0},{7,1},{8,14},{9,15},{10,... | collective-permute-start | bytes 202760 | tf_op jit(solution)/shard_map/ppermute | solution.py:31
  16.9 1.7 %copy-done = bf16[2,10,256,256]{3,2,1,0:T(8,128)(2,1)S(1)} copy-done((bf16[2,10,256,256]{3,2,1,0:T(8,128)(2,1)S(1)}, bf16[2,10,256,256]{3,2,1,0:T(8,128)(2,1)}, u32[]{:S(2)}) %copy-start) | copy-done | bytes 2621464
  18.6 0.9 %copy-done.1 = bf16[512,256]{1,0:T(8,128)(2,1)S(1)} copy-done((bf16[512,256]{1,0:T(8,128)(2,1)S(1)}, bf16[512,256]{1,0:T(8,128)(2,1)}, u32[]{:S(2)}) %copy-start.1) | copy-done | bytes 262168
  19.6 0.7 %copy-done.5 = s32[2,10]{1,0:T(2,128)S(1)} copy-done((s32[2,10]{1,0:T(2,128)S(1)}, s32[2,10]{1,0:T(2,128)}, u32[]{:S(2)}) %copy-start.5) | copy-done | bytes 104
  20.3 1.5 %shard_map.104.near_ref = f32[512,256]{1,0:T(8,128)S(1)} custom-call(s32[2,10]{1,0:T(2,128)S(1)} %copy-done.5, bf16[2,10,256,256]{3,2,1,0:T(8,128)(2,1)S(1)} %copy-done, bf16[512,256]{1,0:T(8,128)(2,1)S(1)} %copy-done.1, bf16[512,256]{1,0:T(8,128)(2,1)S(1)} %collective-permute-done.swap_ref, bf16[512,256]{1,0:T(8,128)(2,1)S(1)} %collective-permute-done.7.cross_ref), custom_call_target="tpu_custom_call" | custom-call | flops 671088640 | bytes 3932160 | tf_op jit(solution)/shard_map/pallas_call | solution.py:374
  21.8 0.6 %shard_map.105 = (f32[1,128,256]{2,1,0:T(8,128)S(1)}, bf16[1,128,256]{2,1,0:T(8,128)(2,1)S(1)}, bf16[1,128,256]{2,1,0:T(8,128)(2,1)S(1)}, bf16[1,128,256]{2,1,0:T(8,128)(2,1)S(1)}) custom-call(bf16[1,136,256]{2,1,0:T(8,128)(2,1)S(1)} %copy-done.2, bf16[1,136,256]{2,1,0:T(8,128)(2,1)S(1)} %collective-permute-done.1.refs_1_, ...), custom_call_target="tpu_custom_call" | custom-call | tf_op jit(solution)/shard_map/pallas_call | solution.py:392
  22.4 0.2 collective-permute-start.8
  22.6 1.6 %collective-permute-start.9 = (bf16[1,128,256]{2,1,0:T(8,128)(2,1)S(1)}, bf16[1,128,256]{2,1,0:T(8,128)(2,1)S(1)}, u32[]{:S(2)}, u32[]{:S(2)}) collective-permute-start(bf16[1,128,256]{2,1,0:T(8,128)(2,1)S(1)} %get-tuple-element.43), channel_id=1, source_target_pairs={{0,4},{1,5},{2,6},{3,7},{4,0},{5,1},{6,2},{7,3},{8,12},{9,13},{10,... | collective-permute-start | bytes 196616 | tf_op jit(solution)/shard_map/ppermute | solution.py:31
  24.1 1.8 %collective-permute-start.10 = (bf16[1,128,256]{2,1,0:T(8,128)(2,1)S(1)}, bf16[1,128,256]{2,1,0:T(8,128)(2,1)S(1)}, u32[]{:S(2)}, u32[]{:S(2)}) collective-permute-start(bf16[1,128,256]{2,1,0:T(8,128)(2,1)S(1)} %get-tuple-element.44), channel_id=1, source_target_pairs={{0,6},{1,7},{2,4},{3,5},{4,2},{5,3},{6,0},{7,1},{8,14},{9,15},{10,... | collective-permute-start | bytes 196616 | tf_op jit(solution)/shard_map/ppermute | solution.py:31
  25.9 1.5 %collective-permute-done.8.refs_0_ = bf16[1,128,256]{2,1,0:T(8,128)(2,1)S(1)} collective-permute-done((bf16[1,128,256]{2,1,0:T(8,128)(2,1)S(1)}, bf16[1,128,256]{2,1,0:T(8,128)(2,1)S(1)}, u32[]{:S(2)}, u32[]{:S(2)}) %collective-permute-start.8) | collective-permute-done | bytes 65568 | tf_op jit(solution)/shard_map/ppermute | solution.py:31
  27.4 0.1 collective-permute-done.9.refs_1_
  27.5 1.8 %collective-permute-done.10.refs_2_ = bf16[1,128,256]{2,1,0:T(8,128)(2,1)S(1)} collective-permute-done((bf16[1,128,256]{2,1,0:T(8,128)(2,1)S(1)}, bf16[1,128,256]{2,1,0:T(8,128)(2,1)S(1)}, u32[]{:S(2)}, u32[]{:S(2)}) %collective-permute-start.10) | collective-permute-done | bytes 65568 | tf_op jit(solution)/shard_map/ppermute | solution.py:31
  29.3 1.0 %shard_map.106 = (bf16[512,256]{1,0:T(8,128)(2,1)}, f32[320,128]{1,0:T(8,128)S(1)}) custom-call(bf16[2,64,256]{2,1,0:T(8,128)(2,1)S(1)} %copy-done.4, f32[512,256]{1,0:T(8,128)S(1)} %shard_map.104.near_ref, f32[1,128,256]{2,1,0:T(8,128)S(1)} %get-tuple-element.41.own_ref, bf16[1,128,256]{2,1,0:T(8,128)(2,1)S(1)} %collective-permute-done.8.refs_0_, ...), custom_call_target="tpu_custom_call" | custom-call | tf_op jit(solution)/shard_map/pallas_call | solution.py:402
  30.3 1.4 %collective-permute-done.11 = f32[320,128]{1,0:T(8,128)S(1)} collective-permute-done((f32[320,128]{1,0:T(8,128)S(1)}, f32[320,128]{1,0:T(8,128)S(1)}, u32[]{:S(2)}, u32[]{:S(2)}) %collective-permute-start.11) | collective-permute-done | bytes 163872 | tf_op jit(solution)/shard_map/ppermute | solution.py:35
  31.7 0.7 %collective-permute-start.15 = (bf16[320,128]{1,0:T(8,128)(2,1)S(1)}, bf16[320,128]{1,0:T(8,128)(2,1)S(1)}, u32[]{:S(2)}, u32[]{:S(2)}) collective-permute-start(bf16[320,128]{1,0:T(8,128)(2,1)S(1)} %get-tuple-element.49), channel_id=1, source_target_pairs={{1,15},{3,13},{5,11},{7,9},{9,7},{11,5},{13,3},{15,1},{17,31},{19,... | collective-permute-start | bytes 245768 | tf_op jit(solution)/shard_map/ppermute | solution.py:31
  32.4 1.8 %collective-permute-start.14 = (bf16[320,128]{1,0:T(8,128)(2,1)S(1)}, bf16[320,128]{1,0:T(8,128)(2,1)S(1)}, u32[]{:S(2)}, u32[]{:S(2)}) collective-permute-start(bf16[320,128]{1,0:T(8,128)(2,1)S(1)} %get-tuple-element.49), channel_id=1, source_target_pairs={{0,6},{1,11},{2,4},{3,9},{4,2},{5,15},{6,0},{7,13},{8,14},{9,3},{1... | collective-permute-start | bytes 245768 | tf_op jit(solution)/shard_map/ppermute | solution.py:31
  34.2 0.8 %collective-permute-start.13 = (bf16[320,128]{1,0:T(8,128)(2,1)S(1)}, bf16[320,128]{1,0:T(8,128)(2,1)S(1)}, u32[]{:S(2)}, u32[]{:S(2)}) collective-permute-start(bf16[320,128]{1,0:T(8,128)(2,1)S(1)} %get-tuple-element.49), channel_id=1, source_target_pairs={{0,4},{1,13},{2,6},{3,15},{4,0},{5,9},{6,2},{7,11},{8,12},{9,5},{1... | collective-permute-start | bytes 245768 | tf_op jit(solution)/shard_map/ppermute | solution.py:31
  35.1 0.9 %collective-permute-start.12 = (bf16[320,128]{1,0:T(8,128)(2,1)S(1)}, bf16[320,128]{1,0:T(8,128)(2,1)S(1)}, u32[]{:S(2)}, u32[]{:S(2)}) collective-permute-start(bf16[320,128]{1,0:T(8,128)(2,1)S(1)} %get-tuple-element.49), channel_id=1, source_target_pairs={{0,2},{1,9},{2,0},{3,11},{4,6},{5,13},{6,4},{7,15},{8,10},{9,1},{1... | collective-permute-start | bytes 245768 | tf_op jit(solution)/shard_map/ppermute | solution.py:31
  36.0 1.8 %collective-permute-done.14 = bf16[320,128]{1,0:T(8,128)(2,1)S(1)} collective-permute-done((bf16[320,128]{1,0:T(8,128)(2,1)S(1)}, bf16[320,128]{1,0:T(8,128)(2,1)S(1)}, u32[]{:S(2)}, u32[]{:S(2)}) %collective-permute-start.14) | collective-permute-done | bytes 81952 | tf_op jit(solution)/shard_map/ppermute | solution.py:31
  37.8 1.8 %collective-permute-done.13 = bf16[320,128]{1,0:T(8,128)(2,1)S(1)} collective-permute-done((bf16[320,128]{1,0:T(8,128)(2,1)S(1)}, bf16[320,128]{1,0:T(8,128)(2,1)S(1)}, u32[]{:S(2)}, u32[]{:S(2)}) %collective-permute-start.13) | collective-permute-done | bytes 81952 | tf_op jit(solution)/shard_map/ppermute | solution.py:31
  39.6 0.1 fusion.3
  39.7 2.4 %collective-permute-start.16 = (f32[2,320,128]{2,1,0:T(8,128)S(1)}, f32[2,320,128]{2,1,0:T(8,128)S(1)}, u32[]{:S(2)}, u32[]{:S(2)}) collective-permute-start(f32[2,320,128]{2,1,0:T(8,128)S(1)} %pad_maximum_fusion.mine_ref), channel_id=1, source_target_pairs={{0,1},{1,0},{2,3},{3,2},{4,5},{5,4},{6,7},{7,6},{8,9},{9,8},{10,11... | collective-permute-start | bytes 983048 | tf_op jit(solution)/shard_map/ppermute | solution.py:35
  42.1 1.3 %collective-permute-done.16.other_ref = f32[2,320,128]{2,1,0:T(8,128)S(1)} collective-permute-done((f32[2,320,128]{2,1,0:T(8,128)S(1)}, f32[2,320,128]{2,1,0:T(8,128)S(1)}, u32[]{:S(2)}, u32[]{:S(2)}) %collective-permute-start.16) | collective-permute-done | bytes 327712 | tf_op jit(solution)/shard_map/ppermute | solution.py:35
  43.3 10.1 %shard_map.107 = (f32[256,256]{1,0:T(8,128)}, bf16[3,256,256]{2,1,0:T(8,128)(2,1)}) custom-call(f32[320,128]{1,0:T(8,128)S(1)} %get-tuple-element.50.seg_ref, f32[2,320,128]{2,1,0:T(8,128)S(1)} %pad_maximum_fusion.mine_ref, f32[2,320,128]{2,1,0:T(8,128)S(1)} %collective-permute-done.16.other_ref), custom_call_target="tpu_custom_call" | custom-call | tf_op jit(solution)/shard_map/pallas_call | solution.py:310
  (22 shorter events, 0.1 us)
Async XLA Ops:
  0.6 1.9 %collective-permute-start = (bf16[512,256]{1,0:T(8,128)(2,1)}, bf16[512,256]{1,0:T(8,128)(2,1)S(1)}, u32[]{:S(2)}, u32[]{:S(2)}) collective-permute-start(bf16[512,256]{1,0:T(8,128)(2,1)} %own_hbm.1), channel_id=1, source_target_pairs={{0,1},{1,0},{2,3},{3,2},{4,5},{5,4},{6,7},{7,6},{8,9},{9,8},{10,11... | collective-permute-start | bytes 786440 | tf_op jit(solution)/shard_map/ppermute | solution.py:337
  1.1 12.4 %collective-permute-start.7 = (bf16[512,256]{1,0:T(8,128)(2,1)}, bf16[512,256]{1,0:T(8,128)(2,1)S(1)}, u32[]{:S(2)}, u32[]{:S(2)}) collective-permute-start(bf16[512,256]{1,0:T(8,128)(2,1)} %own_hbm.1), channel_id=1, source_target_pairs={{1,2},{3,4},{5,6},{7,8},{9,10},{11,12},{13,14},{15,16},{17,18},{19... | collective-permute-start | bytes 786440 | tf_op jit(solution)/shard_map/ppermute | solution.py:339
  5.2 10.0 %collective-permute-start.4 = (bf16[1,264,128]{2,1,0:T(8,128)(2,1)}, bf16[1,264,128]{2,1,0:T(8,128)(2,1)S(1)}, u32[]{:S(2)}, u32[]{:S(2)}) collective-permute-start(bf16[1,264,128]{2,1,0:T(8,128)(2,1)} %get-tuple-element.29), channel_id=1, source_target_pairs={{0,2},{1,3},{2,0},{3,1},{4,6},{5,7},{6,4},{7,5},{8,10},{9,11},{10,... | collective-permute-start | bytes 202760 | tf_op jit(solution)/shard_map/ppermute | solution.py:31
  8.3 13.4 %collective-permute-start.3 = (bf16[1,136,256]{2,1,0:T(8,128)(2,1)}, bf16[1,136,256]{2,1,0:T(8,128)(2,1)S(1)}, u32[]{:S(2)}, u32[]{:S(2)}) collective-permute-start(bf16[1,136,256]{2,1,0:T(8,128)(2,1)} %get-tuple-element.28.refs_0_), channel_id=1, source_target_pairs={{0,24},{1,25},{2,26},{3,27},{4,28},{5,29},{6,30},{7,31},{8,16},{9,... | collective-permute-start | bytes 208904 | tf_op jit(solution)/shard_map/ppermute | solution.py:31
  12.9 8.9 %collective-permute-start.2 = (bf16[1,136,256]{2,1,0:T(8,128)(2,1)}, bf16[1,136,256]{2,1,0:T(8,128)(2,1)S(1)}, u32[]{:S(2)}, u32[]{:S(2)}) collective-permute-start(bf16[1,136,256]{2,1,0:T(8,128)(2,1)} %get-tuple-element.28.refs_0_), channel_id=1, source_target_pairs={{0,16},{1,17},{2,18},{3,19},{4,20},{5,21},{6,22},{7,23},{8,24},{9,... | collective-permute-start | bytes 208904 | tf_op jit(solution)/shard_map/ppermute | solution.py:31
  12.9 8.9 %collective-permute-start.1 = (bf16[1,136,256]{2,1,0:T(8,128)(2,1)}, bf16[1,136,256]{2,1,0:T(8,128)(2,1)S(1)}, u32[]{:S(2)}, u32[]{:S(2)}) collective-permute-start(bf16[1,136,256]{2,1,0:T(8,128)(2,1)} %get-tuple-element.28.refs_0_), channel_id=1, source_target_pairs={{0,8},{1,9},{2,10},{3,11},{4,12},{5,13},{6,14},{7,15},{8,0},{9,1},... | collective-permute-start | bytes 208904 | tf_op jit(solution)/shard_map/ppermute | solution.py:31
  13.5 8.2 %collective-permute-start.5 = (bf16[1,264,128]{2,1,0:T(8,128)(2,1)}, bf16[1,264,128]{2,1,0:T(8,128)(2,1)S(1)}, u32[]{:S(2)}, u32[]{:S(2)}) collective-permute-start(bf16[1,264,128]{2,1,0:T(8,128)(2,1)} %get-tuple-element.30), channel_id=1, source_target_pairs={{0,4},{1,5},{2,6},{3,7},{4,0},{5,1},{6,2},{7,3},{8,12},{9,13},{10,... | collective-permute-start | bytes 202760 | tf_op jit(solution)/shard_map/ppermute | solution.py:31
  15.1 6.6 %collective-permute-start.6 = (bf16[1,264,128]{2,1,0:T(8,128)(2,1)}, bf16[1,264,128]{2,1,0:T(8,128)(2,1)S(1)}, u32[]{:S(2)}, u32[]{:S(2)}) collective-permute-start(bf16[1,264,128]{2,1,0:T(8,128)(2,1)} %get-tuple-element.31), channel_id=1, source_target_pairs={{0,6},{1,7},{2,4},{3,5},{4,2},{5,3},{6,0},{7,1},{8,14},{9,15},{10,... | collective-permute-start | bytes 202760 | tf_op jit(solution)/shard_map/ppermute | solution.py:31
  16.9 1.7 %copy-start = (bf16[2,10,256,256]{3,2,1,0:T(8,128)(2,1)S(1)}, bf16[2,10,256,256]{3,2,1,0:T(8,128)(2,1)}, u32[]{:S(2)}) copy-start(bf16[2,10,256,256]{3,2,1,0:T(8,128)(2,1)} %blocks_ref.1) | copy-start | bytes 7864324
  18.6 0.9 %copy-start.1 = (bf16[512,256]{1,0:T(8,128)(2,1)S(1)}, bf16[512,256]{1,0:T(8,128)(2,1)}, u32[]{:S(2)}) copy-start(bf16[512,256]{1,0:T(8,128)(2,1)} %own_hbm.1) | copy-start | bytes 786436
  19.6 0.7 %copy-start.5 = (s32[2,10]{1,0:T(2,128)S(1)}, s32[2,10]{1,0:T(2,128)}, u32[]{:S(2)}) copy-start(s32[2,10]{1,0:T(2,128)} %list_hbm.1) | copy-start | bytes 244
  20.3 1.5 %copy-start.2 = (bf16[1,136,256]{2,1,0:T(8,128)(2,1)S(1)}, bf16[1,136,256]{2,1,0:T(8,128)(2,1)}, u32[]{:S(2)}) copy-start(bf16[1,136,256]{2,1,0:T(8,128)(2,1)} %get-tuple-element.28.refs_0_) | copy-start | bytes 208900
  20.3 1.5 %copy-start.3 = (bf16[1,264,128]{2,1,0:T(8,128)(2,1)S(1)}, bf16[1,264,128]{2,1,0:T(8,128)(2,1)}, u32[]{:S(2)}) copy-start(bf16[1,264,128]{2,1,0:T(8,128)(2,1)} %get-tuple-element.37.refs_4_) | copy-start | bytes 202756
  20.3 9.1 %copy-start.4 = (bf16[2,64,256]{2,1,0:T(8,128)(2,1)S(1)}, bf16[2,64,256]{2,1,0:T(8,128)(2,1)}, u32[]{:S(2)}) copy-start(bf16[2,64,256]{2,1,0:T(8,128)(2,1)} %get-tuple-element.27.basis_ref) | copy-start | bytes 196612
  22.4 5.0 %collective-permute-start.8 = (bf16[1,128,256]{2,1,0:T(8,128)(2,1)S(1)}, bf16[1,128,256]{2,1,0:T(8,128)(2,1)S(1)}, u32[]{:S(2)}, u32[]{:S(2)}) collective-permute-start(bf16[1,128,256]{2,1,0:T(8,128)(2,1)S(1)} %get-tuple-element.42), channel_id=1, source_target_pairs={{0,2},{1,3},{2,0},{3,1},{4,6},{5,7},{6,4},{7,5},{8,10},{9,11},{10,... | collective-permute-start | bytes 196616 | tf_op jit(solution)/shard_map/ppermute | solution.py:31
  22.6 4.9 %collective-permute-start.9 = (bf16[1,128,256]{2,1,0:T(8,128)(2,1)S(1)}, bf16[1,128,256]{2,1,0:T(8,128)(2,1)S(1)}, u32[]{:S(2)}, u32[]{:S(2)}) collective-permute-start(bf16[1,128,256]{2,1,0:T(8,128)(2,1)S(1)} %get-tuple-element.43), channel_id=1, source_target_pairs={{0,4},{1,5},{2,6},{3,7},{4,0},{5,1},{6,2},{7,3},{8,12},{9,13},{10,... | collective-permute-start | bytes 196616 | tf_op jit(solution)/shard_map/ppermute | solution.py:31
  24.1 5.2 %collective-permute-start.10 = (bf16[1,128,256]{2,1,0:T(8,128)(2,1)S(1)}, bf16[1,128,256]{2,1,0:T(8,128)(2,1)S(1)}, u32[]{:S(2)}, u32[]{:S(2)}) collective-permute-start(bf16[1,128,256]{2,1,0:T(8,128)(2,1)S(1)} %get-tuple-element.44), channel_id=1, source_target_pairs={{0,6},{1,7},{2,4},{3,5},{4,2},{5,3},{6,0},{7,1},{8,14},{9,15},{10,... | collective-permute-start | bytes 196616 | tf_op jit(solution)/shard_map/ppermute | solution.py:31
  30.3 1.4 %collective-permute-start.11 = (f32[320,128]{1,0:T(8,128)S(1)}, f32[320,128]{1,0:T(8,128)S(1)}, u32[]{:S(2)}, u32[]{:S(2)}) collective-permute-start(f32[320,128]{1,0:T(8,128)S(1)} %get-tuple-element.46), channel_id=1, source_target_pairs={{0,1},{1,0},{2,3},{3,2},{4,5},{5,4},{6,7},{7,6},{8,9},{9,8},{10,11... | collective-permute-start | bytes 491528 | tf_op jit(solution)/shard_map/ppermute | solution.py:35
  31.7 4.2 %collective-permute-start.15 = (bf16[320,128]{1,0:T(8,128)(2,1)S(1)}, bf16[320,128]{1,0:T(8,128)(2,1)S(1)}, u32[]{:S(2)}, u32[]{:S(2)}) collective-permute-start(bf16[320,128]{1,0:T(8,128)(2,1)S(1)} %get-tuple-element.49), channel_id=1, source_target_pairs={{1,15},{3,13},{5,11},{7,9},{9,7},{11,5},{13,3},{15,1},{17,31},{19,... | collective-permute-start | bytes 245768 | tf_op jit(solution)/shard_map/ppermute | solution.py:31
  32.4 5.4 %collective-permute-start.14 = (bf16[320,128]{1,0:T(8,128)(2,1)S(1)}, bf16[320,128]{1,0:T(8,128)(2,1)S(1)}, u32[]{:S(2)}, u32[]{:S(2)}) collective-permute-start(bf16[320,128]{1,0:T(8,128)(2,1)S(1)} %get-tuple-element.49), channel_id=1, source_target_pairs={{0,6},{1,11},{2,4},{3,9},{4,2},{5,15},{6,0},{7,13},{8,14},{9,3},{1... | collective-permute-start | bytes 245768 | tf_op jit(solution)/shard_map/ppermute | solution.py:31
  34.2 5.3 %collective-permute-start.13 = (bf16[320,128]{1,0:T(8,128)(2,1)S(1)}, bf16[320,128]{1,0:T(8,128)(2,1)S(1)}, u32[]{:S(2)}, u32[]{:S(2)}) collective-permute-start(bf16[320,128]{1,0:T(8,128)(2,1)S(1)} %get-tuple-element.49), channel_id=1, source_target_pairs={{0,4},{1,13},{2,6},{3,15},{4,0},{5,9},{6,2},{7,11},{8,12},{9,5},{1... | collective-permute-start | bytes 245768 | tf_op jit(solution)/shard_map/ppermute | solution.py:31
  35.1 4.5 %collective-permute-start.12 = (bf16[320,128]{1,0:T(8,128)(2,1)S(1)}, bf16[320,128]{1,0:T(8,128)(2,1)S(1)}, u32[]{:S(2)}, u32[]{:S(2)}) collective-permute-start(bf16[320,128]{1,0:T(8,128)(2,1)S(1)} %get-tuple-element.49), channel_id=1, source_target_pairs={{0,2},{1,9},{2,0},{3,11},{4,6},{5,13},{6,4},{7,15},{8,10},{9,1},{1... | collective-permute-start | bytes 245768 | tf_op jit(solution)/shard_map/ppermute | solution.py:31
  39.7 3.7 %collective-permute-start.16 = (f32[2,320,128]{2,1,0:T(8,128)S(1)}, f32[2,320,128]{2,1,0:T(8,128)S(1)}, u32[]{:S(2)}, u32[]{:S(2)}) collective-permute-start(f32[2,320,128]{2,1,0:T(8,128)S(1)} %pad_maximum_fusion.mine_ref), channel_id=1, source_target_pairs={{0,1},{1,0},{2,3},{3,2},{4,5},{5,4},{6,7},{7,6},{8,9},{9,8},{10,11... | collective-permute-start | bytes 983048 | tf_op jit(solution)/shard_map/ppermute | solution.py:35

commit v5 on v4

--- a/solution.py
+++ b/solution.py
@@ -190,32 +190,58 @@
 def mmt(a,b):
     ah,al=split(a); bh,bl=split(b)
     return dg(jnp.concatenate([ah,al,ah],1),jnp.concatenate([bh,bh,bl],1),((1,),(1,)))
-def eliminate(P, lane, row, tick):
+def eliminate(P, Q, lane, row, tick):
     base=lane & ~31
     sub=lane & 31
     V=[jnp.where(row+8*rv==sub,1.0,0.0).astype(jnp.float32) for rv in range(4)]
     P=list(P)
-    for m in range(4):
-        C=[[jnp.take_along_axis(P[rv],base+(8*m+k),axis=1,mode="promise_in_bounds") for rv in range(m,4)] for k in range(8)]
-        piv=jnp.ones((8,128),jnp.float32)
+    late=[]
+    def follow(r,Ms,rs):
         for k in range(8):
-            d=rb(C[k][0],k)
-            piv=jnp.where(row==k,d,piv)
-            inv=1.0/d
-            M=[c*inv for c in C[k]]
-            M[0]=jnp.where(row>k,M[0],0.0)
-            for k2 in range(k+1,8):
-                f=rb(C[k2][0],k)
-                C[k2]=[c-mu*f for c,mu in zip(C[k2],M)]
-            fp=rb(P[m],k); fv=rb(V[m],k)
-            for rv in range(m,4):
-                P[rv]=P[rv]-M[rv-m]*fp
-                V[rv]=V[rv]-M[rv-m]*fv
-            tick(8*m+k)
-        rs=lax.rsqrt(piv)
-        P[m]=P[m]*rs
-        V[m]=V[m]*rs
-    return P,V
+            fq=rb(Q[r],k)
+            for rv in range(r,4):
+                Q[rv]=Q[rv]-Ms[k][rv]*fq
+        Q[r]=Q[r]*rs
+    W=16//8
+    for mb in range(32//16):
+        base_r=mb*W
+        C=[{rv:jnp.take_along_axis(P[rv],base+(16*mb+k),axis=1,mode="promise_in_bounds") for rv in range(base_r,4)} for k in range(16)]
+        for w in range(W):
+            r=base_r+w
+            piv=jnp.ones((8,128),jnp.float32)
+            Ms=[]
+            for kk in range(8):
+                k=8*w+kk
+                d=rb(C[k][r],kk)
+                piv=jnp.where(row==kk,d,piv)
+                inv=1.0/d
+                nxt=None
+                if k+1<16:
+                    r1=base_r+(k+1)//8
+                    f1=rb(C[k+1][r],kk)
+                    t1=C[k][r1]*f1
+                    if r1==r: t1=jnp.where(row>kk,t1,0.0)
+                    nxt=C[k+1][r1]-t1*inv
+                M={rv:C[k][rv]*inv for rv in range(r,4)}
+                M[r]=jnp.where(row>kk,M[r],0.0)
+                Ms.append(M)
+                for k2 in range(k+1,16):
+                    f=rb(C[k2][r],kk)
+                    for rv in range(r,4):
+                        if rv>=base_r+k2//8 or True: C[k2][rv]=C[k2][rv]-M[rv]*f
+                if nxt is not None: C[k+1][r1]=nxt
+                fp=rb(P[r],kk); fv=rb(V[r],kk)
+                for rv in range(r,4):
+                    P[rv]=P[rv]-M[rv]*fp
+                    V[rv]=V[rv]-M[rv]*fv
+                tick(8*r+kk)
+            rs=lax.rsqrt(piv)
+            P[r]=P[r]*rs
+            V[r]=V[r]*rs
+            late.append((r,Ms,rs))
+            if Q is not None and r>=1: follow(*late[r-1])
+    if Q is not None: follow(*late[3])
+    return P,V,Q
 
 def factor_kernel(seg_ref, mine_ref, other_ref, r_ref, tr_ref, X, Rb, Wb):
     lane=lax.broadcasted_iota(jnp.int32,(8,128),1); row=lax.broadcasted_iota(jnp.int32,(8,128),0)
@@ -255,19 +281,21 @@
             v=rows_of(t)
             out.append(pltpu.roll(v,sh,1) if sh else v)
         return out
-    def packed(block, kb_cols):
-        off=32*kb_cols; c0=off//128*128; lo=off%128
-        vs=place(lambda t:X[block,32*t:32*t+32,c0:c0+128],block,lo)
+    grp32=lax.broadcasted_iota(jnp.int32,(32,128),1)//32
+    state={}
+    def placed(block, cb):
+        off=32*cb; c0=off//128*128
+        return place(lambda t:X[block,32*t:32*t+32,c0:c0+128],block,off%128)
+    def pick(vs):
         acc=vs[0]
         for t in range(1,4): acc=jnp.where(grp32==t,vs[t],acc)
         return acc
-    grp32=lax.broadcasted_iota(jnp.int32,(32,128),1)//32
-    state={}
     def prep(kb):
-        off=32*(kb+1); c0=off//128*128; lo=off%128
-        q=jnp.concatenate(place(lambda t:X[kb,32*t:32*t+32,c0:c0+128],kb,lo),0)
-        state['q']=rstack(jnp.where(bd,q,0.0))
-        state['d']=packed(kb+1,kb+1)
+        state['d']=pick(placed(kb+1,kb+1))
+        if kb+2<8:
+            state['q2']=rstack(jnp.where(bd,jnp.concatenate(placed(kb,kb+2),0),0.0))
+            state['qpre']=pick(placed(kb+1,kb+2))
+    def rows(x): return [x[8*r:8*r+8,:] for r in range(4)]
     def make_panel(kb,Vf):
         off=32*kb
         Wbd=jnp.where(bd,jnp.concatenate([Vf]*4,0),0.0)
@@ -282,20 +310,21 @@
         T=state['ch'][c][(i%4)*32:(i%4)*32+32,:]
         update(i,lstack(jnp.where(bd,jnp.concatenate([T]*4,0),0.0)),state['ps'],off)
     def emit_out(kb,Pf): emit(kb,state['panel'],Pf)
-    p32=packed(0,0)
+    p32=pick(placed(0,0)); q32=pick(placed(0,1))
     for kb in range(8):
         if kb==0: pending.append(functools.partial(prep,0))
-        P=[p32[8*r:8*r+8,:] for r in range(4)]
-        P,V=eliminate(P,lane,row,tick)
+        P,V,Q=eliminate(rows(p32),rows(q32) if kb<7 else None,lane,row,tick)
         while pending: pending.pop(0)()
         Pf=jnp.concatenate(P,0); Vf=jnp.concatenate(V,0)
         if kb<7:
-            rn=mms(lstack(Vf),state['q'])
-            h,l=split(rn)
-            G=dg(jnp.concatenate([h,h,l],0),jnp.concatenate([h,l,h],0),((0,),(0,)))
-            g=G[0:32,:]
-            for t in range(1,4): g=jnp.where(grp32==t,G[32*t:32*t+32,:],g)
-            p32=state['d']-g
+            h,l=split(jnp.concatenate(Q,0))
+            left=jnp.concatenate([h,h,l],0)
+            G=dg(left,jnp.concatenate([h,l,h],0),((0,),(0,)))
+            p32=state['d']-pick([G[32*t:32*t+32,:] for t in range(4)])
+            if kb+2<8:
+                h2,l2=split(mms(lstack(Vf),state['q2']))
+                G2=dg(left,jnp.concatenate([h2,l2,h2],0),((0,),(0,)))
+                q32=state['qpre']-pick([G2[32*t:32*t+32,:] for t in range(4)])
         pending.append(functools.partial(make_panel,kb,Vf))
         for i in range(kb+1,8):
             pending.append(functools.partial(go,i,32*kb))

time: 53.7 us -> 51.7 us (0.963)
  Pallas kernels: 15.8 us -> 13.8 us
    pallas_call x1, Pallas kernels: 10.1 us -> 8.14 us  [factor_all(): pl.pallas_call(factor_kernel, out_shape=(jax.ShapeDtypeStruct((256, 256),...]
where the time goes in v5:
time: 51.7 us; the launch traced here: 51.5 us
  starting transfers between devices  23.1 us (45%)
  Pallas kernels  13.8 us (27%)
  waiting for transfers between devices  10.4 us (20%)
  local copies, waits for them, and re-layouts  3.38 us (7%)
  between operations  0.76 us (1%)
    ppermute x13, starting transfers between devices, hop(): return lax.ppermute(value, AXES, pairs)  19.5 us
    pallas_call x1, Pallas kernels, factor_all(): pl.pallas_call(factor_kernel, out_shape=(jax.ShapeDtypeStruct((256, 256),...  8.14 us
    ppermute x13, waiting for transfers between devices, hop(): return lax.ppermute(value, AXES, pairs)  7.03 us
    unnamed x12, local copies, waits for them, and re-layouts  3.38 us
    ppermute x2, waiting for transfers between devices, sub_hop(): lax.ppermute(value, 'sub', [(i, i ^ mask) for i in range(lax.axis_size('s...  2.65 us
    pallas_call x1, Pallas kernels, body(): pl.pallas_call(first_kernel, out_shape=[jax.ShapeDtypeStruct((1, leaf_cou...  2.63 us
    ppermute x2, starting transfers between devices, sub_hop(): lax.ppermute(value, 'sub', [(i, i ^ mask) for i in range(lax.axis_size('s...  2.42 us
    pallas_call x1, Pallas kernels, body(): pl.pallas_call(near_kernel, out_shape=jax.ShapeDtypeStruct((rows, width),...  1.45 us
  transfers between devices with their start and end apart: 17, of which 8 were waited for; matrix products, arithmetic and copies ran while one was open for 0% of the time, Pallas kernels for 8%

profile of v5, /device:TPU:0, one launch (start us, length us, event | category | flops | bytes accessed | tf_op | source)
XLA Modules:
  0.0 51.5 jit_solution(15021704096096759624)
XLA Ops:
  0.6 0.5 %collective-permute-start = (bf16[512,256]{1,0:T(8,128)(2,1)}, bf16[512,256]{1,0:T(8,128)(2,1)S(1)}, u32[]{:S(2)}, u32[]{:S(2)}) collective-permute-start(bf16[512,256]{1,0:T(8,128)(2,1)} %own_hbm.1), channel_id=1, source_target_pairs={{0,1},{1,0},{2,3},{3,2},{4,5},{5,4},{6,7},{7,6},{8,9},{9,8},{10,11... | collective-permute-start | bytes 786440 | tf_op jit(solution)/shard_map/ppermute | solution.py:366
  1.1 0.7 %collective-permute-start.7 = (bf16[512,256]{1,0:T(8,128)(2,1)}, bf16[512,256]{1,0:T(8,128)(2,1)S(1)}, u32[]{:S(2)}, u32[]{:S(2)}) collective-permute-start(bf16[512,256]{1,0:T(8,128)(2,1)} %own_hbm.1), channel_id=1, source_target_pairs={{1,2},{3,4},{5,6},{7,8},{9,10},{11,12},{13,14},{15,16},{17,18},{19... | collective-permute-start | bytes 786440 | tf_op jit(solution)/shard_map/ppermute | solution.py:368
  1.8 0.7 %collective-permute-done.swap_ref = bf16[512,256]{1,0:T(8,128)(2,1)S(1)} collective-permute-done((bf16[512,256]{1,0:T(8,128)(2,1)}, bf16[512,256]{1,0:T(8,128)(2,1)S(1)}, u32[]{:S(2)}, u32[]{:S(2)}) %collective-permute-start) | collective-permute-done | bytes 262176 | tf_op jit(solution)/shard_map/ppermute | solution.py:366
  2.5 2.6 %shard_map.103 = (bf16[1,136,256]{2,1,0:T(8,128)(2,1)}, bf16[2,64,256]{2,1,0:T(8,128)(2,1)}, bf16[1,264,128]{2,1,0:T(8,128)(2,1)}, bf16[1,264,128]{2,1,0:T(8,128...) custom-call(bf16[2,64,256]{2,1,0:T(8,128)(2,1)} %basis_hbm, bf16[512,256]{1,0:T(8,128)(2,1)} %own_hbm.1, ...), custom_call_target="tpu_custom_call" | custom-call | tf_op jit(solution)/shard_map/pallas_call | solution.py:375
  5.2 3.1 %collective-permute-start.4 = (bf16[1,264,128]{2,1,0:T(8,128)(2,1)}, bf16[1,264,128]{2,1,0:T(8,128)(2,1)S(1)}, u32[]{:S(2)}, u32[]{:S(2)}) collective-permute-start(bf16[1,264,128]{2,1,0:T(8,128)(2,1)} %get-tuple-element.29), channel_id=1, source_target_pairs={{0,2},{1,3},{2,0},{3,1},{4,6},{5,7},{6,4},{7,5},{8,10},{9,11},{10,... | collective-permute-start | bytes 202760 | tf_op jit(solution)/shard_map/ppermute | solution.py:31
  8.3 4.6 %collective-permute-start.3 = (bf16[1,136,256]{2,1,0:T(8,128)(2,1)}, bf16[1,136,256]{2,1,0:T(8,128)(2,1)S(1)}, u32[]{:S(2)}, u32[]{:S(2)}) collective-permute-start(bf16[1,136,256]{2,1,0:T(8,128)(2,1)} %get-tuple-element.28.refs_0_), channel_id=1, source_target_pairs={{0,24},{1,25},{2,26},{3,27},{4,28},{5,29},{6,30},{7,31},{8,16},{9,... | collective-permute-start | bytes 208904 | tf_op jit(solution)/shard_map/ppermute | solution.py:31
  12.9 0.6 %collective-permute-start.1 = (bf16[1,136,256]{2,1,0:T(8,128)(2,1)}, bf16[1,136,256]{2,1,0:T(8,128)(2,1)S(1)}, u32[]{:S(2)}, u32[]{:S(2)}) collective-permute-start(bf16[1,136,256]{2,1,0:T(8,128)(2,1)} %get-tuple-element.28.refs_0_), channel_id=1, source_target_pairs={{0,8},{1,9},{2,10},{3,11},{4,12},{5,13},{6,14},{7,15},{8,0},{9,1},... | collective-permute-start | bytes 208904 | tf_op jit(solution)/shard_map/ppermute | solution.py:31
  13.5 1.6 %collective-permute-start.5 = (bf16[1,264,128]{2,1,0:T(8,128)(2,1)}, bf16[1,264,128]{2,1,0:T(8,128)(2,1)S(1)}, u32[]{:S(2)}, u32[]{:S(2)}) collective-permute-start(bf16[1,264,128]{2,1,0:T(8,128)(2,1)} %get-tuple-element.30), channel_id=1, source_target_pairs={{0,4},{1,5},{2,6},{3,7},{4,0},{5,1},{6,2},{7,3},{8,12},{9,13},{10,... | collective-permute-start | bytes 202760 | tf_op jit(solution)/shard_map/ppermute | solution.py:31
  15.1 1.8 %collective-permute-start.6 = (bf16[1,264,128]{2,1,0:T(8,128)(2,1)}, bf16[1,264,128]{2,1,0:T(8,128)(2,1)S(1)}, u32[]{:S(2)}, u32[]{:S(2)}) collective-permute-start(bf16[1,264,128]{2,1,0:T(8,128)(2,1)} %get-tuple-element.31), channel_id=1, source_target_pairs={{0,6},{1,7},{2,4},{3,5},{4,2},{5,3},{6,0},{7,1},{8,14},{9,15},{10,... | collective-permute-start | bytes 202760 | tf_op jit(solution)/shard_map/ppermute | solution.py:31
  16.9 1.7 %copy-done = bf16[2,10,256,256]{3,2,1,0:T(8,128)(2,1)S(1)} copy-done((bf16[2,10,256,256]{3,2,1,0:T(8,128)(2,1)S(1)}, bf16[2,10,256,256]{3,2,1,0:T(8,128)(2,1)}, u32[]{:S(2)}) %copy-start) | copy-done | bytes 2621464
  18.6 0.9 %copy-done.1 = bf16[512,256]{1,0:T(8,128)(2,1)S(1)} copy-done((bf16[512,256]{1,0:T(8,128)(2,1)S(1)}, bf16[512,256]{1,0:T(8,128)(2,1)}, u32[]{:S(2)}) %copy-start.1) | copy-done | bytes 262168
  19.6 0.7 %copy-done.5 = s32[2,10]{1,0:T(2,128)S(1)} copy-done((s32[2,10]{1,0:T(2,128)S(1)}, s32[2,10]{1,0:T(2,128)}, u32[]{:S(2)}) %copy-start.5) | copy-done | bytes 104
  20.3 1.5 %shard_map.104.near_ref = f32[512,256]{1,0:T(8,128)S(1)} custom-call(s32[2,10]{1,0:T(2,128)S(1)} %copy-done.5, bf16[2,10,256,256]{3,2,1,0:T(8,128)(2,1)S(1)} %copy-done, bf16[512,256]{1,0:T(8,128)(2,1)S(1)} %copy-done.1, bf16[512,256]{1,0:T(8,128)(2,1)S(1)} %collective-permute-done.swap_ref, bf16[512,256]{1,0:T(8,128)(2,1)S(1)} %collective-permute-done.7.cross_ref), custom_call_target="tpu_custom_call" | custom-call | flops 671088640 | bytes 3932160 | tf_op jit(solution)/shard_map/pallas_call | solution.py:403
  21.8 0.6 %shard_map.105 = (f32[1,128,256]{2,1,0:T(8,128)S(1)}, bf16[1,128,256]{2,1,0:T(8,128)(2,1)S(1)}, bf16[1,128,256]{2,1,0:T(8,128)(2,1)S(1)}, bf16[1,128,256]{2,1,0:T(8,128)(2,1)S(1)}) custom-call(bf16[1,136,256]{2,1,0:T(8,128)(2,1)S(1)} %copy-done.2, bf16[1,136,256]{2,1,0:T(8,128)(2,1)S(1)} %collective-permute-done.1.refs_1_, ...), custom_call_target="tpu_custom_call" | custom-call | tf_op jit(solution)/shard_map/pallas_call | solution.py:421
  22.4 0.2 collective-permute-start.8
  22.6 1.6 %collective-permute-start.9 = (bf16[1,128,256]{2,1,0:T(8,128)(2,1)S(1)}, bf16[1,128,256]{2,1,0:T(8,128)(2,1)S(1)}, u32[]{:S(2)}, u32[]{:S(2)}) collective-permute-start(bf16[1,128,256]{2,1,0:T(8,128)(2,1)S(1)} %get-tuple-element.43), channel_id=1, source_target_pairs={{0,4},{1,5},{2,6},{3,7},{4,0},{5,1},{6,2},{7,3},{8,12},{9,13},{10,... | collective-permute-start | bytes 196616 | tf_op jit(solution)/shard_map/ppermute | solution.py:31
  24.1 1.8 %collective-permute-start.10 = (bf16[1,128,256]{2,1,0:T(8,128)(2,1)S(1)}, bf16[1,128,256]{2,1,0:T(8,128)(2,1)S(1)}, u32[]{:S(2)}, u32[]{:S(2)}) collective-permute-start(bf16[1,128,256]{2,1,0:T(8,128)(2,1)S(1)} %get-tuple-element.44), channel_id=1, source_target_pairs={{0,6},{1,7},{2,4},{3,5},{4,2},{5,3},{6,0},{7,1},{8,14},{9,15},{10,... | collective-permute-start | bytes 196616 | tf_op jit(solution)/shard_map/ppermute | solution.py:31
  25.9 1.5 %collective-permute-done.8.refs_0_ = bf16[1,128,256]{2,1,0:T(8,128)(2,1)S(1)} collective-permute-done((bf16[1,128,256]{2,1,0:T(8,128)(2,1)S(1)}, bf16[1,128,256]{2,1,0:T(8,128)(2,1)S(1)}, u32[]{:S(2)}, u32[]{:S(2)}) %collective-permute-start.8) | collective-permute-done | bytes 65568 | tf_op jit(solution)/shard_map/ppermute | solution.py:31
  27.4 0.1 collective-permute-done.9.refs_1_
  27.5 1.8 %collective-permute-done.10.refs_2_ = bf16[1,128,256]{2,1,0:T(8,128)(2,1)S(1)} collective-permute-done((bf16[1,128,256]{2,1,0:T(8,128)(2,1)S(1)}, bf16[1,128,256]{2,1,0:T(8,128)(2,1)S(1)}, u32[]{:S(2)}, u32[]{:S(2)}) %collective-permute-start.10) | collective-permute-done | bytes 65568 | tf_op jit(solution)/shard_map/ppermute | solution.py:31
  29.3 1.0 %shard_map.106 = (bf16[512,256]{1,0:T(8,128)(2,1)}, f32[320,128]{1,0:T(8,128)S(1)}) custom-call(bf16[2,64,256]{2,1,0:T(8,128)(2,1)S(1)} %copy-done.4, f32[512,256]{1,0:T(8,128)S(1)} %shard_map.104.near_ref, f32[1,128,256]{2,1,0:T(8,128)S(1)} %get-tuple-element.41.own_ref, bf16[1,128,256]{2,1,0:T(8,128)(2,1)S(1)} %collective-permute-done.8.refs_0_, ...), custom_call_target="tpu_custom_call" | custom-call | tf_op jit(solution)/shard_map/pallas_call | solution.py:431
  30.3 1.4 %collective-permute-done.11 = f32[320,128]{1,0:T(8,128)S(1)} collective-permute-done((f32[320,128]{1,0:T(8,128)S(1)}, f32[320,128]{1,0:T(8,128)S(1)}, u32[]{:S(2)}, u32[]{:S(2)}) %collective-permute-start.11) | collective-permute-done | bytes 163872 | tf_op jit(solution)/shard_map/ppermute | solution.py:35
  31.7 0.7 %collective-permute-start.15 = (bf16[320,128]{1,0:T(8,128)(2,1)S(1)}, bf16[320,128]{1,0:T(8,128)(2,1)S(1)}, u32[]{:S(2)}, u32[]{:S(2)}) collective-permute-start(bf16[320,128]{1,0:T(8,128)(2,1)S(1)} %get-tuple-element.49), channel_id=1, source_target_pairs={{1,15},{3,13},{5,11},{7,9},{9,7},{11,5},{13,3},{15,1},{17,31},{19,... | collective-permute-start | bytes 245768 | tf_op jit(solution)/shard_map/ppermute | solution.py:31
  32.4 1.8 %collective-permute-start.14 = (bf16[320,128]{1,0:T(8,128)(2,1)S(1)}, bf16[320,128]{1,0:T(8,128)(2,1)S(1)}, u32[]{:S(2)}, u32[]{:S(2)}) collective-permute-start(bf16[320,128]{1,0:T(8,128)(2,1)S(1)} %get-tuple-element.49), channel_id=1, source_target_pairs={{0,6},{1,11},{2,4},{3,9},{4,2},{5,15},{6,0},{7,13},{8,14},{9,3},{1... | collective-permute-start | bytes 245768 | tf_op jit(solution)/shard_map/ppermute | solution.py:31
  34.2 0.8 %collective-permute-start.13 = (bf16[320,128]{1,0:T(8,128)(2,1)S(1)}, bf16[320,128]{1,0:T(8,128)(2,1)S(1)}, u32[]{:S(2)}, u32[]{:S(2)}) collective-permute-start(bf16[320,128]{1,0:T(8,128)(2,1)S(1)} %get-tuple-element.49), channel_id=1, source_target_pairs={{0,4},{1,13},{2,6},{3,15},{4,0},{5,9},{6,2},{7,11},{8,12},{9,5},{1... | collective-permute-start | bytes 245768 | tf_op jit(solution)/shard_map/ppermute | solution.py:31
  35.1 0.9 %collective-permute-start.12 = (bf16[320,128]{1,0:T(8,128)(2,1)S(1)}, bf16[320,128]{1,0:T(8,128)(2,1)S(1)}, u32[]{:S(2)}, u32[]{:S(2)}) collective-permute-start(bf16[320,128]{1,0:T(8,128)(2,1)S(1)} %get-tuple-element.49), channel_id=1, source_target_pairs={{0,2},{1,9},{2,0},{3,11},{4,6},{5,13},{6,4},{7,15},{8,10},{9,1},{1... | collective-permute-start | bytes 245768 | tf_op jit(solution)/shard_map/ppermute | solution.py:31
  36.0 1.8 %collective-permute-done.14 = bf16[320,128]{1,0:T(8,128)(2,1)S(1)} collective-permute-done((bf16[320,128]{1,0:T(8,128)(2,1)S(1)}, bf16[320,128]{1,0:T(8,128)(2,1)S(1)}, u32[]{:S(2)}, u32[]{:S(2)}) %collective-permute-start.14) | collective-permute-done | bytes 81952 | tf_op jit(solution)/shard_map/ppermute | solution.py:31
  37.8 1.8 %collective-permute-done.13 = bf16[320,128]{1,0:T(8,128)(2,1)S(1)} collective-permute-done((bf16[320,128]{1,0:T(8,128)(2,1)S(1)}, bf16[320,128]{1,0:T(8,128)(2,1)S(1)}, u32[]{:S(2)}, u32[]{:S(2)}) %collective-permute-start.13) | collective-permute-done | bytes 81952 | tf_op jit(solution)/shard_map/ppermute | solution.py:31
  39.6 0.1 fusion.3
  39.7 2.4 %collective-permute-start.16 = (f32[2,320,128]{2,1,0:T(8,128)S(1)}, f32[2,320,128]{2,1,0:T(8,128)S(1)}, u32[]{:S(2)}, u32[]{:S(2)}) collective-permute-start(f32[2,320,128]{2,1,0:T(8,128)S(1)} %pad_maximum_fusion.mine_ref), channel_id=1, source_target_pairs={{0,1},{1,0},{2,3},{3,2},{4,5},{5,4},{6,7},{7,6},{8,9},{9,8},{10,11... | collective-permute-start | bytes 983048 | tf_op jit(solution)/shard_map/ppermute | solution.py:35
  42.1 1.3 %collective-permute-done.16.other_ref = f32[2,320,128]{2,1,0:T(8,128)S(1)} collective-permute-done((f32[2,320,128]{2,1,0:T(8,128)S(1)}, f32[2,320,128]{2,1,0:T(8,128)S(1)}, u32[]{:S(2)}, u32[]{:S(2)}) %collective-permute-start.16) | collective-permute-done | bytes 327712 | tf_op jit(solution)/shard_map/ppermute | solution.py:35
  43.3 8.1 %shard_map.107 = (f32[256,256]{1,0:T(8,128)}, bf16[3,256,256]{2,1,0:T(8,128)(2,1)}) custom-call(f32[320,128]{1,0:T(8,128)S(1)} %get-tuple-element.50.seg_ref, f32[2,320,128]{2,1,0:T(8,128)S(1)} %pad_maximum_fusion.mine_ref, f32[2,320,128]{2,1,0:T(8,128)S(1)} %collective-permute-done.16.other_ref), custom_call_target="tpu_custom_call" | custom-call | tf_op jit(solution)/shard_map/pallas_call | solution.py:339
  (22 shorter events, 0.1 us)
Async XLA Ops:
  0.6 1.9 %collective-permute-start = (bf16[512,256]{1,0:T(8,128)(2,1)}, bf16[512,256]{1,0:T(8,128)(2,1)S(1)}, u32[]{:S(2)}, u32[]{:S(2)}) collective-permute-start(bf16[512,256]{1,0:T(8,128)(2,1)} %own_hbm.1), channel_id=1, source_target_pairs={{0,1},{1,0},{2,3},{3,2},{4,5},{5,4},{6,7},{7,6},{8,9},{9,8},{10,11... | collective-permute-start | bytes 786440 | tf_op jit(solution)/shard_map/ppermute | solution.py:366
  1.1 12.4 %collective-permute-start.7 = (bf16[512,256]{1,0:T(8,128)(2,1)}, bf16[512,256]{1,0:T(8,128)(2,1)S(1)}, u32[]{:S(2)}, u32[]{:S(2)}) collective-permute-start(bf16[512,256]{1,0:T(8,128)(2,1)} %own_hbm.1), channel_id=1, source_target_pairs={{1,2},{3,4},{5,6},{7,8},{9,10},{11,12},{13,14},{15,16},{17,18},{19... | collective-permute-start | bytes 786440 | tf_op jit(solution)/shard_map/ppermute | solution.py:368
  5.2 10.0 %collective-permute-start.4 = (bf16[1,264,128]{2,1,0:T(8,128)(2,1)}, bf16[1,264,128]{2,1,0:T(8,128)(2,1)S(1)}, u32[]{:S(2)}, u32[]{:S(2)}) collective-permute-start(bf16[1,264,128]{2,1,0:T(8,128)(2,1)} %get-tuple-element.29), channel_id=1, source_target_pairs={{0,2},{1,3},{2,0},{3,1},{4,6},{5,7},{6,4},{7,5},{8,10},{9,11},{10,... | collective-permute-start | bytes 202760 | tf_op jit(solution)/shard_map/ppermute | solution.py:31
  8.3 13.4 %collective-permute-start.3 = (bf16[1,136,256]{2,1,0:T(8,128)(2,1)}, bf16[1,136,256]{2,1,0:T(8,128)(2,1)S(1)}, u32[]{:S(2)}, u32[]{:S(2)}) collective-permute-start(bf16[1,136,256]{2,1,0:T(8,128)(2,1)} %get-tuple-element.28.refs_0_), channel_id=1, source_target_pairs={{0,24},{1,25},{2,26},{3,27},{4,28},{5,29},{6,30},{7,31},{8,16},{9,... | collective-permute-start | bytes 208904 | tf_op jit(solution)/shard_map/ppermute | solution.py:31
  12.9 8.9 %collective-permute-start.2 = (bf16[1,136,256]{2,1,0:T(8,128)(2,1)}, bf16[1,136,256]{2,1,0:T(8,128)(2,1)S(1)}, u32[]{:S(2)}, u32[]{:S(2)}) collective-permute-start(bf16[1,136,256]{2,1,0:T(8,128)(2,1)} %get-tuple-element.28.refs_0_), channel_id=1, source_target_pairs={{0,16},{1,17},{2,18},{3,19},{4,20},{5,21},{6,22},{7,23},{8,24},{9,... | collective-permute-start | bytes 208904 | tf_op jit(solution)/shard_map/ppermute | solution.py:31
  12.9 8.9 %collective-permute-start.1 = (bf16[1,136,256]{2,1,0:T(8,128)(2,1)}, bf16[1,136,256]{2,1,0:T(8,128)(2,1)S(1)}, u32[]{:S(2)}, u32[]{:S(2)}) collective-permute-start(bf16[1,136,256]{2,1,0:T(8,128)(2,1)} %get-tuple-element.28.refs_0_), channel_id=1, source_target_pairs={{0,8},{1,9},{2,10},{3,11},{4,12},{5,13},{6,14},{7,15},{8,0},{9,1},... | collective-permute-start | bytes 208904 | tf_op jit(solution)/shard_map/ppermute | solution.py:31
  13.5 8.2 %collective-permute-start.5 = (bf16[1,264,128]{2,1,0:T(8,128)(2,1)}, bf16[1,264,128]{2,1,0:T(8,128)(2,1)S(1)}, u32[]{:S(2)}, u32[]{:S(2)}) collective-permute-start(bf16[1,264,128]{2,1,0:T(8,128)(2,1)} %get-tuple-element.30), channel_id=1, source_target_pairs={{0,4},{1,5},{2,6},{3,7},{4,0},{5,1},{6,2},{7,3},{8,12},{9,13},{10,... | collective-permute-start | bytes 202760 | tf_op jit(solution)/shard_map/ppermute | solution.py:31
  15.1 6.6 %collective-permute-start.6 = (bf16[1,264,128]{2,1,0:T(8,128)(2,1)}, bf16[1,264,128]{2,1,0:T(8,128)(2,1)S(1)}, u32[]{:S(2)}, u32[]{:S(2)}) collective-permute-start(bf16[1,264,128]{2,1,0:T(8,128)(2,1)} %get-tuple-element.31), channel_id=1, source_target_pairs={{0,6},{1,7},{2,4},{3,5},{4,2},{5,3},{6,0},{7,1},{8,14},{9,15},{10,... | collective-permute-start | bytes 202760 | tf_op jit(solution)/shard_map/ppermute | solution.py:31
  16.9 1.7 %copy-start = (bf16[2,10,256,256]{3,2,1,0:T(8,128)(2,1)S(1)}, bf16[2,10,256,256]{3,2,1,0:T(8,128)(2,1)}, u32[]{:S(2)}) copy-start(bf16[2,10,256,256]{3,2,1,0:T(8,128)(2,1)} %blocks_ref.1) | copy-start | bytes 7864324
  18.6 0.9 %copy-start.1 = (bf16[512,256]{1,0:T(8,128)(2,1)S(1)}, bf16[512,256]{1,0:T(8,128)(2,1)}, u32[]{:S(2)}) copy-start(bf16[512,256]{1,0:T(8,128)(2,1)} %own_hbm.1) | copy-start | bytes 786436
  19.6 0.7 %copy-start.5 = (s32[2,10]{1,0:T(2,128)S(1)}, s32[2,10]{1,0:T(2,128)}, u32[]{:S(2)}) copy-start(s32[2,10]{1,0:T(2,128)} %list_hbm.1) | copy-start | bytes 244
  20.3 1.5 %copy-start.2 = (bf16[1,136,256]{2,1,0:T(8,128)(2,1)S(1)}, bf16[1,136,256]{2,1,0:T(8,128)(2,1)}, u32[]{:S(2)}) copy-start(bf16[1,136,256]{2,1,0:T(8,128)(2,1)} %get-tuple-element.28.refs_0_) | copy-start | bytes 208900
  20.3 1.5 %copy-start.3 = (bf16[1,264,128]{2,1,0:T(8,128)(2,1)S(1)}, bf16[1,264,128]{2,1,0:T(8,128)(2,1)}, u32[]{:S(2)}) copy-start(bf16[1,264,128]{2,1,0:T(8,128)(2,1)} %get-tuple-element.37.refs_4_) | copy-start | bytes 202756
  20.3 9.1 %copy-start.4 = (bf16[2,64,256]{2,1,0:T(8,128)(2,1)S(1)}, bf16[2,64,256]{2,1,0:T(8,128)(2,1)}, u32[]{:S(2)}) copy-start(bf16[2,64,256]{2,1,0:T(8,128)(2,1)} %get-tuple-element.27.basis_ref) | copy-start | bytes 196612
  22.4 5.0 %collective-permute-start.8 = (bf16[1,128,256]{2,1,0:T(8,128)(2,1)S(1)}, bf16[1,128,256]{2,1,0:T(8,128)(2,1)S(1)}, u32[]{:S(2)}, u32[]{:S(2)}) collective-permute-start(bf16[1,128,256]{2,1,0:T(8,128)(2,1)S(1)} %get-tuple-element.42), channel_id=1, source_target_pairs={{0,2},{1,3},{2,0},{3,1},{4,6},{5,7},{6,4},{7,5},{8,10},{9,11},{10,... | collective-permute-start | bytes 196616 | tf_op jit(solution)/shard_map/ppermute | solution.py:31
  22.6 4.9 %collective-permute-start.9 = (bf16[1,128,256]{2,1,0:T(8,128)(2,1)S(1)}, bf16[1,128,256]{2,1,0:T(8,128)(2,1)S(1)}, u32[]{:S(2)}, u32[]{:S(2)}) collective-permute-start(bf16[1,128,256]{2,1,0:T(8,128)(2,1)S(1)} %get-tuple-element.43), channel_id=1, source_target_pairs={{0,4},{1,5},{2,6},{3,7},{4,0},{5,1},{6,2},{7,3},{8,12},{9,13},{10,... | collective-permute-start | bytes 196616 | tf_op jit(solution)/shard_map/ppermute | solution.py:31
  24.1 5.2 %collective-permute-start.10 = (bf16[1,128,256]{2,1,0:T(8,128)(2,1)S(1)}, bf16[1,128,256]{2,1,0:T(8,128)(2,1)S(1)}, u32[]{:S(2)}, u32[]{:S(2)}) collective-permute-start(bf16[1,128,256]{2,1,0:T(8,128)(2,1)S(1)} %get-tuple-element.44), channel_id=1, source_target_pairs={{0,6},{1,7},{2,4},{3,5},{4,2},{5,3},{6,0},{7,1},{8,14},{9,15},{10,... | collective-permute-start | bytes 196616 | tf_op jit(solution)/shard_map/ppermute | solution.py:31
  30.3 1.4 %collective-permute-start.11 = (f32[320,128]{1,0:T(8,128)S(1)}, f32[320,128]{1,0:T(8,128)S(1)}, u32[]{:S(2)}, u32[]{:S(2)}) collective-permute-start(f32[320,128]{1,0:T(8,128)S(1)} %get-tuple-element.46), channel_id=1, source_target_pairs={{0,1},{1,0},{2,3},{3,2},{4,5},{5,4},{6,7},{7,6},{8,9},{9,8},{10,11... | collective-permute-start | bytes 491528 | tf_op jit(solution)/shard_map/ppermute | solution.py:35
  31.7 4.2 %collective-permute-start.15 = (bf16[320,128]{1,0:T(8,128)(2,1)S(1)}, bf16[320,128]{1,0:T(8,128)(2,1)S(1)}, u32[]{:S(2)}, u32[]{:S(2)}) collective-permute-start(bf16[320,128]{1,0:T(8,128)(2,1)S(1)} %get-tuple-element.49), channel_id=1, source_target_pairs={{1,15},{3,13},{5,11},{7,9},{9,7},{11,5},{13,3},{15,1},{17,31},{19,... | collective-permute-start | bytes 245768 | tf_op jit(solution)/shard_map/ppermute | solution.py:31
  32.4 5.4 %collective-permute-start.14 = (bf16[320,128]{1,0:T(8,128)(2,1)S(1)}, bf16[320,128]{1,0:T(8,128)(2,1)S(1)}, u32[]{:S(2)}, u32[]{:S(2)}) collective-permute-start(bf16[320,128]{1,0:T(8,128)(2,1)S(1)} %get-tuple-element.49), channel_id=1, source_target_pairs={{0,6},{1,11},{2,4},{3,9},{4,2},{5,15},{6,0},{7,13},{8,14},{9,3},{1... | collective-permute-start | bytes 245768 | tf_op jit(solution)/shard_map/ppermute | solution.py:31
  34.2 5.3 %collective-permute-start.13 = (bf16[320,128]{1,0:T(8,128)(2,1)S(1)}, bf16[320,128]{1,0:T(8,128)(2,1)S(1)}, u32[]{:S(2)}, u32[]{:S(2)}) collective-permute-start(bf16[320,128]{1,0:T(8,128)(2,1)S(1)} %get-tuple-element.49), channel_id=1, source_target_pairs={{0,4},{1,13},{2,6},{3,15},{4,0},{5,9},{6,2},{7,11},{8,12},{9,5},{1... | collective-permute-start | bytes 245768 | tf_op jit(solution)/shard_map/ppermute | solution.py:31
  35.1 4.5 %collective-permute-start.12 = (bf16[320,128]{1,0:T(8,128)(2,1)S(1)}, bf16[320,128]{1,0:T(8,128)(2,1)S(1)}, u32[]{:S(2)}, u32[]{:S(2)}) collective-permute-start(bf16[320,128]{1,0:T(8,128)(2,1)S(1)} %get-tuple-element.49), channel_id=1, source_target_pairs={{0,2},{1,9},{2,0},{3,11},{4,6},{5,13},{6,4},{7,15},{8,10},{9,1},{1... | collective-permute-start | bytes 245768 | tf_op jit(solution)/shard_map/ppermute | solution.py:31
  39.7 3.7 %collective-permute-start.16 = (f32[2,320,128]{2,1,0:T(8,128)S(1)}, f32[2,320,128]{2,1,0:T(8,128)S(1)}, u32[]{:S(2)}, u32[]{:S(2)}) collective-permute-start(f32[2,320,128]{2,1,0:T(8,128)S(1)} %pad_maximum_fusion.mine_ref), channel_id=1, source_target_pairs={{0,1},{1,0},{2,3},{3,2},{4,5},{5,4},{6,7},{7,6},{8,9},{9,8},{10,11... | collective-permute-start | bytes 983048 | tf_op jit(solution)/shard_map/ppermute | solution.py:35

commit v6 on v5

--- a/solution.py
+++ b/solution.py
@@ -132,8 +132,9 @@
         outs[m][0] = total.astype(outs[m].dtype)
 
 
-def near_kernel(list_hbm, blocks_ref, own_hbm, swap_ref, cross_ref, out_ref, held, entries, sems):
-    leaves, count, rows, _ = blocks_ref.shape
+def near_kernel(leaf, list_hbm, blocks_ref, own_hbm, swap_ref, cross_ref, out_ref, held, entries, sems):
+    leaves = entries.shape[0]
+    _, count, rows, _ = blocks_ref.shape
     pairs = [(list_hbm, entries)]
     pairs += [(own_hbm.at[pl.ds(j * rows, rows)], held.at[j]) for j in range(leaves)]
     copies = [pltpu.make_async_copy(src, dst, sems.at[i]) for i, (src, dst) in enumerate(pairs)]
@@ -149,21 +150,21 @@
     odd = device % 2
     before = (2 - odd) * leaves
     after = (1 + odd) * leaves
-    for l in range(leaves):
-        acc = jnp.zeros((rows, held.shape[2]), jnp.float32)
-        for k in range(count):
-            entry = entries[l, k]
-            shift = entry - device * leaves
-            outside = jnp.where(shift < 0, before + leaves + shift, after + shift - leaves)
-            slot = jnp.where((shift < 0) | (shift >= leaves), outside, shift)
-            slot = jnp.where(entry < 0, 3 * leaves, slot)
-            acc = acc + dot(blocks_ref[l, k], held[slot])
-        out_ref[l * rows : (l + 1) * rows, :] = acc
-
-
-def combine_kernel(basis_ref, near_ref, own_ref, *refs):
-    *got, samples_ref, gram_ref = refs
+    acc = jnp.zeros((rows, held.shape[2]), jnp.float32)
+    for k in range(count):
+        entry = entries[leaf, k]
+        shift = entry - device * leaves
+        outside = jnp.where(shift < 0, before + leaves + shift, after + shift - leaves)
+        slot = jnp.where((shift < 0) | (shift >= leaves), outside, shift)
+        slot = jnp.where(entry < 0, 3 * leaves, slot)
+        acc = acc + dot(blocks_ref[0, k], held[slot])
+    out_ref[...] = acc
+
+
+def combine_kernel(basis_ref, own_ref, *refs):
     leaves, rank, rows = basis_ref.shape
+    nears = refs[:leaves]
+    *got, samples_ref, gram_ref = refs[leaves:]
     total = own_ref[0]
     for ref in got:
         total = total + ref[0].astype(jnp.float32)
@@ -171,7 +172,7 @@
     for l in range(leaves):
         far = dot_t(basis_ref[l], coeff[l * rank : (l + 1) * rank, :])
         at = slice(l * rows, (l + 1) * rows)
-        samples_ref[at, :] = (near_ref[at, :] + far).astype(jnp.bfloat16)
+        samples_ref[at, :] = (nears[l][...] + far).astype(jnp.bfloat16)
     left, right = samples_ref[:, 0:128], samples_ref[:, 128:256]
     top = dot_t(left, samples_ref[...])
     gram_ref[...] = pack(top, dot_t(right, right))
@@ -400,24 +401,27 @@
 
     column = [hop(mine, PLANE * k, PLANE * k) for k in range(1, high)]
     gathered = [hop(pays[m], m, m) for m in range(1, PLANE)]
-    near_part = pl.pallas_call(
-        near_kernel,
-        out_shape=jax.ShapeDtypeStruct((rows, width), jnp.float32),
-        in_specs=[hbm, VMEM, hbm, VMEM, VMEM],
-        out_specs=VMEM,
-        scratch_shapes=[
-            pltpu.VMEM((3 * leaf_count + 1, leaf_rows, width), bf16),
-            pltpu.SMEM(near_list.shape, jnp.int32),
-            pltpu.SemaphoreType.DMA((1 + leaf_count,)),
-        ],
-        compiler_params=params(NEAR_KIB),
-        cost_estimate=pl.CostEstimate(
-            flops=2 * rows * near_count * leaf_rows * width,
-            bytes_accessed=near_blocks.size * 2 + 5 * rows * width * 2,
-            transcendentals=0,
-        ),
-    )(near_list, near_blocks, sample_cols, swap, cross)
-    column, gathered, near_part = lax.optimization_barrier((column, gathered, near_part))
+    def near_leaf(leaf):
+        return pl.pallas_call(
+            functools.partial(near_kernel, leaf),
+            out_shape=jax.ShapeDtypeStruct((leaf_rows, width), jnp.float32),
+            in_specs=[hbm, VMEM, hbm, VMEM, VMEM],
+            out_specs=VMEM,
+            scratch_shapes=[
+                pltpu.VMEM((3 * leaf_count + 1, leaf_rows, width), bf16),
+                pltpu.SMEM(near_list.shape, jnp.int32),
+                pltpu.SemaphoreType.DMA((1 + leaf_count,)),
+            ],
+            compiler_params=params(NEAR_KIB),
+            cost_estimate=pl.CostEstimate(
+                flops=2 * leaf_rows * near_count * leaf_rows * width,
+                bytes_accessed=near_blocks.size + 5 * rows * width * 2,
+                transcendentals=0,
+            ),
+        )(near_list, lax.slice_in_dim(near_blocks, leaf, leaf + 1, axis=0), sample_cols, swap, cross)
+
+    near_parts = [near_leaf(0)]
+    column, gathered, near_parts = lax.optimization_barrier((column, gathered, near_parts))
     own, *parts = pl.pallas_call(
         functools.partial(partial_kernel, leaf_count, slots),
         out_shape=[jax.ShapeDtypeStruct((1, leaf_count * rank, width), jnp.float32)]
@@ -426,18 +430,19 @@
         out_specs=[VMEM] * PLANE,
         compiler_params=params(),
     )(mine, *column, pays[0], *gathered)
-    got = [hop(parts[m - 1], m, m) for m in range(1, PLANE)]
-
+    got = [hop(parts[m - 1], m, m) for m in range(PLANE - 1, 0, -1)]
+
+    near_parts = near_parts + [near_leaf(leaf) for leaf in range(1, leaf_count)]
     samples, gram = pl.pallas_call(
         combine_kernel,
         out_shape=(
             jax.ShapeDtypeStruct((rows, width), jnp.bfloat16),
             jax.ShapeDtypeStruct((320, 128), jnp.float32),
         ),
-        in_specs=[VMEM] * (3 + PLANE - 1),
+        in_specs=[VMEM] * (2 + leaf_count + PLANE - 1),
         out_specs=[VMEM] * 2,
         compiler_params=params(),
-    )(row_basis, near_part, own, *got)
+    )(row_basis, own, *near_parts, *got)
 
     total, mask = gram, 1
     while mask < n_sub:

time: 51.7 us -> 51.5 us (level)
  local copies, waits for them, and re-layouts: 3.38 us -> 1.96 us
  Pallas kernels: 13.8 us -> 14.5 us
  starting transfers between devices: 23.1 us -> 23.7 us
    unnamed x12 -> x10, local copies, waits for them, and re-layouts: 3.38 us -> 0.02 us
    slice x0 -> x1, local copies, waits for them, and re-layouts: none -> 1.94 us  [near_leaf(): lax.slice_in_dim(near_blocks, leaf, leaf + 1, axis=0)]
    pallas_call x1 -> x2, Pallas kernels: 1.45 us -> 2.23 us  [near_leaf(): pl.pallas_call(functools.partial(near_kernel, leaf), out_shape=jax.ShapeD...]
    ppermute x2, starting transfers between devices: 2.42 us -> 3.02 us  [sub_hop(): lax.ppermute(value, 'sub', [(i, i ^ mask) for i in range(lax.axis_size('s...]
  transfers between devices with their start and end apart: 17 -> 17, of which waited for: 8 -> 9; matrix products, arithmetic and copies ran while one was open for 0% -> 4% of each run, Pallas kernels for 8% -> 9%
where the time goes in v6:
time: 51.5 us; the launch traced here: 51.3 us
  starting transfers between devices  23.7 us (46%)
  Pallas kernels  14.5 us (28%)
  waiting for transfers between devices  10.2 us (20%)
  local copies, waits for them, and re-layouts  1.96 us (4%)
  between operations  0.8 us (2%)
    ppermute x13, starting transfers between devices, hop(): return lax.ppermute(value, AXES, pairs)  19.5 us
    pallas_call x1, Pallas kernels, factor_all(): pl.pallas_call(factor_kernel, out_shape=(jax.ShapeDtypeStruct((256, 256),...  8.14 us
    ppermute x13, waiting for transfers between devices, hop(): return lax.ppermute(value, AXES, pairs)  6.83 us
    ppermute x2, starting transfers between devices, sub_hop(): lax.ppermute(value, 'sub', [(i, i ^ mask) for i in range(lax.axis_size('s...  3.02 us
    ppermute x2, waiting for transfers between devices, sub_hop(): lax.ppermute(value, 'sub', [(i, i ^ mask) for i in range(lax.axis_size('s...  2.65 us
    pallas_call x1, Pallas kernels, body(): pl.pallas_call(first_kernel, out_shape=[jax.ShapeDtypeStruct((1, leaf_cou...  2.63 us
    pallas_call x2, Pallas kernels, near_leaf(): pl.pallas_call(functools.partial(near_kernel, leaf), out_shape=jax.ShapeD...  2.23 us
    slice x1, local copies, waits for them, and re-layouts, near_leaf(): lax.slice_in_dim(near_blocks, leaf, leaf + 1, axis=0)  1.94 us
  transfers between devices with their start and end apart: 17, of which 9 were waited for; matrix products, arithmetic and copies ran while one was open for 4% of the time, Pallas kernels for 9%

profile of v6, /device:TPU:0, one launch (start us, length us, event | category | flops | bytes accessed | tf_op | source)
XLA Modules:
  0.0 51.3 jit_solution(12438958265472586557)
XLA Ops:
  0.6 0.5 %collective-permute-start = (bf16[512,256]{1,0:T(8,128)(2,1)}, bf16[512,256]{1,0:T(8,128)(2,1)S(1)}, u32[]{:S(2)}, u32[]{:S(2)}) collective-permute-start(bf16[512,256]{1,0:T(8,128)(2,1)} %own_hbm.3), channel_id=1, source_target_pairs={{0,1},{1,0},{2,3},{3,2},{4,5},{5,4},{6,7},{7,6},{8,9},{9,8},{10,11... | collective-permute-start | bytes 786440 | tf_op jit(solution)/shard_map/ppermute | solution.py:367
  1.1 0.7 %collective-permute-start.7 = (bf16[512,256]{1,0:T(8,128)(2,1)}, bf16[512,256]{1,0:T(8,128)(2,1)S(1)}, u32[]{:S(2)}, u32[]{:S(2)}) collective-permute-start(bf16[512,256]{1,0:T(8,128)(2,1)} %own_hbm.3), channel_id=1, source_target_pairs={{1,2},{3,4},{5,6},{7,8},{9,10},{11,12},{13,14},{15,16},{17,18},{19... | collective-permute-start | bytes 786440 | tf_op jit(solution)/shard_map/ppermute | solution.py:369
  1.8 0.7 %collective-permute-done.swap_ref = bf16[512,256]{1,0:T(8,128)(2,1)S(1)} collective-permute-done((bf16[512,256]{1,0:T(8,128)(2,1)}, bf16[512,256]{1,0:T(8,128)(2,1)S(1)}, u32[]{:S(2)}, u32[]{:S(2)}) %collective-permute-start) | collective-permute-done | bytes 262176 | tf_op jit(solution)/shard_map/ppermute | solution.py:367
  2.5 2.6 %shard_map.103 = (bf16[1,136,256]{2,1,0:T(8,128)(2,1)}, bf16[2,64,256]{2,1,0:T(8,128)(2,1)}, bf16[1,264,128]{2,1,0:T(8,128)(2,1)}, bf16[1,264,128]{2,1,0:T(8,128...) custom-call(bf16[2,64,256]{2,1,0:T(8,128)(2,1)} %basis_hbm, bf16[512,256]{1,0:T(8,128)(2,1)} %own_hbm.3, ...), custom_call_target="tpu_custom_call" | custom-call | tf_op jit(solution)/shard_map/pallas_call | solution.py:376
  5.2 3.1 %collective-permute-start.4 = (bf16[1,264,128]{2,1,0:T(8,128)(2,1)}, bf16[1,264,128]{2,1,0:T(8,128)(2,1)S(1)}, u32[]{:S(2)}, u32[]{:S(2)}) collective-permute-start(bf16[1,264,128]{2,1,0:T(8,128)(2,1)} %get-tuple-element.29), channel_id=1, source_target_pairs={{0,2},{1,3},{2,0},{3,1},{4,6},{5,7},{6,4},{7,5},{8,10},{9,11},{10,... | collective-permute-start | bytes 202760 | tf_op jit(solution)/shard_map/ppermute | solution.py:31
  8.3 2.6 %collective-permute-start.1 = (bf16[1,136,256]{2,1,0:T(8,128)(2,1)}, bf16[1,136,256]{2,1,0:T(8,128)(2,1)S(1)}, u32[]{:S(2)}, u32[]{:S(2)}) collective-permute-start(bf16[1,136,256]{2,1,0:T(8,128)(2,1)} %get-tuple-element.28.refs_0_), channel_id=1, source_target_pairs={{0,8},{1,9},{2,10},{3,11},{4,12},{5,13},{6,14},{7,15},{8,0},{9,1},... | collective-permute-start | bytes 208904 | tf_op jit(solution)/shard_map/ppermute | solution.py:31
  10.9 2.6 %collective-permute-start.2 = (bf16[1,136,256]{2,1,0:T(8,128)(2,1)}, bf16[1,136,256]{2,1,0:T(8,128)(2,1)S(1)}, u32[]{:S(2)}, u32[]{:S(2)}) collective-permute-start(bf16[1,136,256]{2,1,0:T(8,128)(2,1)} %get-tuple-element.28.refs_0_), channel_id=1, source_target_pairs={{0,16},{1,17},{2,18},{3,19},{4,20},{5,21},{6,22},{7,23},{8,24},{9,... | collective-permute-start | bytes 208904 | tf_op jit(solution)/shard_map/ppermute | solution.py:31
  13.5 1.6 %collective-permute-start.5 = (bf16[1,264,128]{2,1,0:T(8,128)(2,1)}, bf16[1,264,128]{2,1,0:T(8,128)(2,1)S(1)}, u32[]{:S(2)}, u32[]{:S(2)}) collective-permute-start(bf16[1,264,128]{2,1,0:T(8,128)(2,1)} %get-tuple-element.30), channel_id=1, source_target_pairs={{0,4},{1,5},{2,6},{3,7},{4,0},{5,1},{6,2},{7,3},{8,12},{9,13},{10,... | collective-permute-start | bytes 202760 | tf_op jit(solution)/shard_map/ppermute | solution.py:31
  15.1 1.8 %collective-permute-start.6 = (bf16[1,264,128]{2,1,0:T(8,128)(2,1)}, bf16[1,264,128]{2,1,0:T(8,128)(2,1)S(1)}, u32[]{:S(2)}, u32[]{:S(2)}) collective-permute-start(bf16[1,264,128]{2,1,0:T(8,128)(2,1)} %get-tuple-element.31), channel_id=1, source_target_pairs={{0,6},{1,7},{2,4},{3,5},{4,2},{5,3},{6,0},{7,1},{8,14},{9,15},{10,... | collective-permute-start | bytes 202760 | tf_op jit(solution)/shard_map/ppermute | solution.py:31
  16.9 1.9 %fusion.8 = (bf16[1,10,256,256]{3,2,1,0:T(8,128)(2,1)S(1)}, bf16[1,10,256,256]{3,2,1,0:T(8,128)(2,1)S(1)}) fusion(bf16[2,10,256,256]{3,2,1,0:T(8,128)(2,1)} %param.8), kind=kLoop, calls=%fused_computation.14 | loop fusion | bytes 5242880 | tf_op jit(solution)/shard_map/slice | solution.py:421
  18.9 1.1 %shard_map.104.refs_0_ = f32[256,256]{1,0:T(8,128)S(1)} custom-call(s32[2,10]{1,0:T(2,128)S(1)} %copy-done.4, bf16[1,10,256,256]{3,2,1,0:T(8,128)(2,1)S(1)} %get-tuple-element.52.blocks_ref, bf16[512,256]{1,0:T(8,128)(2,1)S(1)} %copy-done, bf16[512,256]{1,0:T(8,128)(2,1)S(1)} %collective-permute-done.swap_ref, ...), custom_call_target="tpu_custom_call" | custom-call | flops 335544320 | bytes 2621440 | tf_op jit(solution)/shard_map/pallas_call | solution.py:405
  20.0 0.5 collective-permute-done.6.refs_7_
  20.6 0.6 %shard_map.105 = (f32[1,128,256]{2,1,0:T(8,128)S(1)}, bf16[1,128,256]{2,1,0:T(8,128)(2,1)S(1)}, bf16[1,128,256]{2,1,0:T(8,128)(2,1)S(1)}, bf16[1,128,256]{2,1,0:T(8,128)(2,1)S(1)}) custom-call(bf16[1,136,256]{2,1,0:T(8,128)(2,1)S(1)} %copy-done.1, bf16[1,136,256]{2,1,0:T(8,128)(2,1)S(1)} %collective-permute-done.1.refs_1_, ...), custom_call_target="tpu_custom_call" | custom-call | tf_op jit(solution)/shard_map/pallas_call | solution.py:425
  21.1 1.2 %collective-permute-start.10 = (bf16[1,128,256]{2,1,0:T(8,128)(2,1)S(1)}, bf16[1,128,256]{2,1,0:T(8,128)(2,1)S(1)}, u32[]{:S(2)}, u32[]{:S(2)}) collective-permute-start(bf16[1,128,256]{2,1,0:T(8,128)(2,1)S(1)} %get-tuple-element.44), channel_id=1, source_target_pairs={{0,2},{1,3},{2,0},{3,1},{4,6},{5,7},{6,4},{7,5},{8,10},{9,11},{10,... | collective-permute-start | bytes 196616 | tf_op jit(solution)/shard_map/ppermute | solution.py:31
  22.4 0.7 %collective-permute-start.8 = (bf16[1,128,256]{2,1,0:T(8,128)(2,1)S(1)}, bf16[1,128,256]{2,1,0:T(8,128)(2,1)S(1)}, u32[]{:S(2)}, u32[]{:S(2)}) collective-permute-start(bf16[1,128,256]{2,1,0:T(8,128)(2,1)S(1)} %get-tuple-element.42), channel_id=1, source_target_pairs={{0,6},{1,7},{2,4},{3,5},{4,2},{5,3},{6,0},{7,1},{8,14},{9,15},{10,... | collective-permute-start | bytes 196616 | tf_op jit(solution)/shard_map/ppermute | solution.py:31
  23.1 1.6 %collective-permute-start.9 = (bf16[1,128,256]{2,1,0:T(8,128)(2,1)S(1)}, bf16[1,128,256]{2,1,0:T(8,128)(2,1)S(1)}, u32[]{:S(2)}, u32[]{:S(2)}) collective-permute-start(bf16[1,128,256]{2,1,0:T(8,128)(2,1)S(1)} %get-tuple-element.43), channel_id=1, source_target_pairs={{0,4},{1,5},{2,6},{3,7},{4,0},{5,1},{6,2},{7,3},{8,12},{9,13},{10,... | collective-permute-start | bytes 196616 | tf_op jit(solution)/shard_map/ppermute | solution.py:31
  24.7 1.1 %shard_map.106.refs_1_ = f32[256,256]{1,0:T(8,128)S(1)} custom-call(s32[2,10]{1,0:T(2,128)S(1)} %copy-done.4, bf16[1,10,256,256]{3,2,1,0:T(8,128)(2,1)S(1)} %get-tuple-element.51.blocks_ref, bf16[512,256]{1,0:T(8,128)(2,1)S(1)} %copy-done, bf16[512,256]{1,0:T(8,128)(2,1)S(1)} %collective-permute-done.swap_ref, ...), custom_call_target="tpu_custom_call" | custom-call | flops 335544320 | bytes 2621440 | tf_op jit(solution)/shard_map/pallas_call | solution.py:405
  25.8 1.8 %collective-permute-done.8.refs_2_ = bf16[1,128,256]{2,1,0:T(8,128)(2,1)S(1)} collective-permute-done((bf16[1,128,256]{2,1,0:T(8,128)(2,1)S(1)}, bf16[1,128,256]{2,1,0:T(8,128)(2,1)S(1)}, u32[]{:S(2)}, u32[]{:S(2)}) %collective-permute-start.8) | collective-permute-done | bytes 65568 | tf_op jit(solution)/shard_map/ppermute | solution.py:31
  27.6 0.4 collective-permute-done.9.refs_3_
  28.1 1.0 %shard_map.107 = (bf16[512,256]{1,0:T(8,128)(2,1)}, f32[320,128]{1,0:T(8,128)S(1)}) custom-call(bf16[2,64,256]{2,1,0:T(8,128)(2,1)S(1)} %copy-done.3, f32[1,128,256]{2,1,0:T(8,128)S(1)} %get-tuple-element.40.own_ref, f32[256,256]{1,0:T(8,128)S(1)} %shard_map.104.refs_0_, f32[256,256]{1,0:T(8,128)S(1)} %shard_map.106.refs_1_, ...), custom_call_target="tpu_custom_call" | custom-call | tf_op jit(solution)/shard_map/pallas_call | solution.py:436
  29.0 1.4 %collective-permute-done.11 = f32[320,128]{1,0:T(8,128)S(1)} collective-permute-done((f32[320,128]{1,0:T(8,128)S(1)}, f32[320,128]{1,0:T(8,128)S(1)}, u32[]{:S(2)}, u32[]{:S(2)}) %collective-permute-start.11) | collective-permute-done | bytes 163872 | tf_op jit(solution)/shard_map/ppermute | solution.py:35
  30.5 1.3 %collective-permute-start.12 = (bf16[320,128]{1,0:T(8,128)(2,1)S(1)}, bf16[320,128]{1,0:T(8,128)(2,1)S(1)}, u32[]{:S(2)}, u32[]{:S(2)}) collective-permute-start(bf16[320,128]{1,0:T(8,128)(2,1)S(1)} %get-tuple-element.49), channel_id=1, source_target_pairs={{0,2},{1,9},{2,0},{3,11},{4,6},{5,13},{6,4},{7,15},{8,10},{9,1},{1... | collective-permute-start | bytes 245768 | tf_op jit(solution)/shard_map/ppermute | solution.py:31
  31.7 0.9 %collective-permute-start.13 = (bf16[320,128]{1,0:T(8,128)(2,1)S(1)}, bf16[320,128]{1,0:T(8,128)(2,1)S(1)}, u32[]{:S(2)}, u32[]{:S(2)}) collective-permute-start(bf16[320,128]{1,0:T(8,128)(2,1)S(1)} %get-tuple-element.49), channel_id=1, source_target_pairs={{0,4},{1,13},{2,6},{3,15},{4,0},{5,9},{6,2},{7,11},{8,12},{9,5},{1... | collective-permute-start | bytes 245768 | tf_op jit(solution)/shard_map/ppermute | solution.py:31
  32.6 1.4 %collective-permute-start.14 = (bf16[320,128]{1,0:T(8,128)(2,1)S(1)}, bf16[320,128]{1,0:T(8,128)(2,1)S(1)}, u32[]{:S(2)}, u32[]{:S(2)}) collective-permute-start(bf16[320,128]{1,0:T(8,128)(2,1)S(1)} %get-tuple-element.49), channel_id=1, source_target_pairs={{0,6},{1,11},{2,4},{3,9},{4,2},{5,15},{6,0},{7,13},{8,14},{9,3},{1... | collective-permute-start | bytes 245768 | tf_op jit(solution)/shard_map/ppermute | solution.py:31
  34.0 0.7 %collective-permute-start.15 = (bf16[320,128]{1,0:T(8,128)(2,1)S(1)}, bf16[320,128]{1,0:T(8,128)(2,1)S(1)}, u32[]{:S(2)}, u32[]{:S(2)}) collective-permute-start(bf16[320,128]{1,0:T(8,128)(2,1)S(1)} %get-tuple-element.49), channel_id=1, source_target_pairs={{1,15},{3,13},{5,11},{7,9},{9,7},{11,5},{13,3},{15,1},{17,31},{19,... | collective-permute-start | bytes 245768 | tf_op jit(solution)/shard_map/ppermute | solution.py:31
  34.7 0.3 collective-permute-done.12
  35.0 2.1 %collective-permute-done.13 = bf16[320,128]{1,0:T(8,128)(2,1)S(1)} collective-permute-done((bf16[320,128]{1,0:T(8,128)(2,1)S(1)}, bf16[320,128]{1,0:T(8,128)(2,1)S(1)}, u32[]{:S(2)}, u32[]{:S(2)}) %collective-permute-start.13) | collective-permute-done | bytes 81952 | tf_op jit(solution)/shard_map/ppermute | solution.py:31
  37.0 1.7 %collective-permute-done.14 = bf16[320,128]{1,0:T(8,128)(2,1)S(1)} collective-permute-done((bf16[320,128]{1,0:T(8,128)(2,1)S(1)}, bf16[320,128]{1,0:T(8,128)(2,1)S(1)}, u32[]{:S(2)}, u32[]{:S(2)}) %collective-permute-start.14) | collective-permute-done | bytes 81952 | tf_op jit(solution)/shard_map/ppermute | solution.py:31
  38.7 0.1 fusion.3
  38.9 3.0 %collective-permute-start.16 = (f32[2,320,128]{2,1,0:T(8,128)S(1)}, f32[2,320,128]{2,1,0:T(8,128)S(1)}, u32[]{:S(2)}, u32[]{:S(2)}) collective-permute-start(f32[2,320,128]{2,1,0:T(8,128)S(1)} %pad_maximum_fusion.mine_ref), channel_id=1, source_target_pairs={{0,1},{1,0},{2,3},{3,2},{4,5},{5,4},{6,7},{7,6},{8,9},{9,8},{10,11... | collective-permute-start | bytes 983048 | tf_op jit(solution)/shard_map/ppermute | solution.py:35
  41.9 1.3 %collective-permute-done.16.other_ref = f32[2,320,128]{2,1,0:T(8,128)S(1)} collective-permute-done((f32[2,320,128]{2,1,0:T(8,128)S(1)}, f32[2,320,128]{2,1,0:T(8,128)S(1)}, u32[]{:S(2)}, u32[]{:S(2)}) %collective-permute-start.16) | collective-permute-done | bytes 327712 | tf_op jit(solution)/shard_map/ppermute | solution.py:35
  43.1 8.1 %shard_map.108 = (f32[256,256]{1,0:T(8,128)}, bf16[3,256,256]{2,1,0:T(8,128)(2,1)}) custom-call(f32[320,128]{1,0:T(8,128)S(1)} %get-tuple-element.50.seg_ref, f32[2,320,128]{2,1,0:T(8,128)S(1)} %pad_maximum_fusion.mine_ref, f32[2,320,128]{2,1,0:T(8,128)S(1)} %collective-permute-done.16.other_ref), custom_call_target="tpu_custom_call" | custom-call | tf_op jit(solution)/shard_map/pallas_call | solution.py:340
  (22 shorter events, 0.1 us)
Async XLA Ops:
  0.6 1.9 %collective-permute-start = (bf16[512,256]{1,0:T(8,128)(2,1)}, bf16[512,256]{1,0:T(8,128)(2,1)S(1)}, u32[]{:S(2)}, u32[]{:S(2)}) collective-permute-start(bf16[512,256]{1,0:T(8,128)(2,1)} %own_hbm.3), channel_id=1, source_target_pairs={{0,1},{1,0},{2,3},{3,2},{4,5},{5,4},{6,7},{7,6},{8,9},{9,8},{10,11... | collective-permute-start | bytes 786440 | tf_op jit(solution)/shard_map/ppermute | solution.py:367
  1.1 12.3 %collective-permute-start.7 = (bf16[512,256]{1,0:T(8,128)(2,1)}, bf16[512,256]{1,0:T(8,128)(2,1)S(1)}, u32[]{:S(2)}, u32[]{:S(2)}) collective-permute-start(bf16[512,256]{1,0:T(8,128)(2,1)} %own_hbm.3), channel_id=1, source_target_pairs={{1,2},{3,4},{5,6},{7,8},{9,10},{11,12},{13,14},{15,16},{17,18},{19... | collective-permute-start | bytes 786440 | tf_op jit(solution)/shard_map/ppermute | solution.py:369
  5.2 10.0 %collective-permute-start.4 = (bf16[1,264,128]{2,1,0:T(8,128)(2,1)}, bf16[1,264,128]{2,1,0:T(8,128)(2,1)S(1)}, u32[]{:S(2)}, u32[]{:S(2)}) collective-permute-start(bf16[1,264,128]{2,1,0:T(8,128)(2,1)} %get-tuple-element.29), channel_id=1, source_target_pairs={{0,2},{1,3},{2,0},{3,1},{4,6},{5,7},{6,4},{7,5},{8,10},{9,11},{10,... | collective-permute-start | bytes 202760 | tf_op jit(solution)/shard_map/ppermute | solution.py:31
  8.3 12.2 %collective-permute-start.1 = (bf16[1,136,256]{2,1,0:T(8,128)(2,1)}, bf16[1,136,256]{2,1,0:T(8,128)(2,1)S(1)}, u32[]{:S(2)}, u32[]{:S(2)}) collective-permute-start(bf16[1,136,256]{2,1,0:T(8,128)(2,1)} %get-tuple-element.28.refs_0_), channel_id=1, source_target_pairs={{0,8},{1,9},{2,10},{3,11},{4,12},{5,13},{6,14},{7,15},{8,0},{9,1},... | collective-permute-start | bytes 208904 | tf_op jit(solution)/shard_map/ppermute | solution.py:31
  10.9 9.7 %collective-permute-start.2 = (bf16[1,136,256]{2,1,0:T(8,128)(2,1)}, bf16[1,136,256]{2,1,0:T(8,128)(2,1)S(1)}, u32[]{:S(2)}, u32[]{:S(2)}) collective-permute-start(bf16[1,136,256]{2,1,0:T(8,128)(2,1)} %get-tuple-element.28.refs_0_), channel_id=1, source_target_pairs={{0,16},{1,17},{2,18},{3,19},{4,20},{5,21},{6,22},{7,23},{8,24},{9,... | collective-permute-start | bytes 208904 | tf_op jit(solution)/shard_map/ppermute | solution.py:31
  13.5 7.1 %collective-permute-start.3 = (bf16[1,136,256]{2,1,0:T(8,128)(2,1)}, bf16[1,136,256]{2,1,0:T(8,128)(2,1)S(1)}, u32[]{:S(2)}, u32[]{:S(2)}) collective-permute-start(bf16[1,136,256]{2,1,0:T(8,128)(2,1)} %get-tuple-element.28.refs_0_), channel_id=1, source_target_pairs={{0,24},{1,25},{2,26},{3,27},{4,28},{5,29},{6,30},{7,31},{8,16},{9,... | collective-permute-start | bytes 208904 | tf_op jit(solution)/shard_map/ppermute | solution.py:31
  13.5 6.5 %collective-permute-start.5 = (bf16[1,264,128]{2,1,0:T(8,128)(2,1)}, bf16[1,264,128]{2,1,0:T(8,128)(2,1)S(1)}, u32[]{:S(2)}, u32[]{:S(2)}) collective-permute-start(bf16[1,264,128]{2,1,0:T(8,128)(2,1)} %get-tuple-element.30), channel_id=1, source_target_pairs={{0,4},{1,5},{2,6},{3,7},{4,0},{5,1},{6,2},{7,3},{8,12},{9,13},{10,... | collective-permute-start | bytes 202760 | tf_op jit(solution)/shard_map/ppermute | solution.py:31
  15.1 3.7 %copy-start = (bf16[512,256]{1,0:T(8,128)(2,1)S(1)}, bf16[512,256]{1,0:T(8,128)(2,1)}, u32[]{:S(2)}) copy-start(bf16[512,256]{1,0:T(8,128)(2,1)} %own_hbm.3) | copy-start | bytes 786436
  15.1 3.7 %copy-start.4 = (s32[2,10]{1,0:T(2,128)S(1)}, s32[2,10]{1,0:T(2,128)}, u32[]{:S(2)}) copy-start(s32[2,10]{1,0:T(2,128)} %list_hbm.3) | copy-start | bytes 244
  15.1 5.4 %collective-permute-start.6 = (bf16[1,264,128]{2,1,0:T(8,128)(2,1)}, bf16[1,264,128]{2,1,0:T(8,128)(2,1)S(1)}, u32[]{:S(2)}, u32[]{:S(2)}) collective-permute-start(bf16[1,264,128]{2,1,0:T(8,128)(2,1)} %get-tuple-element.31), channel_id=1, source_target_pairs={{0,6},{1,7},{2,4},{3,5},{4,2},{5,3},{6,0},{7,1},{8,14},{9,15},{10,... | collective-permute-start | bytes 202760 | tf_op jit(solution)/shard_map/ppermute | solution.py:31
  18.8 1.7 %copy-start.1 = (bf16[1,136,256]{2,1,0:T(8,128)(2,1)S(1)}, bf16[1,136,256]{2,1,0:T(8,128)(2,1)}, u32[]{:S(2)}) copy-start(bf16[1,136,256]{2,1,0:T(8,128)(2,1)} %get-tuple-element.28.refs_0_) | copy-start | bytes 208900
  18.8 1.7 %copy-start.2 = (bf16[1,264,128]{2,1,0:T(8,128)(2,1)S(1)}, bf16[1,264,128]{2,1,0:T(8,128)(2,1)}, u32[]{:S(2)}) copy-start(bf16[1,264,128]{2,1,0:T(8,128)(2,1)} %get-tuple-element.36.refs_4_) | copy-start | bytes 202756
  21.1 6.9 %copy-start.3 = (bf16[2,64,256]{2,1,0:T(8,128)(2,1)S(1)}, bf16[2,64,256]{2,1,0:T(8,128)(2,1)}, u32[]{:S(2)}) copy-start(bf16[2,64,256]{2,1,0:T(8,128)(2,1)} %get-tuple-element.27.basis_ref) | copy-start | bytes 196612
  21.1 4.7 %collective-permute-start.10 = (bf16[1,128,256]{2,1,0:T(8,128)(2,1)S(1)}, bf16[1,128,256]{2,1,0:T(8,128)(2,1)S(1)}, u32[]{:S(2)}, u32[]{:S(2)}) collective-permute-start(bf16[1,128,256]{2,1,0:T(8,128)(2,1)S(1)} %get-tuple-element.44), channel_id=1, source_target_pairs={{0,2},{1,3},{2,0},{3,1},{4,6},{5,7},{6,4},{7,5},{8,10},{9,11},{10,... | collective-permute-start | bytes 196616 | tf_op jit(solution)/shard_map/ppermute | solution.py:31
  22.4 5.3 %collective-permute-start.8 = (bf16[1,128,256]{2,1,0:T(8,128)(2,1)S(1)}, bf16[1,128,256]{2,1,0:T(8,128)(2,1)S(1)}, u32[]{:S(2)}, u32[]{:S(2)}) collective-permute-start(bf16[1,128,256]{2,1,0:T(8,128)(2,1)S(1)} %get-tuple-element.42), channel_id=1, source_target_pairs={{0,6},{1,7},{2,4},{3,5},{4,2},{5,3},{6,0},{7,1},{8,14},{9,15},{10,... | collective-permute-start | bytes 196616 | tf_op jit(solution)/shard_map/ppermute | solution.py:31
  23.1 5.0 %collective-permute-start.9 = (bf16[1,128,256]{2,1,0:T(8,128)(2,1)S(1)}, bf16[1,128,256]{2,1,0:T(8,128)(2,1)S(1)}, u32[]{:S(2)}, u32[]{:S(2)}) collective-permute-start(bf16[1,128,256]{2,1,0:T(8,128)(2,1)S(1)} %get-tuple-element.43), channel_id=1, source_target_pairs={{0,4},{1,5},{2,6},{3,7},{4,0},{5,1},{6,2},{7,3},{8,12},{9,13},{10,... | collective-permute-start | bytes 196616 | tf_op jit(solution)/shard_map/ppermute | solution.py:31
  29.0 1.4 %collective-permute-start.11 = (f32[320,128]{1,0:T(8,128)S(1)}, f32[320,128]{1,0:T(8,128)S(1)}, u32[]{:S(2)}, u32[]{:S(2)}) collective-permute-start(f32[320,128]{1,0:T(8,128)S(1)} %get-tuple-element.46), channel_id=1, source_target_pairs={{0,1},{1,0},{2,3},{3,2},{4,5},{5,4},{6,7},{7,6},{8,9},{9,8},{10,11... | collective-permute-start | bytes 491528 | tf_op jit(solution)/shard_map/ppermute | solution.py:35
  30.5 4.5 %collective-permute-start.12 = (bf16[320,128]{1,0:T(8,128)(2,1)S(1)}, bf16[320,128]{1,0:T(8,128)(2,1)S(1)}, u32[]{:S(2)}, u32[]{:S(2)}) collective-permute-start(bf16[320,128]{1,0:T(8,128)(2,1)S(1)} %get-tuple-element.49), channel_id=1, source_target_pairs={{0,2},{1,9},{2,0},{3,11},{4,6},{5,13},{6,4},{7,15},{8,10},{9,1},{1... | collective-permute-start | bytes 245768 | tf_op jit(solution)/shard_map/ppermute | solution.py:31
  31.7 5.3 %collective-permute-start.13 = (bf16[320,128]{1,0:T(8,128)(2,1)S(1)}, bf16[320,128]{1,0:T(8,128)(2,1)S(1)}, u32[]{:S(2)}, u32[]{:S(2)}) collective-permute-start(bf16[320,128]{1,0:T(8,128)(2,1)S(1)} %get-tuple-element.49), channel_id=1, source_target_pairs={{0,4},{1,13},{2,6},{3,15},{4,0},{5,9},{6,2},{7,11},{8,12},{9,5},{1... | collective-permute-start | bytes 245768 | tf_op jit(solution)/shard_map/ppermute | solution.py:31
  32.6 6.1 %collective-permute-start.14 = (bf16[320,128]{1,0:T(8,128)(2,1)S(1)}, bf16[320,128]{1,0:T(8,128)(2,1)S(1)}, u32[]{:S(2)}, u32[]{:S(2)}) collective-permute-start(bf16[320,128]{1,0:T(8,128)(2,1)S(1)} %get-tuple-element.49), channel_id=1, source_target_pairs={{0,6},{1,11},{2,4},{3,9},{4,2},{5,15},{6,0},{7,13},{8,14},{9,3},{1... | collective-permute-start | bytes 245768 | tf_op jit(solution)/shard_map/ppermute | solution.py:31
  34.0 4.7 %collective-permute-start.15 = (bf16[320,128]{1,0:T(8,128)(2,1)S(1)}, bf16[320,128]{1,0:T(8,128)(2,1)S(1)}, u32[]{:S(2)}, u32[]{:S(2)}) collective-permute-start(bf16[320,128]{1,0:T(8,128)(2,1)S(1)} %get-tuple-element.49), channel_id=1, source_target_pairs={{1,15},{3,13},{5,11},{7,9},{9,7},{11,5},{13,3},{15,1},{17,31},{19,... | collective-permute-start | bytes 245768 | tf_op jit(solution)/shard_map/ppermute | solution.py:31
  38.9 4.3 %collective-permute-start.16 = (f32[2,320,128]{2,1,0:T(8,128)S(1)}, f32[2,320,128]{2,1,0:T(8,128)S(1)}, u32[]{:S(2)}, u32[]{:S(2)}) collective-permute-start(f32[2,320,128]{2,1,0:T(8,128)S(1)} %pad_maximum_fusion.mine_ref), channel_id=1, source_target_pairs={{0,1},{1,0},{2,3},{3,2},{4,5},{5,4},{6,7},{7,6},{8,9},{9,8},{10,11... | collective-permute-start | bytes 983048 | tf_op jit(solution)/shard_map/ppermute | solution.py:35

commit v7 on v6

--- a/solution.py
+++ b/solution.py
@@ -311,6 +311,9 @@
         T=state['ch'][c][(i%4)*32:(i%4)*32+32,:]
         update(i,lstack(jnp.where(bd,jnp.concatenate([T]*4,0),0.0)),state['ps'],off)
     def emit_out(kb,Pf): emit(kb,state['panel'],Pf)
+    def first_quarter(t):
+        tr_ref[t,0:128,0:128]=mmt(Rb[t,0:128,0:128],Wb[t,0:128,0:128]).astype(jnp.bfloat16)
+        tr_ref[t,128:256,0:128]=jnp.zeros((128,128),jnp.bfloat16)
     p32=pick(placed(0,0)); q32=pick(placed(0,1))
     for kb in range(8):
         if kb==0: pending.append(functools.partial(prep,0))
@@ -331,10 +334,13 @@
             pending.append(functools.partial(go,i,32*kb))
             if i==min(kb+2,7) and kb+1<7: pending.append(functools.partial(prep,kb+1))
         pending.append(functools.partial(emit_out,kb,Pf))
+        if kb==3:
+            for t in range(3): pending.append(functools.partial(first_quarter,t))
     while pending: pending.pop(0)()
     r_ref[...]=Rb[0]
     for t in range(3):
-        tr_ref[t]=mmt(Rb[t],Wb[t]).astype(jnp.bfloat16)
+        tr_ref[t,0:128,128:256]=mmt(Rb[t,0:128,:],Wb[t,128:256,:]).astype(jnp.bfloat16)
+        tr_ref[t,128:256,128:256]=mmt(Rb[t,128:256,128:256],Wb[t,128:256,128:256]).astype(jnp.bfloat16)
 
 def factor_all(seg_gram, mine, other):
     return pl.pallas_call(

time: 51.5 us -> 51.4 us (level)
  no operation moved by 1% of the time
where the time goes in v7:
time: 51.4 us; the launch traced here: 51.2 us
  starting transfers between devices  23.7 us (46%)
  Pallas kernels  14.5 us (28%)
  waiting for transfers between devices  10.2 us (20%)
  local copies, waits for them, and re-layouts  1.96 us (4%)
  between operations  0.8 us (2%)
    ppermute x13, starting transfers between devices, hop(): return lax.ppermute(value, AXES, pairs)  19.5 us
    pallas_call x1, Pallas kernels, factor_all(): pl.pallas_call(factor_kernel, out_shape=(jax.ShapeDtypeStruct((256, 256),...  8.07 us
    ppermute x13, waiting for transfers between devices, hop(): return lax.ppermute(value, AXES, pairs)  6.83 us
    ppermute x2, starting transfers between devices, sub_hop(): lax.ppermute(value, 'sub', [(i, i ^ mask) for i in range(lax.axis_size('s...  3.02 us
    ppermute x2, waiting for transfers between devices, sub_hop(): lax.ppermute(value, 'sub', [(i, i ^ mask) for i in range(lax.axis_size('s...  2.65 us
    pallas_call x1, Pallas kernels, body(): pl.pallas_call(first_kernel, out_shape=[jax.ShapeDtypeStruct((1, leaf_cou...  2.63 us
    pallas_call x2, Pallas kernels, near_leaf(): pl.pallas_call(functools.partial(near_kernel, leaf), out_shape=jax.ShapeD...  2.23 us
    slice x1, local copies, waits for them, and re-layouts, near_leaf(): lax.slice_in_dim(near_blocks, leaf, leaf + 1, axis=0)  1.94 us
  transfers between devices with their start and end apart: 17, of which 9 were waited for; matrix products, arithmetic and copies ran while one was open for 4% of the time, Pallas kernels for 9%

profile of v7, /device:TPU:0, one launch (start us, length us, event | category | flops | bytes accessed | tf_op | source)
XLA Modules:
  0.0 51.2 jit_solution(3440387367019153330)
XLA Ops:
  0.6 0.5 %collective-permute-start = (bf16[512,256]{1,0:T(8,128)(2,1)}, bf16[512,256]{1,0:T(8,128)(2,1)S(1)}, u32[]{:S(2)}, u32[]{:S(2)}) collective-permute-start(bf16[512,256]{1,0:T(8,128)(2,1)} %own_hbm.3), channel_id=1, source_target_pairs={{0,1},{1,0},{2,3},{3,2},{4,5},{5,4},{6,7},{7,6},{8,9},{9,8},{10,11... | collective-permute-start | bytes 786440 | tf_op jit(solution)/shard_map/ppermute | solution.py:373
  1.1 0.7 %collective-permute-start.7 = (bf16[512,256]{1,0:T(8,128)(2,1)}, bf16[512,256]{1,0:T(8,128)(2,1)S(1)}, u32[]{:S(2)}, u32[]{:S(2)}) collective-permute-start(bf16[512,256]{1,0:T(8,128)(2,1)} %own_hbm.3), channel_id=1, source_target_pairs={{1,2},{3,4},{5,6},{7,8},{9,10},{11,12},{13,14},{15,16},{17,18},{19... | collective-permute-start | bytes 786440 | tf_op jit(solution)/shard_map/ppermute | solution.py:375
  1.8 0.7 %collective-permute-done.swap_ref = bf16[512,256]{1,0:T(8,128)(2,1)S(1)} collective-permute-done((bf16[512,256]{1,0:T(8,128)(2,1)}, bf16[512,256]{1,0:T(8,128)(2,1)S(1)}, u32[]{:S(2)}, u32[]{:S(2)}) %collective-permute-start) | collective-permute-done | bytes 262176 | tf_op jit(solution)/shard_map/ppermute | solution.py:373
  2.5 2.6 %shard_map.103 = (bf16[1,136,256]{2,1,0:T(8,128)(2,1)}, bf16[2,64,256]{2,1,0:T(8,128)(2,1)}, bf16[1,264,128]{2,1,0:T(8,128)(2,1)}, bf16[1,264,128]{2,1,0:T(8,128...) custom-call(bf16[2,64,256]{2,1,0:T(8,128)(2,1)} %basis_hbm, bf16[512,256]{1,0:T(8,128)(2,1)} %own_hbm.3, ...), custom_call_target="tpu_custom_call" | custom-call | tf_op jit(solution)/shard_map/pallas_call | solution.py:382
  5.2 3.1 %collective-permute-start.4 = (bf16[1,264,128]{2,1,0:T(8,128)(2,1)}, bf16[1,264,128]{2,1,0:T(8,128)(2,1)S(1)}, u32[]{:S(2)}, u32[]{:S(2)}) collective-permute-start(bf16[1,264,128]{2,1,0:T(8,128)(2,1)} %get-tuple-element.29), channel_id=1, source_target_pairs={{0,2},{1,3},{2,0},{3,1},{4,6},{5,7},{6,4},{7,5},{8,10},{9,11},{10,... | collective-permute-start | bytes 202760 | tf_op jit(solution)/shard_map/ppermute | solution.py:31
  8.3 2.6 %collective-permute-start.1 = (bf16[1,136,256]{2,1,0:T(8,128)(2,1)}, bf16[1,136,256]{2,1,0:T(8,128)(2,1)S(1)}, u32[]{:S(2)}, u32[]{:S(2)}) collective-permute-start(bf16[1,136,256]{2,1,0:T(8,128)(2,1)} %get-tuple-element.28.refs_0_), channel_id=1, source_target_pairs={{0,8},{1,9},{2,10},{3,11},{4,12},{5,13},{6,14},{7,15},{8,0},{9,1},... | collective-permute-start | bytes 208904 | tf_op jit(solution)/shard_map/ppermute | solution.py:31
  10.9 2.6 %collective-permute-start.2 = (bf16[1,136,256]{2,1,0:T(8,128)(2,1)}, bf16[1,136,256]{2,1,0:T(8,128)(2,1)S(1)}, u32[]{:S(2)}, u32[]{:S(2)}) collective-permute-start(bf16[1,136,256]{2,1,0:T(8,128)(2,1)} %get-tuple-element.28.refs_0_), channel_id=1, source_target_pairs={{0,16},{1,17},{2,18},{3,19},{4,20},{5,21},{6,22},{7,23},{8,24},{9,... | collective-permute-start | bytes 208904 | tf_op jit(solution)/shard_map/ppermute | solution.py:31
  13.5 1.6 %collective-permute-start.5 = (bf16[1,264,128]{2,1,0:T(8,128)(2,1)}, bf16[1,264,128]{2,1,0:T(8,128)(2,1)S(1)}, u32[]{:S(2)}, u32[]{:S(2)}) collective-permute-start(bf16[1,264,128]{2,1,0:T(8,128)(2,1)} %get-tuple-element.30), channel_id=1, source_target_pairs={{0,4},{1,5},{2,6},{3,7},{4,0},{5,1},{6,2},{7,3},{8,12},{9,13},{10,... | collective-permute-start | bytes 202760 | tf_op jit(solution)/shard_map/ppermute | solution.py:31
  15.1 1.8 %collective-permute-start.6 = (bf16[1,264,128]{2,1,0:T(8,128)(2,1)}, bf16[1,264,128]{2,1,0:T(8,128)(2,1)S(1)}, u32[]{:S(2)}, u32[]{:S(2)}) collective-permute-start(bf16[1,264,128]{2,1,0:T(8,128)(2,1)} %get-tuple-element.31), channel_id=1, source_target_pairs={{0,6},{1,7},{2,4},{3,5},{4,2},{5,3},{6,0},{7,1},{8,14},{9,15},{10,... | collective-permute-start | bytes 202760 | tf_op jit(solution)/shard_map/ppermute | solution.py:31
  16.9 1.9 %fusion.8 = (bf16[1,10,256,256]{3,2,1,0:T(8,128)(2,1)S(1)}, bf16[1,10,256,256]{3,2,1,0:T(8,128)(2,1)S(1)}) fusion(bf16[2,10,256,256]{3,2,1,0:T(8,128)(2,1)} %param.8), kind=kLoop, calls=%fused_computation.14 | loop fusion | bytes 5242880 | tf_op jit(solution)/shard_map/slice | solution.py:427
  18.9 1.1 %shard_map.104.refs_0_ = f32[256,256]{1,0:T(8,128)S(1)} custom-call(s32[2,10]{1,0:T(2,128)S(1)} %copy-done.4, bf16[1,10,256,256]{3,2,1,0:T(8,128)(2,1)S(1)} %get-tuple-element.52.blocks_ref, bf16[512,256]{1,0:T(8,128)(2,1)S(1)} %copy-done, bf16[512,256]{1,0:T(8,128)(2,1)S(1)} %collective-permute-done.swap_ref, ...), custom_call_target="tpu_custom_call" | custom-call | flops 335544320 | bytes 2621440 | tf_op jit(solution)/shard_map/pallas_call | solution.py:411
  20.0 0.5 collective-permute-done.6.refs_7_
  20.6 0.6 %shard_map.105 = (f32[1,128,256]{2,1,0:T(8,128)S(1)}, bf16[1,128,256]{2,1,0:T(8,128)(2,1)S(1)}, bf16[1,128,256]{2,1,0:T(8,128)(2,1)S(1)}, bf16[1,128,256]{2,1,0:T(8,128)(2,1)S(1)}) custom-call(bf16[1,136,256]{2,1,0:T(8,128)(2,1)S(1)} %copy-done.1, bf16[1,136,256]{2,1,0:T(8,128)(2,1)S(1)} %collective-permute-done.1.refs_1_, ...), custom_call_target="tpu_custom_call" | custom-call | tf_op jit(solution)/shard_map/pallas_call | solution.py:431
  21.1 1.2 %collective-permute-start.10 = (bf16[1,128,256]{2,1,0:T(8,128)(2,1)S(1)}, bf16[1,128,256]{2,1,0:T(8,128)(2,1)S(1)}, u32[]{:S(2)}, u32[]{:S(2)}) collective-permute-start(bf16[1,128,256]{2,1,0:T(8,128)(2,1)S(1)} %get-tuple-element.44), channel_id=1, source_target_pairs={{0,2},{1,3},{2,0},{3,1},{4,6},{5,7},{6,4},{7,5},{8,10},{9,11},{10,... | collective-permute-start | bytes 196616 | tf_op jit(solution)/shard_map/ppermute | solution.py:31
  22.4 0.7 %collective-permute-start.8 = (bf16[1,128,256]{2,1,0:T(8,128)(2,1)S(1)}, bf16[1,128,256]{2,1,0:T(8,128)(2,1)S(1)}, u32[]{:S(2)}, u32[]{:S(2)}) collective-permute-start(bf16[1,128,256]{2,1,0:T(8,128)(2,1)S(1)} %get-tuple-element.42), channel_id=1, source_target_pairs={{0,6},{1,7},{2,4},{3,5},{4,2},{5,3},{6,0},{7,1},{8,14},{9,15},{10,... | collective-permute-start | bytes 196616 | tf_op jit(solution)/shard_map/ppermute | solution.py:31
  23.1 1.6 %collective-permute-start.9 = (bf16[1,128,256]{2,1,0:T(8,128)(2,1)S(1)}, bf16[1,128,256]{2,1,0:T(8,128)(2,1)S(1)}, u32[]{:S(2)}, u32[]{:S(2)}) collective-permute-start(bf16[1,128,256]{2,1,0:T(8,128)(2,1)S(1)} %get-tuple-element.43), channel_id=1, source_target_pairs={{0,4},{1,5},{2,6},{3,7},{4,0},{5,1},{6,2},{7,3},{8,12},{9,13},{10,... | collective-permute-start | bytes 196616 | tf_op jit(solution)/shard_map/ppermute | solution.py:31
  24.7 1.1 %shard_map.106.refs_1_ = f32[256,256]{1,0:T(8,128)S(1)} custom-call(s32[2,10]{1,0:T(2,128)S(1)} %copy-done.4, bf16[1,10,256,256]{3,2,1,0:T(8,128)(2,1)S(1)} %get-tuple-element.51.blocks_ref, bf16[512,256]{1,0:T(8,128)(2,1)S(1)} %copy-done, bf16[512,256]{1,0:T(8,128)(2,1)S(1)} %collective-permute-done.swap_ref, ...), custom_call_target="tpu_custom_call" | custom-call | flops 335544320 | bytes 2621440 | tf_op jit(solution)/shard_map/pallas_call | solution.py:411
  25.8 1.8 %collective-permute-done.8.refs_2_ = bf16[1,128,256]{2,1,0:T(8,128)(2,1)S(1)} collective-permute-done((bf16[1,128,256]{2,1,0:T(8,128)(2,1)S(1)}, bf16[1,128,256]{2,1,0:T(8,128)(2,1)S(1)}, u32[]{:S(2)}, u32[]{:S(2)}) %collective-permute-start.8) | collective-permute-done | bytes 65568 | tf_op jit(solution)/shard_map/ppermute | solution.py:31
  27.6 0.4 collective-permute-done.9.refs_3_
  28.1 1.0 %shard_map.107 = (bf16[512,256]{1,0:T(8,128)(2,1)}, f32[320,128]{1,0:T(8,128)S(1)}) custom-call(bf16[2,64,256]{2,1,0:T(8,128)(2,1)S(1)} %copy-done.3, f32[1,128,256]{2,1,0:T(8,128)S(1)} %get-tuple-element.40.own_ref, f32[256,256]{1,0:T(8,128)S(1)} %shard_map.104.refs_0_, f32[256,256]{1,0:T(8,128)S(1)} %shard_map.106.refs_1_, ...), custom_call_target="tpu_custom_call" | custom-call | tf_op jit(solution)/shard_map/pallas_call | solution.py:442
  29.0 1.4 %collective-permute-done.11 = f32[320,128]{1,0:T(8,128)S(1)} collective-permute-done((f32[320,128]{1,0:T(8,128)S(1)}, f32[320,128]{1,0:T(8,128)S(1)}, u32[]{:S(2)}, u32[]{:S(2)}) %collective-permute-start.11) | collective-permute-done | bytes 163872 | tf_op jit(solution)/shard_map/ppermute | solution.py:35
  30.5 1.3 %collective-permute-start.12 = (bf16[320,128]{1,0:T(8,128)(2,1)S(1)}, bf16[320,128]{1,0:T(8,128)(2,1)S(1)}, u32[]{:S(2)}, u32[]{:S(2)}) collective-permute-start(bf16[320,128]{1,0:T(8,128)(2,1)S(1)} %get-tuple-element.49), channel_id=1, source_target_pairs={{0,2},{1,9},{2,0},{3,11},{4,6},{5,13},{6,4},{7,15},{8,10},{9,1},{1... | collective-permute-start | bytes 245768 | tf_op jit(solution)/shard_map/ppermute | solution.py:31
  31.7 0.9 %collective-permute-start.13 = (bf16[320,128]{1,0:T(8,128)(2,1)S(1)}, bf16[320,128]{1,0:T(8,128)(2,1)S(1)}, u32[]{:S(2)}, u32[]{:S(2)}) collective-permute-start(bf16[320,128]{1,0:T(8,128)(2,1)S(1)} %get-tuple-element.49), channel_id=1, source_target_pairs={{0,4},{1,13},{2,6},{3,15},{4,0},{5,9},{6,2},{7,11},{8,12},{9,5},{1... | collective-permute-start | bytes 245768 | tf_op jit(solution)/shard_map/ppermute | solution.py:31
  32.6 1.4 %collective-permute-start.14 = (bf16[320,128]{1,0:T(8,128)(2,1)S(1)}, bf16[320,128]{1,0:T(8,128)(2,1)S(1)}, u32[]{:S(2)}, u32[]{:S(2)}) collective-permute-start(bf16[320,128]{1,0:T(8,128)(2,1)S(1)} %get-tuple-element.49), channel_id=1, source_target_pairs={{0,6},{1,11},{2,4},{3,9},{4,2},{5,15},{6,0},{7,13},{8,14},{9,3},{1... | collective-permute-start | bytes 245768 | tf_op jit(solution)/shard_map/ppermute | solution.py:31
  34.0 0.7 %collective-permute-start.15 = (bf16[320,128]{1,0:T(8,128)(2,1)S(1)}, bf16[320,128]{1,0:T(8,128)(2,1)S(1)}, u32[]{:S(2)}, u32[]{:S(2)}) collective-permute-start(bf16[320,128]{1,0:T(8,128)(2,1)S(1)} %get-tuple-element.49), channel_id=1, source_target_pairs={{1,15},{3,13},{5,11},{7,9},{9,7},{11,5},{13,3},{15,1},{17,31},{19,... | collective-permute-start | bytes 245768 | tf_op jit(solution)/shard_map/ppermute | solution.py:31
  34.7 0.3 collective-permute-done.12
  35.0 2.1 %collective-permute-done.13 = bf16[320,128]{1,0:T(8,128)(2,1)S(1)} collective-permute-done((bf16[320,128]{1,0:T(8,128)(2,1)S(1)}, bf16[320,128]{1,0:T(8,128)(2,1)S(1)}, u32[]{:S(2)}, u32[]{:S(2)}) %collective-permute-start.13) | collective-permute-done | bytes 81952 | tf_op jit(solution)/shard_map/ppermute | solution.py:31
  37.0 1.7 %collective-permute-done.14 = bf16[320,128]{1,0:T(8,128)(2,1)S(1)} collective-permute-done((bf16[320,128]{1,0:T(8,128)(2,1)S(1)}, bf16[320,128]{1,0:T(8,128)(2,1)S(1)}, u32[]{:S(2)}, u32[]{:S(2)}) %collective-permute-start.14) | collective-permute-done | bytes 81952 | tf_op jit(solution)/shard_map/ppermute | solution.py:31
  38.7 0.1 fusion.3
  38.9 3.0 %collective-permute-start.16 = (f32[2,320,128]{2,1,0:T(8,128)S(1)}, f32[2,320,128]{2,1,0:T(8,128)S(1)}, u32[]{:S(2)}, u32[]{:S(2)}) collective-permute-start(f32[2,320,128]{2,1,0:T(8,128)S(1)} %pad_maximum_fusion.mine_ref), channel_id=1, source_target_pairs={{0,1},{1,0},{2,3},{3,2},{4,5},{5,4},{6,7},{7,6},{8,9},{9,8},{10,11... | collective-permute-start | bytes 983048 | tf_op jit(solution)/shard_map/ppermute | solution.py:35
  41.9 1.3 %collective-permute-done.16.other_ref = f32[2,320,128]{2,1,0:T(8,128)S(1)} collective-permute-done((f32[2,320,128]{2,1,0:T(8,128)S(1)}, f32[2,320,128]{2,1,0:T(8,128)S(1)}, u32[]{:S(2)}, u32[]{:S(2)}) %collective-permute-start.16) | collective-permute-done | bytes 327712 | tf_op jit(solution)/shard_map/ppermute | solution.py:35
  43.1 8.1 %shard_map.108 = (f32[256,256]{1,0:T(8,128)}, bf16[3,256,256]{2,1,0:T(8,128)(2,1)}) custom-call(f32[320,128]{1,0:T(8,128)S(1)} %get-tuple-element.50.seg_ref, f32[2,320,128]{2,1,0:T(8,128)S(1)} %pad_maximum_fusion.mine_ref, f32[2,320,128]{2,1,0:T(8,128)S(1)} %collective-permute-done.16.other_ref), custom_call_target="tpu_custom_call" | custom-call | tf_op jit(solution)/shard_map/pallas_call | solution.py:346
  (22 shorter events, 0.1 us)
Async XLA Ops:
  0.6 1.9 %collective-permute-start = (bf16[512,256]{1,0:T(8,128)(2,1)}, bf16[512,256]{1,0:T(8,128)(2,1)S(1)}, u32[]{:S(2)}, u32[]{:S(2)}) collective-permute-start(bf16[512,256]{1,0:T(8,128)(2,1)} %own_hbm.3), channel_id=1, source_target_pairs={{0,1},{1,0},{2,3},{3,2},{4,5},{5,4},{6,7},{7,6},{8,9},{9,8},{10,11... | collective-permute-start | bytes 786440 | tf_op jit(solution)/shard_map/ppermute | solution.py:373
  1.1 12.3 %collective-permute-start.7 = (bf16[512,256]{1,0:T(8,128)(2,1)}, bf16[512,256]{1,0:T(8,128)(2,1)S(1)}, u32[]{:S(2)}, u32[]{:S(2)}) collective-permute-start(bf16[512,256]{1,0:T(8,128)(2,1)} %own_hbm.3), channel_id=1, source_target_pairs={{1,2},{3,4},{5,6},{7,8},{9,10},{11,12},{13,14},{15,16},{17,18},{19... | collective-permute-start | bytes 786440 | tf_op jit(solution)/shard_map/ppermute | solution.py:375
  5.2 10.0 %collective-permute-start.4 = (bf16[1,264,128]{2,1,0:T(8,128)(2,1)}, bf16[1,264,128]{2,1,0:T(8,128)(2,1)S(1)}, u32[]{:S(2)}, u32[]{:S(2)}) collective-permute-start(bf16[1,264,128]{2,1,0:T(8,128)(2,1)} %get-tuple-element.29), channel_id=1, source_target_pairs={{0,2},{1,3},{2,0},{3,1},{4,6},{5,7},{6,4},{7,5},{8,10},{9,11},{10,... | collective-permute-start | bytes 202760 | tf_op jit(solution)/shard_map/ppermute | solution.py:31
  8.3 12.2 %collective-permute-start.1 = (bf16[1,136,256]{2,1,0:T(8,128)(2,1)}, bf16[1,136,256]{2,1,0:T(8,128)(2,1)S(1)}, u32[]{:S(2)}, u32[]{:S(2)}) collective-permute-start(bf16[1,136,256]{2,1,0:T(8,128)(2,1)} %get-tuple-element.28.refs_0_), channel_id=1, source_target_pairs={{0,8},{1,9},{2,10},{3,11},{4,12},{5,13},{6,14},{7,15},{8,0},{9,1},... | collective-permute-start | bytes 208904 | tf_op jit(solution)/shard_map/ppermute | solution.py:31
  10.9 9.7 %collective-permute-start.2 = (bf16[1,136,256]{2,1,0:T(8,128)(2,1)}, bf16[1,136,256]{2,1,0:T(8,128)(2,1)S(1)}, u32[]{:S(2)}, u32[]{:S(2)}) collective-permute-start(bf16[1,136,256]{2,1,0:T(8,128)(2,1)} %get-tuple-element.28.refs_0_), channel_id=1, source_target_pairs={{0,16},{1,17},{2,18},{3,19},{4,20},{5,21},{6,22},{7,23},{8,24},{9,... | collective-permute-start | bytes 208904 | tf_op jit(solution)/shard_map/ppermute | solution.py:31
  13.5 7.1 %collective-permute-start.3 = (bf16[1,136,256]{2,1,0:T(8,128)(2,1)}, bf16[1,136,256]{2,1,0:T(8,128)(2,1)S(1)}, u32[]{:S(2)}, u32[]{:S(2)}) collective-permute-start(bf16[1,136,256]{2,1,0:T(8,128)(2,1)} %get-tuple-element.28.refs_0_), channel_id=1, source_target_pairs={{0,24},{1,25},{2,26},{3,27},{4,28},{5,29},{6,30},{7,31},{8,16},{9,... | collective-permute-start | bytes 208904 | tf_op jit(solution)/shard_map/ppermute | solution.py:31
  13.5 6.5 %collective-permute-start.5 = (bf16[1,264,128]{2,1,0:T(8,128)(2,1)}, bf16[1,264,128]{2,1,0:T(8,128)(2,1)S(1)}, u32[]{:S(2)}, u32[]{:S(2)}) collective-permute-start(bf16[1,264,128]{2,1,0:T(8,128)(2,1)} %get-tuple-element.30), channel_id=1, source_target_pairs={{0,4},{1,5},{2,6},{3,7},{4,0},{5,1},{6,2},{7,3},{8,12},{9,13},{10,... | collective-permute-start | bytes 202760 | tf_op jit(solution)/shard_map/ppermute | solution.py:31
  15.1 3.7 %copy-start = (bf16[512,256]{1,0:T(8,128)(2,1)S(1)}, bf16[512,256]{1,0:T(8,128)(2,1)}, u32[]{:S(2)}) copy-start(bf16[512,256]{1,0:T(8,128)(2,1)} %own_hbm.3) | copy-start | bytes 786436
  15.1 3.7 %copy-start.4 = (s32[2,10]{1,0:T(2,128)S(1)}, s32[2,10]{1,0:T(2,128)}, u32[]{:S(2)}) copy-start(s32[2,10]{1,0:T(2,128)} %list_hbm.3) | copy-start | bytes 244
  15.1 5.4 %collective-permute-start.6 = (bf16[1,264,128]{2,1,0:T(8,128)(2,1)}, bf16[1,264,128]{2,1,0:T(8,128)(2,1)S(1)}, u32[]{:S(2)}, u32[]{:S(2)}) collective-permute-start(bf16[1,264,128]{2,1,0:T(8,128)(2,1)} %get-tuple-element.31), channel_id=1, source_target_pairs={{0,6},{1,7},{2,4},{3,5},{4,2},{5,3},{6,0},{7,1},{8,14},{9,15},{10,... | collective-permute-start | bytes 202760 | tf_op jit(solution)/shard_map/ppermute | solution.py:31
  18.8 1.7 %copy-start.1 = (bf16[1,136,256]{2,1,0:T(8,128)(2,1)S(1)}, bf16[1,136,256]{2,1,0:T(8,128)(2,1)}, u32[]{:S(2)}) copy-start(bf16[1,136,256]{2,1,0:T(8,128)(2,1)} %get-tuple-element.28.refs_0_) | copy-start | bytes 208900
  18.8 1.7 %copy-start.2 = (bf16[1,264,128]{2,1,0:T(8,128)(2,1)S(1)}, bf16[1,264,128]{2,1,0:T(8,128)(2,1)}, u32[]{:S(2)}) copy-start(bf16[1,264,128]{2,1,0:T(8,128)(2,1)} %get-tuple-element.36.refs_4_) | copy-start | bytes 202756
  21.1 6.9 %copy-start.3 = (bf16[2,64,256]{2,1,0:T(8,128)(2,1)S(1)}, bf16[2,64,256]{2,1,0:T(8,128)(2,1)}, u32[]{:S(2)}) copy-start(bf16[2,64,256]{2,1,0:T(8,128)(2,1)} %get-tuple-element.27.basis_ref) | copy-start | bytes 196612
  21.1 4.7 %collective-permute-start.10 = (bf16[1,128,256]{2,1,0:T(8,128)(2,1)S(1)}, bf16[1,128,256]{2,1,0:T(8,128)(2,1)S(1)}, u32[]{:S(2)}, u32[]{:S(2)}) collective-permute-start(bf16[1,128,256]{2,1,0:T(8,128)(2,1)S(1)} %get-tuple-element.44), channel_id=1, source_target_pairs={{0,2},{1,3},{2,0},{3,1},{4,6},{5,7},{6,4},{7,5},{8,10},{9,11},{10,... | collective-permute-start | bytes 196616 | tf_op jit(solution)/shard_map/ppermute | solution.py:31
  22.4 5.3 %collective-permute-start.8 = (bf16[1,128,256]{2,1,0:T(8,128)(2,1)S(1)}, bf16[1,128,256]{2,1,0:T(8,128)(2,1)S(1)}, u32[]{:S(2)}, u32[]{:S(2)}) collective-permute-start(bf16[1,128,256]{2,1,0:T(8,128)(2,1)S(1)} %get-tuple-element.42), channel_id=1, source_target_pairs={{0,6},{1,7},{2,4},{3,5},{4,2},{5,3},{6,0},{7,1},{8,14},{9,15},{10,... | collective-permute-start | bytes 196616 | tf_op jit(solution)/shard_map/ppermute | solution.py:31
  23.1 5.0 %collective-permute-start.9 = (bf16[1,128,256]{2,1,0:T(8,128)(2,1)S(1)}, bf16[1,128,256]{2,1,0:T(8,128)(2,1)S(1)}, u32[]{:S(2)}, u32[]{:S(2)}) collective-permute-start(bf16[1,128,256]{2,1,0:T(8,128)(2,1)S(1)} %get-tuple-element.43), channel_id=1, source_target_pairs={{0,4},{1,5},{2,6},{3,7},{4,0},{5,1},{6,2},{7,3},{8,12},{9,13},{10,... | collective-permute-start | bytes 196616 | tf_op jit(solution)/shard_map/ppermute | solution.py:31
  29.0 1.4 %collective-permute-start.11 = (f32[320,128]{1,0:T(8,128)S(1)}, f32[320,128]{1,0:T(8,128)S(1)}, u32[]{:S(2)}, u32[]{:S(2)}) collective-permute-start(f32[320,128]{1,0:T(8,128)S(1)} %get-tuple-element.46), channel_id=1, source_target_pairs={{0,1},{1,0},{2,3},{3,2},{4,5},{5,4},{6,7},{7,6},{8,9},{9,8},{10,11... | collective-permute-start | bytes 491528 | tf_op jit(solution)/shard_map/ppermute | solution.py:35
  30.5 4.5 %collective-permute-start.12 = (bf16[320,128]{1,0:T(8,128)(2,1)S(1)}, bf16[320,128]{1,0:T(8,128)(2,1)S(1)}, u32[]{:S(2)}, u32[]{:S(2)}) collective-permute-start(bf16[320,128]{1,0:T(8,128)(2,1)S(1)} %get-tuple-element.49), channel_id=1, source_target_pairs={{0,2},{1,9},{2,0},{3,11},{4,6},{5,13},{6,4},{7,15},{8,10},{9,1},{1... | collective-permute-start | bytes 245768 | tf_op jit(solution)/shard_map/ppermute | solution.py:31
  31.7 5.3 %collective-permute-start.13 = (bf16[320,128]{1,0:T(8,128)(2,1)S(1)}, bf16[320,128]{1,0:T(8,128)(2,1)S(1)}, u32[]{:S(2)}, u32[]{:S(2)}) collective-permute-start(bf16[320,128]{1,0:T(8,128)(2,1)S(1)} %get-tuple-element.49), channel_id=1, source_target_pairs={{0,4},{1,13},{2,6},{3,15},{4,0},{5,9},{6,2},{7,11},{8,12},{9,5},{1... | collective-permute-start | bytes 245768 | tf_op jit(solution)/shard_map/ppermute | solution.py:31
  32.6 6.1 %collective-permute-start.14 = (bf16[320,128]{1,0:T(8,128)(2,1)S(1)}, bf16[320,128]{1,0:T(8,128)(2,1)S(1)}, u32[]{:S(2)}, u32[]{:S(2)}) collective-permute-start(bf16[320,128]{1,0:T(8,128)(2,1)S(1)} %get-tuple-element.49), channel_id=1, source_target_pairs={{0,6},{1,11},{2,4},{3,9},{4,2},{5,15},{6,0},{7,13},{8,14},{9,3},{1... | collective-permute-start | bytes 245768 | tf_op jit(solution)/shard_map/ppermute | solution.py:31
  34.0 4.7 %collective-permute-start.15 = (bf16[320,128]{1,0:T(8,128)(2,1)S(1)}, bf16[320,128]{1,0:T(8,128)(2,1)S(1)}, u32[]{:S(2)}, u32[]{:S(2)}) collective-permute-start(bf16[320,128]{1,0:T(8,128)(2,1)S(1)} %get-tuple-element.49), channel_id=1, source_target_pairs={{1,15},{3,13},{5,11},{7,9},{9,7},{11,5},{13,3},{15,1},{17,31},{19,... | collective-permute-start | bytes 245768 | tf_op jit(solution)/shard_map/ppermute | solution.py:31
  38.9 4.3 %collective-permute-start.16 = (f32[2,320,128]{2,1,0:T(8,128)S(1)}, f32[2,320,128]{2,1,0:T(8,128)S(1)}, u32[]{:S(2)}, u32[]{:S(2)}) collective-permute-start(f32[2,320,128]{2,1,0:T(8,128)S(1)} %pad_maximum_fusion.mine_ref), channel_id=1, source_target_pairs={{0,1},{1,0},{2,3},{3,2},{4,5},{5,4},{6,7},{7,6},{8,9},{9,8},{10,11... | collective-permute-start | bytes 983048 | tf_op jit(solution)/shard_map/ppermute | solution.py:35
